TPU v7x, 32 devices: a whole 2x2x4 slice. The times are simulated.
32 devices in a mesh: rows: 16 (over z, y, x), hid: 2 (over core).
Axes of the slice: x: 2, y: 2, z: 4, core: 2. Of those that a mesh axis runs over, the one named last changes fastest.
Arguments:
- hidden_in: bfloat16 [16384, 768], P('rows', 'hid'), may hold values from -6 to 6
- teacher: bfloat16 [16384, 768], P('rows', 'hid'), may hold values from -6 to 6
- segment_ids: int32 [16384], P('rows'), may hold values from 0 to 127, never falling along the last dimension, each value on 1 to 512 neighbouring positions
- valid_mask: int32 [16384], P('rows'), may hold values 0 or 1
- w_query: bfloat16 [768, 768], P(None, 'hid'), may hold values from -0.21875 to 0.21875
- b_query: float32 [768], P('hid'), may hold values from -3 to 3
- w_key: bfloat16 [768, 768], P(None, 'hid'), may hold values from -0.21875 to 0.21875
- w_value: bfloat16 [768, 768], P(None, 'hid'), may hold values from -0.21875 to 0.21875
- b_value: float32 [768], P('hid'), may hold values from -3 to 3
- w_attn_out: bfloat16 [768, 768], P('hid'), may hold values from -1.75 to 1.75
- b_attn_out: float32 [768], P('hid'), may hold values from -3 to 3
- gain_one: float32 [768], P('hid'), may hold values from 0.5 to 1.5
- shift_one: float32 [768], P('hid'), may hold values from -3 to 3
- w_up: bfloat16 [768, 3072], P(None, 'hid'), may hold values from -0.21875 to 0.21875
- b_up: float32 [3072], P('hid'), may hold values from -3 to 3
- w_down: bfloat16 [3072, 768], P('hid'), may hold values from -0.21875 to 0.21875
- b_down: float32 [768], P('hid'), may hold values from -3 to 3
- gain_two: float32 [768], P('hid'), may hold values from 0.5 to 1.5
- shift_two: float32 [768], P('hid'), may hold values from -3 to 3
- head_alpha: float32 [12], P('hid'), may hold values from -3 to 5
- mha_alpha: float32 [1], replicated, may hold values from -0.3 to 0.7
- unit_alpha: float32 [3072], P('hid'), may hold values from -3 to 5
- ffn_alpha: float32 [1], replicated, may hold values from -0.3 to 0.7
- hidden_alpha: float32 [768], P('hid'), may hold values from -2 to 5
- head_noise: float32 [12], P('hid'), may hold values from 0.05 to 0.95
- mha_noise: float32 [1], replicated, may hold values from 0.3 to 0.7
- unit_noise: float32 [3072], P('hid'), may hold values from 0.05 to 0.95
- ffn_noise: float32 [1], replicated, may hold values from 0.3 to 0.7
- hidden_noise: float32 [768], P('hid'), may hold values from 0.05 to 0.95
- lagrange: float32 [2], replicated, may hold values from 1 to 4
Outputs:
- output: bfloat16 [16384, 768], P('rows', 'hid')
- grad_input: float32 [16384, 768], P('rows', 'hid')
- grad_w_query: float32 [768, 768], P(None, 'hid')
- grad_b_query: float32 [768], P('hid')
- grad_w_key: float32 [768, 768], P(None, 'hid')
- grad_w_value: float32 [768, 768], P(None, 'hid')
- grad_b_value: float32 [768], P('hid')
- grad_w_attn_out: float32 [768, 768], P('hid')
- grad_b_attn_out: float32 [768], P('hid')
- grad_gain_one: float32 [768], P('hid')
- grad_shift_one: float32 [768], P('hid')
- grad_w_up: float32 [768, 3072], P(None, 'hid')
- grad_b_up: float32 [3072], P('hid')
- grad_w_down: float32 [3072, 768], P('hid')
- grad_b_down: float32 [768], P('hid')
- grad_gain_two: float32 [768], P('hid')
- grad_shift_two: float32 [768], P('hid')
- grad_head_gate: float32 [12], P('hid')
- grad_mha_gate: float32 [1], replicated
- grad_unit_gate: float32 [3072], P('hid')
- grad_ffn_gate: float32 [1], replicated
- grad_hidden_gate: float32 [768], P('hid')
- grad_head_alpha: float32 [12], P('hid')
- grad_mha_alpha: float32 [1], replicated
- grad_unit_alpha: float32 [3072], P('hid')
- grad_ffn_alpha: float32 [1], replicated
- grad_hidden_alpha: float32 [768], P('hid')
- expected_share: float32 [1], replicated
- penalty: float32 [1], replicated
Inputs may be any that keep to these rules, and one draw needn't show every extreme that they name: `segment_ids`: segment numbers never fall along the tokens, and a segment holds at most 512 tokens.
All inputs are finite; a program needn't handle non-finite values. No bound on the sum of `valid_mask` on one device may be relied on, other than what follows from the above.
Results may differ from a plain program's by a relative error of at most 0.013.
Values may be sent and summed in bfloat16 or wider, within the bound.
No kernel may reach another device: no remote copies, remote signals or barrier semaphores. Data moves between devices by JAX's collectives and lax.ppermute only.
A program may use at most 128 MiB of HBM per device.

v0:
```python
from functools import partial
import math

import jax
import jax.numpy as jnp
from jax import lax
from jax.sharding import PartitionSpec as P

D = 768
HD = 64
FF = 3072
BLOCK = 512


norm_eps = 1e-05
gate_temper = 2.0 / 3.0
stretch_low = -0.1
stretch_high = 1.1
target_share = 0.4
masked_score = -1000000000.0


def hard_concrete(gate_noise, log_alpha):
    relaxed = jax.nn.sigmoid(
        (jnp.log(gate_noise) - jnp.log(1.0 - gate_noise) + log_alpha) / gate_temper
    )
    return jnp.clip(relaxed * (stretch_high - stretch_low) + stretch_low, 0.0, 1.0)


def open_share(log_alpha):
    return jax.nn.sigmoid(log_alpha - gate_temper * math.log(-stretch_low / stretch_high))


def lagrangian(head_sum, unit_sum, hidden_sum, mha_alpha, ffn_alpha, lagrange):
    heads_kept = open_share(mha_alpha) * head_sum
    units_kept = open_share(ffn_alpha) * unit_sum
    kept_share = (
        (4.0 * HD * heads_kept + 2.0 * units_kept) * hidden_sum / ((4.0 * D + 2.0 * FF) * D)
    )
    share_gap = kept_share - target_share
    return (lagrange[0:1] * share_gap + lagrange[1:2] * share_gap * share_gap, kept_share)


def to_low(values_in):
    return values_in.astype(jnp.bfloat16)


def contract(first, second, first_dim, second_dim):
    return lax.dot_general(
        first, second, (((first_dim,), (second_dim,)), ((), ())), preferred_element_type=jnp.float32
    )


def column_sum(values_in):
    return jnp.sum(values_in, axis=0)


def block_scores(query_block, key_block, segment, valid):
    raw_scores = jnp.einsum(
        "qhd,khd->hqk", query_block, key_block, preferred_element_type=jnp.float32
    )
    allowed = (segment[:, None] == segment[None, :]) & (
        (valid[None, :] == 1) | (valid[:, None] == 0)
    )
    return jnp.where(allowed[None], raw_scores * HD ** (-0.5), masked_score)


def attend_forward(pieces):
    query_block, key_block, value_block, segment, valid = pieces
    scores = block_scores(query_block, key_block, segment, valid)
    row_top = jnp.max(scores, axis=2, keepdims=True)
    exp_total = jnp.sum(jnp.exp(scores - row_top), axis=2, keepdims=True)
    log_total = row_top + jnp.log(exp_total)
    low_probs = to_low(jnp.exp(scores - log_total))
    context = jnp.einsum("hqk,khd->qhd", low_probs, value_block, preferred_element_type=jnp.float32)
    return (context, log_total)


def attend_backward(pieces):
    query_block, key_block, value_block, segment, valid, log_total, grad_block = pieces
    scores = block_scores(query_block, key_block, segment, valid)
    exact_probs = jnp.exp(scores - log_total)
    low_probs = to_low(exact_probs)
    grad_value = jnp.einsum(
        "hqk,qhd->khd", low_probs, grad_block, preferred_element_type=jnp.float32
    )
    grad_probs = jnp.einsum(
        "qhd,khd->hqk", grad_block, value_block, preferred_element_type=jnp.float32
    )
    grad_scores = exact_probs * (
        grad_probs - jnp.sum(grad_probs * exact_probs, axis=2, keepdims=True)
    )
    grad_raw = to_low(grad_scores * HD ** (-0.5))
    grad_query = jnp.einsum("hqk,khd->qhd", grad_raw, key_block, preferred_element_type=jnp.float32)
    grad_key = jnp.einsum("hqk,qhd->khd", grad_raw, query_block, preferred_element_type=jnp.float32)
    return (grad_query, grad_key, grad_value)


def norm_forward(resid, model_width):
    norm_sums = lax.psum((jnp.sum(resid, axis=1), jnp.sum(resid * resid, axis=1)), "hid")
    row_mean = norm_sums[0] / model_width
    row_var = norm_sums[1] / model_width - row_mean * row_mean
    inv_scale = lax.rsqrt(row_var + norm_eps)
    return ((resid - row_mean[:, None]) * inv_scale[:, None], inv_scale)


def norm_backward(grad_normed, normed, inv_scale, model_width):
    back_sums = lax.psum(
        (jnp.sum(grad_normed, axis=1), jnp.sum(grad_normed * normed, axis=1)), "hid"
    )
    return inv_scale[:, None] * (
        grad_normed
        - back_sums[0][:, None] / model_width
        - normed * (back_sums[1][:, None] / model_width)
    )


def alpha_grad(gate_noise, log_alpha, grad_gate):
    _, gate_back = jax.vjp(hard_concrete, gate_noise, log_alpha)
    return gate_back(grad_gate)[1]


def open_grad(log_alpha, grad_total):
    _, open_back = jax.vjp(open_share, log_alpha)
    return open_back(jnp.broadcast_to(grad_total, log_alpha.shape))[0]


def body(
    hidden_in,
    teacher,
    segment_ids,
    valid_mask,
    w_query,
    b_query,
    w_key,
    w_value,
    b_value,
    w_attn_out,
    b_attn_out,
    gain_one,
    shift_one,
    w_up,
    b_up,
    w_down,
    b_down,
    gain_two,
    shift_two,
    head_alpha,
    mha_alpha,
    unit_alpha,
    ffn_alpha,
    hidden_alpha,
    head_noise,
    mha_noise,
    unit_noise,
    ffn_noise,
    hidden_noise,
    lagrange,
):
    model_width = w_query.shape[0]
    row_count = hidden_in.shape[0]
    local_width = hidden_in.shape[1]
    head_count = local_width // HD
    blocks = row_count // BLOCK
    head_gate = hard_concrete(head_noise, head_alpha)
    mha_gate = hard_concrete(mha_noise, mha_alpha)
    unit_gate = hard_concrete(unit_noise, unit_alpha)
    ffn_gate = hard_concrete(ffn_noise, ffn_alpha)
    hidden_gate = hard_concrete(hidden_noise, hidden_alpha)
    head_cols = jnp.repeat(head_gate, HD)
    source = hidden_in.astype(jnp.float32)

    def to_blocks(values_in):
        return values_in.reshape(blocks, BLOCK, head_count, HD)

    block_segments = segment_ids.reshape(blocks, BLOCK)
    block_valid = valid_mask.reshape(blocks, BLOCK)
    inputs_full = lax.all_gather(hidden_in, "hid", axis=1, tiled=True)
    query_low = to_low(jnp.dot(inputs_full, w_query, preferred_element_type=jnp.float32) + b_query)
    key_low = to_low(jnp.dot(inputs_full, w_key, preferred_element_type=jnp.float32))
    value_low = to_low(jnp.dot(inputs_full, w_value, preferred_element_type=jnp.float32) + b_value)
    context, log_total = lax.map(
        attend_forward,
        (
            to_blocks(query_low),
            to_blocks(key_low),
            to_blocks(value_low),
            block_segments,
            block_valid,
        ),
    )
    context = context.reshape(row_count, local_width)
    gated_context = to_low(context * head_cols)
    attn_sum = lax.psum_scatter(
        jnp.dot(gated_context, w_attn_out, preferred_element_type=jnp.float32),
        "hid",
        scatter_dimension=1,
        tiled=True,
    )
    attn_biased = attn_sum + b_attn_out
    resid_one = source + attn_biased * mha_gate * hidden_gate
    normed_one, inv_one = norm_forward(resid_one, model_width)
    ln_one = normed_one * gain_one + shift_one
    hidden_one = ln_one * hidden_gate
    hidden_full = lax.all_gather(to_low(hidden_one), "hid", axis=1, tiled=True)
    pre_act = jnp.dot(hidden_full, w_up, preferred_element_type=jnp.float32) + b_up
    activated, gelu_back = jax.vjp(partial(jax.nn.gelu, approximate=False), pre_act)
    mixed_low = to_low(activated * unit_gate)
    ffn_out = lax.psum_scatter(
        jnp.dot(mixed_low, w_down, preferred_element_type=jnp.float32),
        "hid",
        scatter_dimension=1,
        tiled=True,
    )
    ffn_biased = ffn_out + b_down
    resid_two = hidden_one + ffn_biased * ffn_gate * hidden_gate
    normed_two, inv_two = norm_forward(resid_two, model_width)
    ln_two = normed_two * gain_two + shift_two
    final = ln_two * hidden_gate
    grad_final = (final - teacher.astype(jnp.float32)) * valid_mask.astype(jnp.float32)[:, None]
    grad_gate_hidden = column_sum(grad_final * ln_two)
    grad_ln_two = grad_final * hidden_gate
    grad_gain_two = column_sum(grad_ln_two * normed_two)
    grad_shift_two = column_sum(grad_ln_two)
    grad_resid_two = norm_backward(grad_ln_two * gain_two, normed_two, inv_two, model_width)
    grad_gate_hidden = grad_gate_hidden + column_sum(grad_resid_two * ffn_biased * ffn_gate)
    ffn_scalar = jnp.reshape(jnp.sum(grad_resid_two * ffn_biased * hidden_gate), (1,))
    grad_ffn = grad_resid_two * ffn_gate * hidden_gate
    grad_b_down = column_sum(grad_ffn)
    grad_ffn_full = lax.all_gather(to_low(grad_ffn), "hid", axis=1, tiled=True)
    grad_mixed = contract(grad_ffn_full, w_down, 1, 1)
    grad_w_down = contract(mixed_low, grad_ffn_full, 0, 0)
    grad_gate_unit = column_sum(grad_mixed * activated)
    grad_pre = to_low(gelu_back(grad_mixed * unit_gate)[0])
    grad_b_up = column_sum(grad_pre.astype(jnp.float32))
    grad_w_up = contract(hidden_full, grad_pre, 0, 0)
    grad_hidden_part = lax.psum_scatter(
        contract(grad_pre, w_up, 1, 1), "hid", scatter_dimension=1, tiled=True
    )
    grad_hidden_one = grad_resid_two + grad_hidden_part
    grad_gate_hidden = grad_gate_hidden + column_sum(grad_hidden_one * ln_one)
    grad_ln_one = grad_hidden_one * hidden_gate
    grad_gain_one = column_sum(grad_ln_one * normed_one)
    grad_shift_one = column_sum(grad_ln_one)
    grad_resid_one = norm_backward(grad_ln_one * gain_one, normed_one, inv_one, model_width)
    grad_gate_hidden = grad_gate_hidden + column_sum(grad_resid_one * attn_biased * mha_gate)
    mha_scalar = jnp.reshape(jnp.sum(grad_resid_one * attn_biased * hidden_gate), (1,))
    grad_attn = grad_resid_one * mha_gate * hidden_gate
    grad_b_attn_out = column_sum(grad_attn)
    grad_attn_full = lax.all_gather(to_low(grad_attn), "hid", axis=1, tiled=True)
    grad_context = contract(grad_attn_full, w_attn_out, 1, 1)
    grad_w_attn_out = contract(gated_context, grad_attn_full, 0, 0)
    grad_gate_head = jnp.sum(
        (grad_context * context).reshape(row_count, head_count, HD), axis=(0, 2)
    )
    grad_context_low = to_low(grad_context * head_cols)
    grad_q, grad_k, grad_v = lax.map(
        attend_backward,
        (
            to_blocks(query_low),
            to_blocks(key_low),
            to_blocks(value_low),
            block_segments,
            block_valid,
            log_total,
            to_blocks(grad_context_low),
        ),
    )
    grad_query = to_low(grad_q.reshape(row_count, local_width))
    grad_key = to_low(grad_k.reshape(row_count, local_width))
    grad_value = to_low(grad_v.reshape(row_count, local_width))
    grad_b_query = column_sum(grad_query.astype(jnp.float32))
    grad_b_value = column_sum(grad_value.astype(jnp.float32))
    grad_w_query = contract(inputs_full, grad_query, 0, 0)
    grad_w_key = contract(inputs_full, grad_key, 0, 0)
    grad_w_value = contract(inputs_full, grad_value, 0, 0)
    back_sum = (
        contract(grad_query, w_query, 1, 1)
        + contract(grad_key, w_key, 1, 1)
        + contract(grad_value, w_value, 1, 1)
    )
    grad_input = grad_resid_one + lax.psum_scatter(
        back_sum.astype(jnp.bfloat16), "hid", scatter_dimension=1, tiled=True
    ).astype(jnp.float32)
    totals = lax.psum(
        (
            grad_w_up,
            grad_w_down,
            grad_b_up,
            grad_b_down,
            grad_gain_two,
            grad_shift_two,
            grad_gate_unit,
            ffn_scalar,
            grad_w_query,
            grad_w_key,
            grad_w_value,
            grad_w_attn_out,
            grad_b_query,
            grad_b_value,
            grad_b_attn_out,
            grad_gain_one,
            grad_shift_one,
            grad_gate_head,
            grad_gate_hidden,
            mha_scalar,
        ),
        "rows",
    )
    ffn_totals = totals[0:8]
    attn_totals = totals[8:20]
    (
        sum_w_up,
        sum_w_down,
        sum_b_up,
        sum_b_down,
        sum_gain_two,
        sum_shift_two,
        sum_gate_unit,
        sum_ffn_scalar,
    ) = ffn_totals
    (
        sum_w_query,
        sum_w_key,
        sum_w_value,
        sum_w_attn_out,
        sum_b_query,
        sum_b_value,
        sum_b_attn_out,
        sum_gain_one,
        sum_shift_one,
        sum_gate_head,
        sum_gate_hidden,
        sum_mha_scalar,
    ) = attn_totals
    gate_sums = lax.psum(
        (
            sum_mha_scalar,
            sum_ffn_scalar,
            jnp.sum(open_share(head_alpha)),
            jnp.sum(open_share(unit_alpha)),
            jnp.sum(open_share(hidden_alpha)),
        ),
        "hid",
    )
    grad_mha_gate, grad_ffn_gate, head_sum, unit_sum, hidden_sum = gate_sums

    def penalty_part(head_total, unit_total, hidden_total, mha_log, ffn_log):
        return lagrangian(head_total, unit_total, hidden_total, mha_log, ffn_log, lagrange)

    penalty, penalty_back, kept_share = jax.vjp(
        penalty_part, head_sum, unit_sum, hidden_sum, mha_alpha, ffn_alpha, has_aux=True
    )
    grad_head_sum, grad_unit_sum, grad_hidden_sum, grad_mha_open, grad_ffn_open = penalty_back(
        jnp.ones_like(penalty)
    )
    grad_head_alpha = alpha_grad(head_noise, head_alpha, sum_gate_head) + open_grad(
        head_alpha, grad_head_sum
    )
    grad_unit_alpha = alpha_grad(unit_noise, unit_alpha, sum_gate_unit) + open_grad(
        unit_alpha, grad_unit_sum
    )
    grad_hidden_alpha = alpha_grad(hidden_noise, hidden_alpha, sum_gate_hidden) + open_grad(
        hidden_alpha, grad_hidden_sum
    )
    grad_mha_alpha = alpha_grad(mha_noise, mha_alpha, grad_mha_gate) + grad_mha_open
    grad_ffn_alpha = alpha_grad(ffn_noise, ffn_alpha, grad_ffn_gate) + grad_ffn_open
    return (
        final.astype(jnp.bfloat16),
        grad_input,
        sum_w_query,
        sum_b_query,
        sum_w_key,
        sum_w_value,
        sum_b_value,
        sum_w_attn_out,
        sum_b_attn_out,
        sum_gain_one,
        sum_shift_one,
        sum_w_up,
        sum_b_up,
        sum_w_down,
        sum_b_down,
        sum_gain_two,
        sum_shift_two,
        sum_gate_head,
        grad_mha_gate,
        sum_gate_unit,
        grad_ffn_gate,
        sum_gate_hidden,
        grad_head_alpha,
        grad_mha_alpha,
        grad_unit_alpha,
        grad_ffn_alpha,
        grad_hidden_alpha,
        kept_share,
        penalty,
    )


def solution(mesh):
    in_specs = (
        P("rows", "hid"),
        P("rows", "hid"),
        P("rows"),
        P("rows"),
        P(None, "hid"),
        P("hid"),
        P(None, "hid"),
        P(None, "hid"),
        P("hid"),
        P("hid", None),
        P("hid"),
        P("hid"),
        P("hid"),
        P(None, "hid"),
        P("hid"),
        P("hid", None),
        P("hid"),
        P("hid"),
        P("hid"),
        P("hid"),
        P(),
        P("hid"),
        P(),
        P("hid"),
        P("hid"),
        P(),
        P("hid"),
        P(),
        P("hid"),
        P(),
    )
    out_specs = (
        P("rows", "hid"),
        P("rows", "hid"),
        P(None, "hid"),
        P("hid"),
        P(None, "hid"),
        P(None, "hid"),
        P("hid"),
        P("hid", None),
        P("hid"),
        P("hid"),
        P("hid"),
        P(None, "hid"),
        P("hid"),
        P("hid", None),
        P("hid"),
        P("hid"),
        P("hid"),
        P("hid"),
        P(),
        P("hid"),
        P(),
        P("hid"),
        P("hid"),
        P(),
        P("hid"),
        P(),
        P("hid"),
        P(),
        P(),
    )
    return jax.shard_map(body, mesh=mesh, in_specs=in_specs, out_specs=out_specs, check_vma=False)
```

profile of v0, /device:TPU:0, one launch (start us, length us, event | category | flops | bytes accessed | tf_op | source)
XLA Modules:
  0.0 791.1 jit_solution(8584182022896840375)
XLA Ops:
  9.4 1.9 fusion.132
  11.4 10.7 %all-gather.5.cloned.1.call-done = bf16[1024,768]{1,0:T(8,128)(2,1)} async-done(((bf16[1024,384]{1,0:T(8,128)(2,1)}), bf16[1024,768]{1,0:T(8,128)(2,1)}) %all-gather.5.cloned.1.call-update) | async-done | bytes 1572880 | tf_op jit(solution)/shard_map/all_gather | solution.py:178
  22.1 3.4 convolution_convert_fusion
  28.4 2.1 copy.131
  30.5 3.4 add_convert_fusion.2
  36.8 2.1 copy.130
  38.9 3.4 add_convert_fusion.3
  45.1 2.1 copy.129
  47.2 45.1 %while.26 = (s32[]{:T(128)}, f32[2,512,6,64]{1,0,3,2:T(2,128)}, f32[2,6,512,1]{2,1,3,0:T(8,128)S(1)}, bf16[2,512,6,64]{1,3,2,0:T(8,128)(2,1)}, s32[2,512]{1,0:T(...) while((s32[]{:T(128)}, f32[2,512,6,64]{1,0,3,2:T(2,128)}, ...), condition=%wide.region_3.4_spmd, body=%wide.region_0.3_spmd.sunk | while | flops 420739072 | bytes 25160832 | solution.py:182
  47.6 2.3 fusion.194
  51.2 2.8 fusion.195
  54.8 15.0 %dynamic_update_slice.27 = f32[2,512,6,64]{1,0,3,2:T(2,128)} dynamic-update-slice(f32[2,512,6,64]{1,0,3,2:T(2,128)} %get-tuple-element.612, f32[1,512,6,64]{1,0,3,2:T(1,128)S(1)} %copy.188, s32[]{:T(128)S(6)} %copy.197, s32[]{:T(128)} %constant.74.clone.1..sunk, s32[]{:T(128)} %constant.74.clone.1..sunk, s32[]{:T(128)} %constant.74.clone.1..sunk) | dynamic-update-slice | bytes 1572868 | tf_op jit(solution)/shard_map/while/body/jit(dynamic_update_index_in_dim)/dynamic_update_slice | solution.py:182
  70.1 2.3 fusion.194
  73.8 2.8 fusion.195
  77.4 15.0 %dynamic_update_slice.27 = f32[2,512,6,64]{1,0,3,2:T(2,128)} dynamic-update-slice(f32[2,512,6,64]{1,0,3,2:T(2,128)} %get-tuple-element.612, f32[1,512,6,64]{1,0,3,2:T(1,128)S(1)} %copy.188, s32[]{:T(128)S(6)} %copy.197, s32[]{:T(128)} %constant.74.clone.1..sunk, s32[]{:T(128)} %constant.74.clone.1..sunk, s32[]{:T(128)} %constant.74.clone.1..sunk) | dynamic-update-slice | bytes 1572868 | tf_op jit(solution)/shard_map/while/body/jit(dynamic_update_index_in_dim)/dynamic_update_slice | solution.py:182
  92.4 2.9 copy.183
  95.3 3.1 copy.133
  98.3 4.0 fusion.108
  105.4 9.3 %reduce-scatter.7.cloned.1.call-done = f32[1024,384]{1,0:T(8,128)} async-done(((f32[1024,768]{1,0:T(8,128)}), f32[1024,384]{1,0:T(8,128)}) %reduce-scatter.7.cloned.1.call-update) | async-done | bytes 1572880 | tf_op jit(solution)/shard_map/reduce_scatter | solution.py:194
  114.7 1.9 fusion.109
  116.6 2.5 all-reduce.6
  119.2 3.4 multiply_convert_fusion.5
  123.3 10.4 %all-gather.7.cloned.1.call-done = bf16[1024,768]{1,0:T(8,128)(2,1)} async-done(((bf16[1024,384]{1,0:T(8,128)(2,1)}), bf16[1024,768]{1,0:T(8,128)(2,1)}) %all-gather.7.cloned.1.call-update) | async-done | bytes 1572880 | tf_op jit(solution)/shard_map/all_gather | solution.py:205
  133.7 18.5 %multiply_convert_fusion.1 = (bf16[1024,1536]{1,0:T(8,128)(2,1)S(1)}, f32[1024,1536]{1,0:T(8,128)}, f32[1024,1536]{1,0:T(8,128)}) fusion(f32[1536]{0:T(1024)S(1)} %get-tuple-element.456, f32[1536]{0:T(1024)S(1)} %copy-done.51, bf16[1024,768]{1,0:T(8,128)(2,1)} %all-gather.7.cloned.1.call-done, bf16[768,1536]{1,0:T(8,128)(2,1)S(1)} %copy-done), kind=kOutput, calls=%fused_computation.89 | convolution fusion | flops 2521300992 | bytes 19673088 | tf_op jit(solution)/shard_map/dot_general | solution.py:206
  153.8 4.3 fusion.135
  159.7 10.7 %reduce-scatter.9.cloned.1.call-done = f32[1024,384]{1,0:T(8,128)} async-done(((f32[1024,768]{1,0:T(8,128)}), f32[1024,384]{1,0:T(8,128)}) %reduce-scatter.9.cloned.1.call-update) | async-done | bytes 1572880 | tf_op jit(solution)/shard_map/reduce_scatter | solution.py:209
  170.4 3.5 fusion.131
  173.9 2.5 all-reduce.5
  176.4 2.6 multiply_reduce_fusion.5
  178.9 2.5 all-reduce.4
  181.4 4.3 multiply_reduce_fusion.4
  188.4 10.6 %all-gather.9.cloned.1.call-done = bf16[1024,768]{1,0:T(8,128)(2,1)} async-done(((bf16[1024,384]{1,0:T(8,128)(2,1)}), bf16[1024,768]{1,0:T(8,128)(2,1)}) %all-gather.9.cloned.1.call-update) | async-done | bytes 1572880 | tf_op jit(solution)/shard_map/all_gather | solution.py:230
  199.1 9.8 %convert_reduce_fusion = (f32[1536]{0:T(1024)S(1)}, bf16[1024,1536]{1,0:T(8,128)(2,1)S(1)}, f32[1536]{0:T(1024)S(1)}) fusion(f32[1024,1536]{1,0:T(8,128)} %get-tuple-element.442, f32[1536]{0:T(1024)S(1)} %get-tuple-element.456, f32[1024,1536]{1,0:T(8,128)} %get-tuple-element.466, f32[1536]{0:T(1024)S(1)} %copy-done.51, ...), kind=kOutput, calls=%fused_computation.87 | convolution fusion | flops 2448946176 | bytes 19685376 | tf_op jit(solution)/shard_map/dot_general | solution.py:49
  210.6 4.3 fusion.136
  215.0 12.2 %reduce-scatter.11.cloned.1.call-done = f32[1024,384]{1,0:T(8,128)} async-done(((f32[1024,768]{1,0:T(8,128)}), f32[1024,384]{1,0:T(8,128)}) %reduce-scatter.11.cloned.1.call-update) | async-done | bytes 1572880 | tf_op jit(solution)/shard_map/reduce_scatter | solution.py:237
  227.2 3.7 multiply_reduce_fusion.3
  230.9 2.5 all-reduce.3
  233.3 3.2 multiply_reduce_fusion.2
  238.8 11.0 %all-gather.11.cloned.1.call-done = bf16[1024,768]{1,0:T(8,128)(2,1)} async-done(((bf16[1024,384]{1,0:T(8,128)(2,1)}), bf16[1024,768]{1,0:T(8,128)(2,1)}) %all-gather.11.cloned.1.call-update) | async-done | bytes 1572880 | tf_op jit(solution)/shard_map/all_gather | solution.py:250
  249.8 3.3 multiply_reduce_fusion.8
  257.2 73.8 %while.27 = (s32[]{:T(128)}, bf16[2,512,6,64]{1,3,2,0:T(8,128)(2,1)}, bf16[2,512,6,64]{1,3,2,0:T(8,128)(2,1)}, bf16[2,512,6,64]{1,3,2,0:T(8,128)(2,1)S(1)}, bf16...) while((s32[]{:T(128)}, ...), condition=%wide.region_25.26_spmd, body=%wide.region_23.25_spmd.sunk | while | flops 1048322048 | bytes 101178536 | solution.py:257
  257.8 2.1 fusion.207
  262.6 4.6 fusion.206
  267.2 13.5 %fusion.209 = bf16[2,512,6,64]{1,3,2,0:T(8,128)(2,1)} fusion(bf16[2,512,6,64]{1,3,2,0:T(8,128)(2,1)} %get-tuple-element.645, s32[]{:T(128)S(6)} %copy.207, f32[6,512,512]{1,2,0:T(8,128)} %fusion.206, f32[6,512,512]{1,2,0:T(8,128)} %copy-done.2, f32[6,512]{1,0:T(8,128)S(1)} %dynamic-slice_bitcast_fusion.2, pred[512,512]{0,1:T(8,128)(4,1)S(1)} %or_and_fusion.5, ...), kind=kOutput, calls=%fused_computation.46.clone.1 | convolution fusion | flops 218631680 | bytes 26903552 | tf_op jit(solution)/shard_map/while/body/eval_jaxpr/hqk,qhd->khd/dot_general | solution.py:95
  280.7 13.4 %fusion.208 = bf16[2,512,6,64]{1,3,2,0:T(8,128)(2,1)} fusion(bf16[2,512,6,64]{1,3,2,0:T(8,128)(2,1)} %get-tuple-element.644, s32[]{:T(128)S(6)} %copy.207, f32[6,512,512]{1,2,0:T(8,128)} %fusion.206, f32[6,512,512]{1,2,0:T(8,128)} %copy-done.2, f32[6,512]{1,0:T(8,128)S(1)} %dynamic-slice_bitcast_fusion.2, pred[512,512]{0,1:T(8,128)(4,1)S(1)} %or_and_fusion.5, ...), kind=kOutput, calls=%fused_computation.44.clone.1 | convolution fusion | flops 218631680 | bytes 26903552 | tf_op jit(solution)/shard_map/while/body/eval_jaxpr/hqk,khd->qhd/dot_general | solution.py:94
  294.4 2.1 fusion.207
  299.2 4.6 fusion.206
  303.8 13.5 %fusion.209 = bf16[2,512,6,64]{1,3,2,0:T(8,128)(2,1)} fusion(bf16[2,512,6,64]{1,3,2,0:T(8,128)(2,1)} %get-tuple-element.645, s32[]{:T(128)S(6)} %copy.207, f32[6,512,512]{1,2,0:T(8,128)} %fusion.206, f32[6,512,512]{1,2,0:T(8,128)} %copy-done.2, f32[6,512]{1,0:T(8,128)S(1)} %dynamic-slice_bitcast_fusion.2, pred[512,512]{0,1:T(8,128)(4,1)S(1)} %or_and_fusion.5, ...), kind=kOutput, calls=%fused_computation.46.clone.1 | convolution fusion | flops 218631680 | bytes 26903552 | tf_op jit(solution)/shard_map/while/body/eval_jaxpr/hqk,qhd->khd/dot_general | solution.py:95
  317.3 13.5 %fusion.208 = bf16[2,512,6,64]{1,3,2,0:T(8,128)(2,1)} fusion(bf16[2,512,6,64]{1,3,2,0:T(8,128)(2,1)} %get-tuple-element.644, s32[]{:T(128)S(6)} %copy.207, f32[6,512,512]{1,2,0:T(8,128)} %fusion.206, f32[6,512,512]{1,2,0:T(8,128)} %copy-done.2, f32[6,512]{1,0:T(8,128)S(1)} %dynamic-slice_bitcast_fusion.2, pred[512,512]{0,1:T(8,128)(4,1)S(1)} %or_and_fusion.5, ...), kind=kOutput, calls=%fused_computation.44.clone.1 | convolution fusion | flops 218631680 | bytes 26903552 | tf_op jit(solution)/shard_map/while/body/eval_jaxpr/hqk,khd->qhd/dot_general | solution.py:94
  331.0 1.9 copy.140
  337.6 2.2 add_convert_fusion.1
  339.8 2.6 copy.150
  342.5 7.4 fusion.140
  349.9 4.6 fusion.139
  354.5 1.8 convolution_bitcast_fusion.2
  356.3 1.8 convolution_bitcast_fusion
  358.1 1.8 convolution_bitcast_fusion.1
  359.9 1.8 fusion.107
  363.8 82.1 %all-reduce = (f32[384]{0:T(512)}, f32[384]{0:T(512)}, f32[384]{0:T(512)}, f32[384]{0:T(512)}, f32[384]{0:T(512)}, /*index=5*/f32[1536]{0:T(1024)}, f32[384]{0:T...) all-reduce(f32[384]{0:T(512)S(1)} %reduce_sum.308, ...), channel_id=1, replica_groups=mesh['rows'=16,'hid'=2] {'rows'}, use_global_device_ids=true, to_apply=%region_29.30 | all-reduce | flops 6536 | bytes 52288 | tf_op jit(solution)/shard_map/psum | solution.py:285
  445.9 3.1 all-reduce.2
  460.7 303.4 %all-reduce.9.cloned.1.call-done = (f32[768,384]{0,1:T(8,128)}, f32[768,384]{0,1:T(8,128)}, f32[768,384]{0,1:T(8,128)}, f32[384,768]{1,0:T(8,128)}, f32[768,1536]{1,0:T(8,128)}, /*index=5*/f32[1536,768]{1,0:T(8,128)}) async-done(((f32[768,384]{0,1:T(8,128)}, f32[768,384]{0,1:T(8,128)}, f32[768,384]{0,1:T(8,128)}, f32[384,768]{1,0:T(8,128)}, f32[768,1536]{1,0:T(8,128)}, /*index=5*/f32[1536,768]{1,0:T(8,128)}), ...) | async-done | bytes 14155792 | tf_op jit(solution)/shard_map/psum | solution.py:285
  764.1 2.8 copy.143
  770.7 5.5 copy.228
  776.2 2.4 copy.229
  (209 shorter events, 52.2 us)
Async XLA Ops:
  7.2 126.5 %copy-start = (bf16[768,1536]{1,0:T(8,128)(2,1)S(1)}, bf16[768,1536]{1,0:T(8,128)(2,1)}, u32[]{:S(2)}) copy-start(bf16[768,1536]{1,0:T(8,128)(2,1)} %param.50) | copy-start | bytes 7077892
  7.2 14.9 %all-gather.5.cloned.1.call-start = ((), (), s32[]{:S(2)}) async-start(), calls=%async_computation.4 | async-start | bytes 2359296 | tf_op jit(solution)/shard_map/all_gather | solution.py:178
  8.0 106.7 %reduce-scatter.7.cloned.1.call-start = ((), (), s32[]{:S(2)}) async-start(), calls=%async_computation.5 | async-start | bytes 4718592 | tf_op jit(solution)/shard_map/reduce_scatter | solution.py:194
  25.5 5.0 copy-start.52
  33.9 5.0 copy-start.53
  95.3 3.1 copy-start.23
  102.4 1.8 copy-start.39
  102.4 1.8 copy-start.43
  102.4 12.3 %copy-start.8 = (bf16[1024,384]{1,0:T(8,128)(2,1)S(1)}, bf16[1024,384]{1,0:T(8,128)(2,1)}, u32[]{:S(2)}) copy-start(bf16[1024,384]{1,0:T(8,128)(2,1)} %param.37) | copy-start | bytes 2359300
  102.4 12.3 %copy-start.34 = (f32[384]{0:T(512)S(1)}, f32[384]{0:T(512)}, u32[]{:S(2)}) copy-start(f32[384]{0:T(512)} %param.47) | copy-start | bytes 4612
  102.4 16.7 %copy-start.28 = (f32[384]{0:T(512)S(1)}, f32[384]{0:T(512)}, u32[]{:S(2)}) copy-start(f32[384]{0:T(512)} %param.48) | copy-start | bytes 4612
  102.4 16.7 %copy-start.33 = (f32[384]{0:T(512)S(1)}, f32[384]{0:T(512)}, u32[]{:S(2)}) copy-start(f32[384]{0:T(512)} %param.49) | copy-start | bytes 4612
  102.5 31.2 %all-gather.7.cloned.1.call-start = ((), (), s32[]{:S(2)}) async-start(), calls=%async_computation.6 | async-start | bytes 2359296 | tf_op jit(solution)/shard_map/all_gather | solution.py:205
  119.1 3.5 copy-start.29
  119.2 3.5 copy-start.31
  119.2 14.5 %copy-start.51 = (f32[1536]{0:T(1024)S(1)}, f32[1536]{0:T(1024)}, u32[]{:S(2)}) copy-start(f32[1536]{0:T(1024)} %param.51) | copy-start | bytes 18436
  122.6 47.8 %reduce-scatter.9.cloned.1.call-start = ((), (), s32[]{:S(2)}) async-start(), calls=%async_computation.7 | async-start | bytes 4718592 | tf_op jit(solution)/shard_map/reduce_scatter | solution.py:209
  133.7 20.2 %copy-start.49 = (bf16[1536,768]{1,0:T(8,128)(2,1)S(1)}, bf16[1536,768]{1,0:T(8,128)(2,1)}, u32[]{:S(2)}) copy-start(bf16[1536,768]{1,0:T(8,128)(2,1)} %param.52) | copy-start | bytes 7077892
  152.2 1.7 copy-start.54
  158.1 12.2 %copy-start.36 = (f32[384]{0:T(512)S(1)}, f32[384]{0:T(512)}, u32[]{:S(2)}) copy-start(f32[384]{0:T(512)} %param.53) | copy-start | bytes 4612
  158.1 41.0 %all-gather.9.cloned.1.call-start = ((), (), s32[]{:S(2)}) async-start(), calls=%async_computation.8 | async-start | bytes 2359296 | tf_op jit(solution)/shard_map/all_gather | solution.py:230
  170.4 6.0 copy-start.17
  170.4 6.0 copy-start.37
  170.4 6.0 copy-start.38
  185.8 1.2 copy-start.7
  188.0 39.2 %reduce-scatter.11.cloned.1.call-start = ((), (), s32[]{:S(2)}) async-start(), calls=%async_computation.9 | async-start | bytes 4718592 | tf_op jit(solution)/shard_map/reduce_scatter | solution.py:237
  208.9 1.7 copy-start.11
  214.9 12.3 %copy-start.3 = (f32[1024,384]{1,0:T(8,128)S(1)}, f32[1024,384]{1,0:T(8,128)}, u32[]{:S(2)}) copy-start(f32[1024,384]{1,0:T(8,128)} %get-tuple-element.444) | copy-start | bytes 4718596
  215.0 34.9 %all-gather.11.cloned.1.call-start = ((), (), s32[]{:S(2)}) async-start(), calls=%async_computation.10 | async-start | bytes 2359296 | tf_op jit(solution)/shard_map/all_gather | solution.py:250
  236.5 13.3 %copy-start.4 = (f32[1024,384]{1,0:T(8,128)S(1)}, f32[1024,384]{1,0:T(8,128)}, u32[]{:S(2)}) copy-start(f32[1024,384]{1,0:T(8,128)} %copy.133) | copy-start | bytes 4718596
  236.5 13.3 %copy-start.24 = (bf16[384,768]{1,0:T(8,128)(2,1)S(1)}, bf16[384,768]{1,0:T(8,128)(2,1)}, u32[]{:S(2)}) copy-start(bf16[384,768]{1,0:T(8,128)(2,1)} %param.46) | copy-start | bytes 1769476
  238.7 219.2 %reduce-scatter.13.cloned.1.call-start = ((), (), s32[]{:S(2)}) async-start(), calls=%async_computation.11 | async-start | bytes 2359296
  259.9 2.7 copy-start.2
  296.6 2.7 copy-start.2
  333.0 1.3 copy-start.9
  333.1 2.1 copy-start.13
  333.9 1.3 copy-start.25
  335.2 2.4 copy-start.15
  335.2 1.4 copy-start.26
  336.3 1.3 copy-start.27
  342.5 421.7 %all-reduce.9.cloned.1.call-start = ((), (), s32[]{:S(2)}) async-start(), calls=%async_computation.12 | async-start | bytes 28311552 | tf_op jit(solution)/shard_map/psum | solution.py:285
  342.5 7.4 copy-start.12
  342.5 7.4 copy-start.18
  349.9 4.6 copy-start.16
  349.9 4.6 copy-start.50
  356.3 1.8 copy-start.14
  358.1 1.8 copy-start.19
  361.8 1.6 copy-start.10
  361.8 94.4 %copy-start.46 = (f32[6]{0:T(128)S(1)}, f32[6]{0:T(128)}, u32[]{:S(2)}) copy-start(f32[6]{0:T(128)} %get-tuple-element.434) | copy-start | bytes 76
  361.8 94.4 %copy-start.47 = (f32[6]{0:T(128)S(1)}, f32[6]{0:T(128)}, u32[]{:S(2)}) copy-start(f32[6]{0:T(128)} %get-tuple-element.465) | copy-start | bytes 76
  361.8 94.9 %copy-start.40 = (f32[384]{0:T(512)S(1)}, f32[384]{0:T(512)}, u32[]{:S(2)}) copy-start(f32[384]{0:T(512)} %param.60) | copy-start | bytes 4612
  361.8 94.9 %copy-start.41 = (f32[384]{0:T(512)S(1)}, f32[384]{0:T(512)}, u32[]{:S(2)}) copy-start(f32[384]{0:T(512)} %get-tuple-element.448) | copy-start | bytes 4612
  361.8 95.5 %copy-start.30 = (f32[1536]{0:T(1024)S(1)}, f32[1536]{0:T(1024)}, u32[]{:S(2)}) copy-start(f32[1536]{0:T(1024)} %param.58) | copy-start | bytes 18436
  361.8 95.5 %copy-start.32 = (f32[1536]{0:T(1024)S(1)}, f32[1536]{0:T(1024)}, u32[]{:S(2)}) copy-start(f32[1536]{0:T(1024)} %param.63) | copy-start | bytes 18436
  361.9 97.6 %copy-start.6 = (f32[1024,384]{1,0:T(8,128)S(1)}, f32[1024,384]{1,0:T(8,128)}, u32[]{:S(2)}) copy-start(f32[1024,384]{1,0:T(8,128)} %copy-done.5) | copy-start | bytes 4718596
  445.9 14.8 %copy-start.42 = (f32[1536]{0:T(1024)}, f32[1536]{0:T(1024)S(1)}, u32[]{:S(2)}) copy-start(f32[1536]{0:T(1024)S(1)} %get-tuple-element.686) | copy-start | bytes 18436
  445.9 14.8 %copy-start.44 = (f32[384]{0:T(512)}, f32[384]{0:T(512)S(1)}, u32[]{:S(2)}) copy-start(f32[384]{0:T(512)S(1)} %get-tuple-element.688) | copy-start | bytes 4612
  445.9 14.8 %copy-start.48 = (f32[6]{0:T(128)}, f32[6]{0:T(128)S(1)}, u32[]{:S(2)}) copy-start(f32[6]{0:T(128)S(1)} %get-tuple-element.684) | copy-start | bytes 76
  764.1 2.8 copy-start.22
  764.1 4.2 copy-start.21
  766.9 2.8 copy-start.20
  769.7 6.5 slice-start
  770.7 5.5 slice-start.1
  776.2 3.4 copy-start.1
  (3 other events, 2.6 us)
Sparse Core Ops, SparseCore 0:
  9.6 12.4 all-gather.4
  102.6 12.0 reduce-scatter.6
  122.7 10.9 all-gather.6
  158.3 12.0 reduce-scatter.8
  188.1 10.9 all-gather.8
  215.1 12.0 reduce-scatter.10
  238.9 10.9 all-gather.10
  342.6 10.2 reduce-scatter.12
  362.0 402.0 all-reduce.8
where the time goes:
time: 803 us; the launch traced here: 791 us
  waiting for transfers between devices  379 us (47%)
  matrix products  159 us (20%)
  blocking collectives  95.2 us (12%)
  local copies, waits for them, and re-layouts  91.2 us (11%)
  other arithmetic  35.8 us (4%)
  between operations  29.7 us (4%)
    psum x1, waiting for transfers between devices, body(): lax.psum((grad_w_up, grad_w_down, grad_b_up, grad_b_down, grad_gain_two,...  303 us
    psum x1, blocking collectives, body(): lax.psum((grad_w_up, grad_w_down, grad_b_up, grad_b_down, grad_gain_two,...  82.1 us
    dot_general x12, matrix products, contract(): lax.dot_general(first, second, (((first_dim,), (second_dim,)), ((), ())),...  40.8 us
    dynamic_update_slice x4, local copies, waits for them, and re-layouts, body(): lax.map(attend_forward, (to_blocks(query_low), to_blocks(key_low), to_blo...  31.6 us
    unnamed x124, local copies, waits for them, and re-layouts  29.6 us
    dot_general x2, matrix products, attend_backward(): jnp.einsum('hqk,qhd->khd', grad_raw, query_block, preferred_element_type=...  27 us
    dot_general x2, matrix products, attend_backward(): jnp.einsum('hqk,khd->qhd', grad_raw, key_block, preferred_element_type=jn...  26.9 us
    dot_general x1, matrix products, body(): jnp.dot(hidden_full, w_up, preferred_element_type=jnp.float32) + b_up  18.5 us
  transfers between devices with their start and end apart: 9, of which 8 were waited for; matrix products, arithmetic and copies ran while one was open for 4% of the time, Pallas kernels for 0%

commit v1 on v0

v1 whole, which is shorter than its diff:
```python
from functools import partial
import math

import jax
import jax.numpy as jnp
from jax import lax
from jax.experimental import pallas as pl
from jax.experimental.pallas import tpu as pltpu
from jax.sharding import PartitionSpec as P

HD = 64
BLOCK = 512
LANES = 128
TILE = 512

norm_eps = 1e-05
gate_temper = 2.0 / 3.0
stretch_low = -0.1
stretch_high = 1.1
target_share = 0.4
masked_score = -1000000000.0
open_shift = gate_temper * math.log(-stretch_low / stretch_high)
vmem_bytes = 58 * 2**20

f32 = jnp.float32
bf16 = jnp.bfloat16


def to_low(values_in):
    return values_in.astype(bf16)


def contract(first, second, first_dim, second_dim):
    return lax.dot_general(
        first, second, (((first_dim,), (second_dim,)), ((), ())), preferred_element_type=f32
    )


def column_sum(values_in):
    return jnp.sum(values_in, axis=0, keepdims=True)


def row_sum(values_in):
    return jnp.sum(values_in, axis=1, keepdims=True)


def sigmoid(values_in):
    return 1.0 / (1.0 + jnp.exp(-values_in))


def stretched(gate_noise, log_alpha):
    relaxed = sigmoid(
        (jnp.log(gate_noise) - jnp.log(1.0 - gate_noise) + log_alpha) / gate_temper
    )
    return relaxed, relaxed * (stretch_high - stretch_low) + stretch_low


def hard_concrete(gate_noise, log_alpha):
    return jnp.clip(stretched(gate_noise, log_alpha)[1], 0.0, 1.0)


def gate_slope(gate_noise, log_alpha):
    relaxed, wide = stretched(gate_noise, log_alpha)
    slope = relaxed * (1.0 - relaxed) * ((stretch_high - stretch_low) / gate_temper)
    return jnp.where((wide > 0.0) & (wide < 1.0), slope, 0.0)


def open_share(log_alpha):
    return sigmoid(log_alpha - open_shift)


class Pack:
    def __init__(self, width, units):
        self.width, self.units = width, units
        at = 0
        for name in ("b_query", "b_value", "b_attn_out", "gain_one", "shift_one"):
            setattr(self, name, (at, width))
            at += width
        for name in ("b_down", "gain_two", "shift_two", "hidden_alpha", "hidden_noise"):
            setattr(self, name, (at, width))
            at += width
        for name in ("b_up", "unit_alpha", "unit_noise"):
            setattr(self, name, (at, units))
            at += units
        for name in ("head_alpha", "head_noise", "scalars"):
            setattr(self, name, (at, LANES))
            at += LANES
        self.total = at


def take(pack_ref, spot):
    return pack_ref[:, spot[0] : spot[0] + spot[1]]


def natural(core, own, peer):
    at_peer = core.astype(f32)
    at_own = 1.0 - at_peer
    return jnp.concatenate((own * at_own + peer * at_peer, peer * at_own + own * at_peer), axis=1)


def both(core, own_ref, peer_ref, spot):
    return natural(core, take(own_ref, spot), take(peer_ref, spot))


def hidden_gates(core, pack, own_ref, peer_ref):
    return hard_concrete(
        both(core, own_ref, peer_ref, pack.hidden_noise),
        both(core, own_ref, peer_ref, pack.hidden_alpha),
    )


def head_row(pack, own_ref, peer_ref, heads):
    parts = []
    for ref in (own_ref, peer_ref):
        gates = hard_concrete(take(ref, pack.head_noise), take(ref, pack.head_alpha))
        for at in range(heads):
            parts.append(jnp.broadcast_to(gates[:, at : at + 1], (1, HD)))
    return jnp.concatenate(parts, axis=1)


def scalar_gate(pack, own_ref, at):
    numbers = take(own_ref, pack.scalars)
    return hard_concrete(numbers[:, at + 1 : at + 2], numbers[:, at : at + 1])


def half_mask(side, dtype):
    lane = lax.broadcasted_iota(jnp.int32, (1, LANES), 1)
    inside = (lane < HD) if side == 0 else (lane >= HD)
    return jnp.where(inside, 1.0, 0.0).astype(dtype)


def pick_half(first, second):
    lane = lax.broadcasted_iota(jnp.int32, (1, LANES), 1)
    return jnp.where(lane < HD, first, second)


def norm_back(grad_normed, normed, inv_scale):
    width = normed.shape[1]
    mean_grad = row_sum(grad_normed) * (1.0 / width)
    mean_both = row_sum(grad_normed * normed) * (1.0 / width)
    return inv_scale * (grad_normed - mean_grad - normed * mean_both)


def norm_forward(resid):
    width = resid.shape[1]
    row_mean = row_sum(resid) * (1.0 / width)
    row_var = row_sum(resid * resid) * (1.0 / width) - row_mean * row_mean
    inv_scale = lax.rsqrt(row_var + norm_eps)
    return (resid - row_mean) * inv_scale, inv_scale


def own_rows(ref, core):
    return ref[pl.ds(pl.multiple_of(core * BLOCK, BLOCK), BLOCK), :]


def attend_kernel(
    pack,
    core_ref,
    x_own,
    x_peer,
    wq_own,
    wk_own,
    wv_own,
    wq_peer,
    wk_peer,
    wv_peer,
    wa_own,
    wa_peer,
    pack_own,
    pack_peer,
    segments,
    valid,
    weights_out,
    query_out,
    key_out,
    value_out,
    context_out,
    gated_own_out,
    gated_peer_out,
    stats_out,
    biased_out,
    normed_out,
    hidden_out,
    x_nat,
    mask_bias,
    gate_row,
    gated,
):
    pair = pl.program_id(0)
    core = core_ref[0]
    width = pack.width
    heads = width // HD

    @pl.when(pair == 0)
    def _():
        own_at = pl.multiple_of(core * width, LANES)
        peer_at = pl.multiple_of((1 - core) * width, LANES)
        x_nat[:, pl.ds(own_at, width)] = own_rows(x_own, core)
        x_nat[:, pl.ds(peer_at, width)] = own_rows(x_peer, core)
        source = x_nat[...]
        for at, query_ref, key_ref, value_ref, row in (
            (0, wq_own, wk_own, wv_own, pack_own),
            (width, wq_peer, wk_peer, wv_peer, pack_peer),
        ):
            query = to_low(contract(source, query_ref[...], 1, 0) + take(row, pack.b_query))
            query_out[:, at : at + width] = query * jnp.asarray(HD ** (-0.5), bf16)
            key_out[:, at : at + width] = to_low(contract(source, key_ref[...], 1, 0))
            value_out[:, at : at + width] = to_low(
                contract(source, value_ref[...], 1, 0) + take(row, pack.b_value)
            )
        gate_row[...] = head_row(pack, pack_own, pack_peer, heads)

        lanes_of = BLOCK // LANES
        start = core * lanes_of

        def line(ref):
            return jnp.concatenate(
                [ref[pl.ds(start + at, 1), :] for at in range(lanes_of)], axis=1
            ).astype(f32)

        segment_line, valid_line = line(segments), line(valid)
        segment_side = jnp.broadcast_to(segment_line, (LANES, BLOCK)).T[:, 0:1]
        valid_side = jnp.broadcast_to(valid_line, (LANES, BLOCK)).T[:, 0:1]
        allowed = (segment_side == segment_line) & ((valid_line == 1.0) | (valid_side == 0.0))
        mask_bias[...] = jnp.where(allowed, 0.0, masked_score)

    columns = pl.ds(pl.multiple_of(pair * LANES, LANES), LANES)
    query, key, value = query_out[:, columns], key_out[:, columns], value_out[:, columns]
    ones = jnp.ones((BLOCK, LANES), bf16)
    value_wide = jnp.concatenate((value, ones), axis=1)
    contexts = []
    lane = lax.broadcasted_iota(jnp.int32, (1, LANES), 1)
    stats = stats_out[...]
    for side in range(2):
        scores = contract(query * half_mask(side, bf16), key, 1, 1) + mask_bias[...]
        row_top = jnp.max(scores, axis=1, keepdims=True)
        weights = to_low(jnp.exp(scores - row_top))
        weights_out[side] = weights
        summed = contract(weights, value_wide, 1, 0)
        inverse = 1.0 / summed[:, LANES : 2 * LANES]
        contexts.append(summed[:, :LANES] * inverse)
        stats = jnp.where(lane == 2 * pair + side, inverse, stats)
    stats_out[...] = stats
    context = pick_half(contexts[0], contexts[1])
    context_out[:, columns] = to_low(context)
    gated[:, columns] = to_low(context * gate_row[:, columns])

    @pl.when(pair == pl.num_programs(0) - 1)
    def _():
        gated_own, gated_peer = gated[:, :width], gated[:, width:]
        gated_own_out[...] = gated_own
        gated_peer_out[...] = gated_peer
        attn_sum = contract(gated_own, wa_own[...], 1, 0) + contract(gated_peer, wa_peer[...], 1, 0)
        biased = attn_sum + both(core, pack_own, pack_peer, pack.b_attn_out)
        biased_out[...] = biased
        gates = hidden_gates(core, pack, pack_own, pack_peer)
        mha_gate = scalar_gate(pack, pack_own, 0)
        resid = x_nat[...].astype(f32) + biased * (mha_gate * gates)
        normed, inv_scale = norm_forward(resid)
        normed_out[...] = normed
        gain = both(core, pack_own, pack_peer, pack.gain_one)
        shift = both(core, pack_own, pack_peer, pack.shift_one)
        hidden_out[...] = to_low((normed * gain + shift) * gates)
        stats_out[...] = jnp.where(lane == LANES - 1, inv_scale, stats)


def gelu_parts(pre_act):
    size = jnp.abs(pre_act) * (0.5**0.5)
    inverse = 1.0 / (1.0 + 0.3275911 * size)
    falling = jnp.exp(-size * size)
    poly = 1.061405429 * inverse - 1.453152027
    poly = poly * inverse + 1.421413741
    poly = poly * inverse - 0.284496736
    poly = poly * inverse + 0.254829592
    tail = 0.5 * poly * inverse * falling
    return jnp.where(pre_act >= 0.0, 1.0 - tail, tail), falling * (1.0 / math.sqrt(2.0 * math.pi))


def ffn_forward_kernel(
    pack,
    core_ref,
    hidden,
    normed,
    up_own,
    up_peer,
    down_own,
    down_peer,
    pack_own,
    pack_peer,
    teacher_own,
    teacher_peer,
    valid,
    mixed_own_out,
    mixed_peer_out,
    active_out,
    slope_out,
    output_own,
    output_peer,
    grad_resid_out,
    grad_ffn_out,
    sums_out,
    total,
):
    step = pl.program_id(0)
    core = core_ref[0]
    own_steps = pl.num_programs(0) // 2
    width, units = pack.width, pack.units

    def tile(at, up_ref, down_ref, pack_ref, mixed_ref):
        spot = pl.multiple_of(at * TILE, TILE)

        def cut(place):
            return pack_ref[:, pl.ds(place[0] + spot, TILE)]

        pre_act = contract(hidden[...], up_ref[...], 1, 0) + cut(pack.b_up)
        whole, density = gelu_parts(pre_act)
        active = pre_act * whole
        unit_gate = hard_concrete(cut(pack.unit_noise), cut(pack.unit_alpha))
        mixed = to_low(active * unit_gate)
        mixed_ref[...] = mixed
        active_out[...] = to_low(active)
        slope_out[...] = to_low((whole + pre_act * density) * unit_gate)
        return contract(mixed, down_ref[...], 1, 0)

    @pl.when(step == 0)
    def _():
        total[...] = tile(step, up_own, down_own, pack_own, mixed_own_out)

    @pl.when((step > 0) & (step < own_steps))
    def _():
        total[...] += tile(step, up_own, down_own, pack_own, mixed_own_out)

    @pl.when(step >= own_steps)
    def _():
        total[...] += tile(step - own_steps, up_peer, down_peer, pack_peer, mixed_peer_out)

    @pl.when(step == pl.num_programs(0) - 1)
    def _():
        gates = hidden_gates(core, pack, pack_own, pack_peer)
        ffn_gate = scalar_gate(pack, pack_own, 2)

        def vector(spot):
            return both(core, pack_own, pack_peer, spot)

        biased = total[...] + vector(pack.b_down)
        hidden_one = (normed[...] * vector(pack.gain_one) + vector(pack.shift_one)) * gates
        normed_two, inv_two = norm_forward(hidden_one + biased * (ffn_gate * gates))
        gain = vector(pack.gain_two)
        final = (normed_two * gain + vector(pack.shift_two)) * gates
        final_low = to_low(final)

        def split(own_ref, peer_ref, values_in):
            @pl.when(core == 0)
            def _():
                own_ref[...] = values_in[:, :width]
                peer_ref[...] = values_in[:, width:]

            @pl.when(core == 1)
            def _():
                own_ref[...] = values_in[:, width:]
                peer_ref[...] = values_in[:, :width]

        split(output_own, output_peer, final_low)
        lanes_of = BLOCK // LANES
        start = core * lanes_of
        valid_line = jnp.concatenate(
            [valid[pl.ds(start + at, 1), :] for at in range(lanes_of)], axis=1
        ).astype(f32)
        valid_side = jnp.broadcast_to(valid_line, (LANES, BLOCK)).T[:, 0:1]
        own_at = pl.multiple_of(core * width, LANES)
        peer_at = pl.multiple_of((1 - core) * width, LANES)
        grad_resid_out[:, pl.ds(own_at, width)] = own_rows(teacher_own, core).astype(f32)
        grad_resid_out[:, pl.ds(peer_at, width)] = own_rows(teacher_peer, core).astype(f32)
        grad_final = (final - grad_resid_out[...]) * valid_side
        grad_resid = norm_back(grad_final * (gates * gain), normed_two, inv_two)
        grad_resid_out[...] = grad_resid
        grad_ffn_out[...] = to_low(grad_resid * (ffn_gate * gates))
        sums_out[0:1, :] = column_sum(grad_final * normed_two)
        sums_out[1:2, :] = column_sum(grad_final)
        sums_out[2:3, :] = column_sum(grad_resid * biased)
        sums_out[3:4, :] = column_sum(grad_resid)


def ffn_backward_kernel(
    pack,
    core_ref,
    grad_ffn,
    grad_resid_two,
    normed,
    biased,
    stats,
    active,
    slope,
    up_own,
    up_peer,
    down_own,
    down_peer,
    pack_own,
    pack_peer,
    grad_pre_own,
    grad_pre_peer,
    grad_resid_out,
    grad_attn_out,
    sums_out,
    unit_sums_out,
    total,
):
    step = pl.program_id(0)
    core = core_ref[0]
    own_steps = pl.num_programs(0) // 2
    units = pack.units

    def tile(at, side, up_ref, down_ref, pre_ref):
        grad_mixed = contract(grad_ffn[...], down_ref[...], 1, 1)
        grad_pre = to_low(grad_mixed * slope[...].astype(f32))
        pre_ref[...] = grad_pre
        spot = pl.multiple_of(side * units + at * TILE, TILE)
        unit_sums_out[0:1, pl.ds(spot, TILE)] = column_sum(grad_mixed * active[...].astype(f32))
        unit_sums_out[1:2, pl.ds(spot, TILE)] = column_sum(grad_pre.astype(f32))
        return contract(grad_pre, up_ref[...], 1, 1)

    @pl.when(step == 0)
    def _():
        total[...] = grad_resid_two[...] + tile(step, core, up_own, down_own, grad_pre_own)

    @pl.when((step > 0) & (step < own_steps))
    def _():
        total[...] += tile(step, core, up_own, down_own, grad_pre_own)

    @pl.when(step >= own_steps)
    def _():
        total[...] += tile(step - own_steps, 1 - core, up_peer, down_peer, grad_pre_peer)

    @pl.when(step == pl.num_programs(0) - 1)
    def _():
        gates = hidden_gates(core, pack, pack_own, pack_peer)
        mha_gate = scalar_gate(pack, pack_own, 0)
        gain = both(core, pack_own, pack_peer, pack.gain_one)
        grad_hidden = total[...]
        sums_out[0:1, :] = column_sum(grad_hidden * normed[...])
        sums_out[1:2, :] = column_sum(grad_hidden)
        inv_scale = stats[:, LANES - 1 : LANES]
        grad_resid = norm_back(grad_hidden * (gates * gain), normed[...], inv_scale)
        grad_resid_out[...] = grad_resid
        grad_attn_out[...] = to_low(grad_resid * (mha_gate * gates))
        sums_out[2:3, :] = column_sum(grad_resid * biased[...])
        sums_out[3:4, :] = column_sum(grad_resid)


def attend_back_kernel(
    pack,
    core_ref,
    weights,
    query_ref,
    key_ref,
    value_ref,
    context_ref,
    stats,
    grad_attn,
    wa_own,
    wa_peer,
    pack_own,
    pack_peer,
    grad_own_out,
    grad_peer_out,
    sums_out,
    gate_row,
):
    pair = pl.program_id(0)
    core = core_ref[0]
    width = pack.width
    own_pairs = pl.num_programs(0) // 2

    @pl.when(pair == 0)
    def _():
        gate_row[...] = head_row(pack, pack_own, pack_peer, width // HD)

    columns = pl.ds(pl.multiple_of(pair * LANES, LANES), LANES)
    lane = lax.broadcasted_iota(jnp.int32, (1, LANES), 1)

    def run(at, side_of, wa_ref, out_ref):
        query, key, value = query_ref[:, columns], key_ref[:, columns], value_ref[:, columns]
        context = context_ref[:, columns].astype(f32)
        grad_context = contract(grad_attn[...], wa_ref[...], 1, 1)
        spot = pl.ds(pl.multiple_of(side_of * width + at * LANES, LANES), LANES)
        sums_out[0:1, spot] = column_sum(grad_context * context)
        inverses = [
            row_sum(jnp.where(lane == 2 * pair + side, stats[...], 0.0)) for side in range(2)
        ]
        grad_low = to_low(grad_context * gate_row[:, columns] * pick_half(inverses[0], inverses[1]))
        product = grad_low.astype(f32) * context
        found = []
        for side in range(2):
            mask = half_mask(side, f32)
            level = row_sum(product * mask)
            grad_probs = contract(grad_low * mask.astype(bf16), value, 1, 1)
            chosen = weights[side]
            grad_raw = to_low(chosen.astype(f32) * (grad_probs - level))
            found.append(
                (
                    contract(grad_raw, key, 1, 0),
                    contract(grad_raw, query, 0, 0),
                    contract(chosen, grad_low, 0, 0),
                )
            )
        grad_query = to_low(pick_half(found[0][0], found[1][0]) * HD ** (-0.5))
        grad_key = to_low(pick_half(found[0][1], found[1][1]))
        grad_value = to_low(pick_half(found[0][2], found[1][2]))
        for place, grad in enumerate((grad_query, grad_key, grad_value)):
            at_lane = pl.multiple_of(place * width + at * LANES, LANES)
            out_ref[:, pl.ds(at_lane, LANES)] = grad
        sums_out[1:2, spot] = column_sum(grad_query.astype(f32))
        sums_out[2:3, spot] = column_sum(grad_value.astype(f32))

    @pl.when(pair < own_pairs)
    def _():
        run(pair, core, wa_own, grad_own_out)

    @pl.when(pair >= own_pairs)
    def _():
        run(pair - own_pairs, 1 - core, wa_peer, grad_peer_out)


def down_grad_kernel(half_ref, mixed, mixed_near, grad, grad_near, out_ref):
    summed = contract(mixed[...], grad[...], 0, 0) + contract(mixed_near[...], grad_near[...], 0, 0)
    out_ref[...] = to_low(summed)


def up_grad_kernel(half_ref, hidden, hidden_near, grad, grad_near, out_ref):
    summed = contract(hidden[...], grad[...], 0, 0) + contract(hidden_near[...], grad_near[...], 0, 0)
    out_ref[...] = to_low(summed)


def attend_grad_kernel(
    width,
    half_ref,
    core_ref,
    x_own,
    x_peer,
    grad,
    grad_near,
    gated,
    gated_near,
    grad_attn,
    grad_attn_near,
    out_ref,
):
    core = core_ref[0]
    half = half_ref[0]

    def from_source(x_ref, at, columns):
        rows = pl.ds(pl.multiple_of(at * width, LANES), width)
        summed = contract(own_rows(x_ref, core), grad[:, columns], 0, 0) + contract(
            own_rows(x_ref, 1 - core), grad_near[:, columns], 0, 0
        )
        for place in range(summed.shape[1] // width):
            out_ref[place, rows, :] = to_low(summed[:, place * width : (place + 1) * width])

    @pl.when(half == 0)
    def _():
        from_source(x_own, core, slice(0, 2 * width))
        from_source(x_peer, 1 - core, slice(0, 2 * width))

    @pl.when(half == 1)
    def _():
        from_source(x_own, core, slice(2 * width, 3 * width))
        from_source(x_peer, 1 - core, slice(2 * width, 3 * width))
        summed = contract(gated[...], grad_attn[...], 0, 0) + contract(
            gated_near[...], grad_attn_near[...], 0, 0
        )
        out_ref[1, :width, :] = to_low(summed[:, :width])
        out_ref[1, width:, :] = to_low(summed[:, width:])


def input_grad_kernel(
    width,
    core_ref,
    grad_resid,
    grad_own,
    grad_peer,
    wq_own,
    wk_own,
    wv_own,
    wq_peer,
    wk_peer,
    wv_peer,
    own_out,
    peer_out,
):
    core = core_ref[0]
    summed = grad_resid[...]
    for grad, weights in (
        (grad_own, (wq_own, wk_own, wv_own)),
        (grad_peer, (wq_peer, wk_peer, wv_peer)),
    ):
        for place, weight in enumerate(weights):
            summed = summed + contract(
                grad[:, place * width : (place + 1) * width], weight[...], 1, 1
            )

    @pl.when(core == 0)
    def _():
        own_out[...] = summed[:, :width]
        peer_out[...] = summed[:, width:]

    @pl.when(core == 1)
    def _():
        own_out[...] = summed[:, width:]
        peer_out[...] = summed[:, :width]


def place_kernel(bit_ref, half, other, out_ref):
    step = pl.program_id(0)

    @pl.when(step < 2)
    def _():
        out_ref[...] = half[...].astype(f32)

    @pl.when(step >= 2)
    def _():
        out_ref[...] = other[...].astype(f32)


def place_attend_kernel(bit_ref, half, other, query_out, key_out, value_out, attn_out):
    width = attn_out.shape[0]

    def put(first, second):
        query_out[...] = first[0].astype(f32)
        key_out[...] = first[1].astype(f32)
        value_out[...] = second[0].astype(f32)
        attn_out[:, :width] = second[1, :width, :].astype(f32)
        attn_out[:, width:] = second[1, width:, :].astype(f32)

    @pl.when(bit_ref[0] == 0)
    def _():
        put(half, other)

    @pl.when(bit_ref[0] == 1)
    def _():
        put(other, half)


def finish_kernel(
    pack,
    core_ref,
    sums,
    pack_own,
    pack_peer,
    b_query,
    b_value,
    b_attn_out,
    gain_one,
    shift_one,
    b_up,
    b_down,
    gain_two,
    shift_two,
    head_gate,
    mha_gate,
    unit_gate,
    ffn_gate,
    hidden_gate,
    head_alpha,
    mha_alpha,
    unit_alpha,
    ffn_alpha,
    hidden_alpha,
    share_out,
    penalty_out,
):
    core = core_ref[0]
    width, units = pack.width, pack.units
    columns = pl.ds(pl.multiple_of(core * width, LANES), width)
    heads = width // HD

    def own(row):
        return sums[row : row + 1, columns]

    def vector(spot):
        return take(pack_own, spot)

    gates = hard_concrete(vector(pack.hidden_noise), vector(pack.hidden_alpha))
    mha, ffn = scalar_gate(pack, pack_own, 0), scalar_gate(pack, pack_own, 2)
    gain_two[...] = gates * own(0)
    shift_two[...] = gates * own(1)
    b_down[...] = (ffn * gates) * own(3)
    gain_one[...] = gates * own(4)
    shift_one[...] = gates * own(5)
    b_attn_out[...] = (mha * gates) * own(7)
    b_query[...] = own(9)
    b_value[...] = own(10)
    grad_hidden = (
        vector(pack.gain_two) * own(0)
        + vector(pack.shift_two) * own(1)
        + ffn * own(2)
        + vector(pack.gain_one) * own(4)
        + vector(pack.shift_one) * own(5)
        + mha * own(6)
    )
    hidden_gate[...] = grad_hidden
    all_gates = hidden_gates(core, pack, pack_own, pack_peer)
    grad_ffn_gate = row_sum(all_gates * sums[2:3, :])
    grad_mha_gate = row_sum(all_gates * sums[6:7, :])
    ffn_gate[...] = grad_ffn_gate
    mha_gate[...] = grad_mha_gate

    unit_rows = units // (2 * width)

    def unit_line(first):
        at = first + core * unit_rows
        return jnp.concatenate([sums[pl.ds(at + k, 1), :] for k in range(unit_rows)], axis=1)

    grad_unit = unit_line(11)
    b_up[...] = unit_line(11 + 2 * unit_rows)
    unit_gate[...] = grad_unit
    by_head = own(8)
    lane = lax.broadcasted_iota(jnp.int32, (1, LANES), 1)
    grad_head = jnp.zeros((1, LANES), f32)
    for at in range(heads):
        grad_head = jnp.where(
            lane == at, row_sum(by_head[:, at * HD : (at + 1) * HD]), grad_head
        )
    head_gate[...] = grad_head[:, :heads]

    numbers = vector(pack.scalars)
    mha_open, ffn_open = open_share(numbers[:, 0:1]), open_share(numbers[:, 2:3])
    first_weight, second_weight = numbers[:, 4:5], numbers[:, 5:6]

    def open_total(spot, count):
        return row_sum(open_share(take(pack_own, spot)[:, :count])) + row_sum(
            open_share(take(pack_peer, spot)[:, :count])
        )

    head_sum = open_total(pack.head_alpha, heads)
    unit_sum = open_total(pack.unit_alpha, units)
    hidden_sum = open_total(pack.hidden_alpha, width)
    model, inner = 2.0 * width, 2.0 * units
    scale = 1.0 / ((4.0 * model + 2.0 * inner) * model)
    kept = 4.0 * HD * mha_open * head_sum + 2.0 * ffn_open * unit_sum
    share = kept * hidden_sum * scale
    gap = share - target_share
    share_out[...] = share
    penalty_out[...] = first_weight * gap + second_weight * gap * gap
    slope = (first_weight + 2.0 * second_weight * gap) * scale
    by_heads = slope * hidden_sum * (4.0 * HD)
    by_units = slope * hidden_sum * 2.0

    def alpha_grad(noise, alpha, grad_gate, grad_open):
        opened = open_share(alpha)
        return gate_slope(noise, alpha) * grad_gate + grad_open * (opened * (1.0 - opened))

    head_alpha[...] = alpha_grad(
        vector(pack.head_noise), vector(pack.head_alpha), grad_head, by_heads * mha_open
    )[:, :heads]
    unit_alpha[...] = alpha_grad(
        vector(pack.unit_noise), vector(pack.unit_alpha), grad_unit, by_units * ffn_open
    )
    hidden_alpha[...] = alpha_grad(
        vector(pack.hidden_noise), vector(pack.hidden_alpha), grad_hidden, slope * kept
    )
    mha_alpha[...] = alpha_grad(
        numbers[:, 1:2], numbers[:, 0:1], grad_mha_gate, by_heads * head_sum
    )
    ffn_alpha[...] = alpha_grad(
        numbers[:, 3:4], numbers[:, 2:3], grad_ffn_gate, by_units * unit_sum
    )


def full(shape):
    return pl.BlockSpec(shape, lambda *at: (0,) * len(shape))


def one_number():
    return pl.BlockSpec(memory_space=pltpu.SMEM)


def shaped(shape, dtype):
    return jax.ShapeDtypeStruct(shape, dtype)


def call(kernel, grid, in_specs, out_specs, out_shape, scratch, cost, args):
    return pl.pallas_call(
        kernel,
        grid=grid,
        in_specs=in_specs,
        out_specs=out_specs,
        out_shape=out_shape,
        scratch_shapes=scratch,
        compiler_params=pltpu.CompilerParams(vmem_limit_bytes=vmem_bytes),
        cost_estimate=pl.CostEstimate(
            flops=int(cost[0] * 1e9), bytes_accessed=int(cost[1] * 1e6), transcendentals=int(cost[2] * 1e6)
        ),
    )(*args)


def call_by_half(kernel, grid, in_specs, out_specs, out_shape, cost, half, args):
    return pl.pallas_call(
        kernel,
        grid_spec=pltpu.PrefetchScalarGridSpec(
            num_scalar_prefetch=1, grid=grid, in_specs=in_specs, out_specs=out_specs
        ),
        out_shape=out_shape,
        compiler_params=pltpu.CompilerParams(vmem_limit_bytes=vmem_bytes),
        cost_estimate=pl.CostEstimate(
            flops=int(cost[0] * 1e9), bytes_accessed=int(cost[1] * 1e6), transcendentals=0
        ),
    )(half, *args)


def swap_pairs(core_masks):
    rows, cores = lax.axis_size("rows"), lax.axis_size("hid")
    return [
        (row * cores + core, (row ^ core_masks[core]) * cores + core)
        for row in range(rows)
        for core in range(cores)
    ]


def swap(values_in, core_masks):
    return lax.ppermute(values_in, ("rows", "hid"), swap_pairs(core_masks))


def near(values_in):
    return lax.ppermute(values_in, "hid", [(0, 1), (1, 0)])


def spread_masks():
    rest = lax.axis_size("rows") // 4
    masks = [4 * (2**k * 2 - 1) for k in range(rest.bit_length() - 1)]
    return [(masks[k], masks[len(masks) - 1 - k]) for k in range(len(masks))]


def add_low(first, second):
    return to_low(first.astype(f32) + second.astype(f32))


def pick(values_in, at):
    return lax.dynamic_index_in_dim(values_in, at, 0, keepdims=False)


def reduce_rows(make_half, first_bit, second_bit):
    sent = swap(make_half(1 - first_bit), (1, 2))
    kept = make_half(first_bit)
    to_send = add_low(pick(kept, 1 - second_bit), pick(sent, 1 - second_bit))
    to_keep = add_low(pick(kept, second_bit), pick(sent, second_bit))
    own = add_low(to_keep, swap(to_send, (2, 1)))
    for core_masks in spread_masks():
        own = add_low(own, swap(own, core_masks))
    beside = swap(own, (2, 1))
    half = jnp.where(second_bit == 0, jnp.stack((own, beside)), jnp.stack((beside, own)))
    return half, swap(half, (1, 2))


def sum_small(values_in):
    values_in = values_in + near(values_in)
    for core_masks in [(1, 2), (2, 1)] + spread_masks():
        values_in = values_in + swap(values_in, core_masks)
    return values_in


def body(
    hidden_in,
    teacher,
    segment_ids,
    valid_mask,
    w_query,
    b_query,
    w_key,
    w_value,
    b_value,
    w_attn_out,
    b_attn_out,
    gain_one,
    shift_one,
    w_up,
    b_up,
    w_down,
    b_down,
    gain_two,
    shift_two,
    head_alpha,
    mha_alpha,
    unit_alpha,
    ffn_alpha,
    hidden_alpha,
    head_noise,
    mha_noise,
    unit_noise,
    ffn_noise,
    hidden_noise,
    lagrange,
):
    model, width = w_query.shape
    units = w_up.shape[1]
    heads = width // HD
    pairs = model // LANES
    tokens = hidden_in.shape[0] // 2
    pack = Pack(width, units)
    core = lax.axis_index("hid")
    row = lax.axis_index("rows")
    core_at = jnp.reshape(core, (1,)).astype(jnp.int32)
    low_bit, high_bit = row & 1, (row >> 1) & 1
    first_bit = jnp.where(core == 0, low_bit, high_bit).astype(jnp.int32)
    second_bit = jnp.where(core == 0, high_bit, low_bit).astype(jnp.int32)

    def filled(values_in, fill):
        return jnp.pad(values_in, (0, LANES - values_in.shape[0]), constant_values=fill)

    scalars = jnp.concatenate((mha_alpha, mha_noise, ffn_alpha, ffn_noise, lagrange))
    pack_own = jnp.concatenate(
        (
            b_query,
            b_value,
            b_attn_out,
            gain_one,
            shift_one,
            b_down,
            gain_two,
            shift_two,
            hidden_alpha,
            hidden_noise,
            b_up,
            unit_alpha,
            unit_noise,
            filled(head_alpha, 0.0),
            filled(head_noise, 0.5),
            filled(scalars, 0.5),
        )
    ).reshape(1, -1)
    x_peer = near(hidden_in)
    pack_peer = near(pack_own)
    wq_peer, wk_peer, wv_peer = near(w_query), near(w_key), near(w_value)
    wa_peer = near(w_attn_out)
    up_peer, down_peer = near(w_up), near(w_down)
    teacher_peer = near(teacher)
    segments = segment_ids.reshape(-1, LANES)
    valid = valid_mask.reshape(-1, LANES)
    packs = [full((1, pack.total))] * 2
    token_low = shaped((tokens, model), bf16)
    token_wide = shaped((tokens, model), f32)
    token_half = shaped((tokens, width), bf16)

    (
        weights,
        query,
        key,
        value,
        context,
        gated_own,
        gated_peer,
        stats,
        biased,
        normed,
        hidden,
    ) = call(
        partial(attend_kernel, pack),
        (pairs,),
        [one_number()]
        + [full(hidden_in.shape)] * 2
        + [full((model, width))] * 6
        + [full((width, model))] * 2
        + packs
        + [full(segments.shape)] * 2,
        [pl.BlockSpec((2, BLOCK, BLOCK), lambda i: (i, 0, 0))]
        + [full((tokens, model))] * 4
        + [full((tokens, width))] * 2
        + [full((tokens, LANES))]
        + [full((tokens, model))] * 3,
        [
            shaped((2 * pairs, BLOCK, BLOCK), bf16),
            token_low,
            token_low,
            token_low,
            token_low,
            token_half,
            token_half,
            shaped((tokens, LANES), f32),
            token_wide,
            token_wide,
            token_low,
        ],
        [
            pltpu.VMEM((tokens, model), bf16),
            pltpu.VMEM((BLOCK, BLOCK), f32),
            pltpu.VMEM((1, model), f32),
            pltpu.VMEM((tokens, model), bf16),
        ],
        (4.0, 20, 3),
        (
            core_at,
            hidden_in,
            x_peer,
            w_query,
            w_key,
            w_value,
            wq_peer,
            wk_peer,
            wv_peer,
            w_attn_out,
            wa_peer,
            pack_own,
            pack_peer,
            segments,
            valid,
        ),
    )
    hidden_near = near(hidden)
    gated_near = near(gated_peer)

    tiles = units // TILE

    def early(shape, dim):
        return pl.BlockSpec(
            shape, lambda i: tuple(jnp.minimum(i, tiles - 1) if d == dim else 0 for d in range(2))
        )

    def late(shape, dim):
        return pl.BlockSpec(
            shape, lambda i: tuple(jnp.maximum(i - tiles, 0) if d == dim else 0 for d in range(2))
        )

    def every(shape, dim):
        return pl.BlockSpec(shape, lambda i: tuple(i if d == dim else 0 for d in range(2)))

    (
        mixed_own,
        mixed_peer,
        active,
        slope,
        output_own,
        output_peer,
        grad_resid_two,
        grad_ffn,
        sums_two,
    ) = call(
        partial(ffn_forward_kernel, pack),
        (2 * tiles,),
        [one_number(), full((tokens, model)), full((tokens, model))]
        + [early((model, TILE), 1), late((model, TILE), 1)]
        + [early((TILE, model), 0), late((TILE, model), 0)]
        + packs
        + [full(teacher.shape)] * 2
        + [full(valid.shape)],
        [early((tokens, TILE), 1), late((tokens, TILE), 1)]
        + [every((tokens, TILE), 1)] * 2
        + [full((tokens, width))] * 2
        + [full((tokens, model))] * 2
        + [full((4, model))],
        [
            shaped((tokens, units), bf16),
            shaped((tokens, units), bf16),
            shaped((tokens, 2 * units), bf16),
            shaped((tokens, 2 * units), bf16),
            token_half,
            token_half,
            token_wide,
            token_low,
            shaped((4, model), f32),
        ],
        [pltpu.VMEM((tokens, model), f32)],
        (5.0, 25, 3),
        (
            core_at,
            hidden,
            normed,
            w_up,
            up_peer,
            w_down,
            down_peer,
            pack_own,
            pack_peer,
            teacher,
            teacher_peer,
            valid,
        ),
    )
    mixed_near = near(mixed_peer)
    grad_ffn_near = near(grad_ffn)
    output_near = near(output_peer)

    grad_pre_own, grad_pre_peer, grad_resid_one, grad_attn, sums_one, unit_sums = call(
        partial(ffn_backward_kernel, pack),
        (2 * tiles,),
        [one_number()]
        + [full((tokens, model))] * 4
        + [full((tokens, LANES))]
        + [every((tokens, TILE), 1)] * 2
        + [early((model, TILE), 1), late((model, TILE), 1)]
        + [early((TILE, model), 0), late((TILE, model), 0)]
        + packs,
        [early((tokens, TILE), 1), late((tokens, TILE), 1)]
        + [full((tokens, model))] * 2
        + [full((4, model)), full((2, 2 * units))],
        [
            shaped((tokens, units), bf16),
            shaped((tokens, units), bf16),
            token_wide,
            token_low,
            shaped((4, model), f32),
            shaped((2, 2 * units), f32),
        ],
        [pltpu.VMEM((tokens, model), f32)],
        (5.0, 25, 0),
        (
            core_at,
            grad_ffn,
            grad_resid_two,
            normed,
            biased,
            stats,
            active,
            slope,
            w_up,
            up_peer,
            w_down,
            down_peer,
            pack_own,
            pack_peer,
        ),
    )
    grad_pre_near = near(grad_pre_peer)
    grad_attn_near = near(grad_attn)

    half_units = units // 2
    step_units = half_units // 3

    def down_half(half):
        blocks = half_units // step_units
        by_units = pl.BlockSpec((tokens, step_units), lambda i, t: (0, t[0] * blocks + i))
        whole = pl.BlockSpec((tokens, model), lambda i, t: (0, 0))
        out = call_by_half(
            down_grad_kernel,
            (blocks,),
            [by_units, by_units, whole, whole],
            pl.BlockSpec((step_units, model), lambda i, t: (i, 0)),
            shaped((half_units, model), bf16),
            (1.2, 4.5),
            jnp.reshape(half, (1,)),
            (mixed_own, mixed_near, grad_ffn, grad_ffn_near),
        )
        return out.reshape(2, half_units // 2, model)

    def up_half(half):
        by_features = pl.BlockSpec((tokens, width), lambda i, t: (0, t[0]))
        by_units = pl.BlockSpec((tokens, TILE), lambda i, t: (0, i))
        out = call_by_half(
            up_grad_kernel,
            (tiles,),
            [by_features, by_features, by_units, by_units],
            pl.BlockSpec((width, TILE), lambda i, t: (0, i)),
            shaped((width, units), bf16),
            (1.2, 5.1),
            jnp.reshape(half, (1,)),
            (hidden, hidden_near, grad_pre_own, grad_pre_near),
        )
        return out.reshape(2, width // 2, units)

    down_sums = reduce_rows(down_half, first_bit, second_bit)
    up_sums = reduce_rows(up_half, first_bit, second_bit)

    own_pairs = pairs // 2
    grad_own, grad_peer, sums_attn = call(
        partial(attend_back_kernel, pack),
        (pairs,),
        [one_number(), pl.BlockSpec((2, BLOCK, BLOCK), lambda i: (i, 0, 0))]
        + [full((tokens, model))] * 4
        + [full((tokens, LANES)), full((tokens, model))]
        + [
            pl.BlockSpec((LANES, model), lambda i: (jnp.minimum(i, own_pairs - 1), 0)),
            pl.BlockSpec((LANES, model), lambda i: (jnp.maximum(i - own_pairs, 0), 0)),
        ]
        + packs,
        [full((tokens, 3 * width))] * 2 + [full((3, model))],
        [
            shaped((tokens, 3 * width), bf16),
            shaped((tokens, 3 * width), bf16),
            shaped((3, model), f32),
        ],
        [pltpu.VMEM((1, model), f32)],
        (4.0, 20, 0),
        (
            core_at,
            weights,
            query,
            key,
            value,
            context,
            stats,
            grad_attn,
            w_attn_out,
            wa_peer,
            pack_own,
            pack_peer,
        ),
    )
    grad_near = near(grad_peer)

    def attend_half(half):
        return call(
            partial(attend_grad_kernel, width),
            (),
            [one_number()] * 2
            + [full(hidden_in.shape)] * 2
            + [full((tokens, 3 * width))] * 2
            + [full((tokens, width))] * 2
            + [full((tokens, model))] * 2,
            full((2, model, width)),
            shaped((2, model, width), bf16),
            [],
            (1.2, 8, 0),
            (
                jnp.reshape(half, (1,)),
                core_at,
                hidden_in,
                x_peer,
                grad_own,
                grad_near,
                gated_own,
                gated_near,
                grad_attn,
                grad_attn_near,
            ),
        )

    attend_sums = reduce_rows(attend_half, first_bit, second_bit)

    input_own, input_peer = call(
        partial(input_grad_kernel, width),
        (),
        [one_number(), full((tokens, model))]
        + [full((tokens, 3 * width))] * 2
        + [full((model, width))] * 6,
        [full((tokens, width))] * 2,
        [shaped((tokens, width), f32)] * 2,
        [],
        (1.8, 8, 0),
        (
            core_at,
            grad_resid_one,
            grad_own,
            grad_peer,
            w_query,
            w_key,
            w_value,
            wq_peer,
            wk_peer,
            wv_peer,
        ),
    )
    input_near = near(input_peer)

    def by_token(own, other):
        return jnp.where(
            core == 0, jnp.concatenate((own, other), axis=0), jnp.concatenate((other, own), axis=0)
        )

    output = by_token(output_own, output_near)
    grad_input = by_token(input_own, input_near)

    small = sum_small(
        jnp.concatenate((sums_two, sums_one, sums_attn, unit_sums.reshape(-1, model)), axis=0)
    )
    sizes = (width,) * 5 + (units,) + (width,) * 3 + (heads, 1, units, 1, width)
    sizes = sizes + (heads, 1, units, 1, width, 1, 1)
    finished = call(
        partial(finish_kernel, pack),
        (),
        [one_number(), full(small.shape)] + packs,
        [full((1, size)) for size in sizes],
        [shaped((1, size), f32) for size in sizes],
        [],
        (0.01, 0.3, 0.1),
        (core_at, small, pack_own, pack_peer),
    )
    done = [item.reshape(-1) for item in finished]

    bit_at = jnp.reshape(first_bit, (1,))

    def place(pieces):
        _, height, across = pieces[0].shape

        def block(at):
            return pl.BlockSpec((1, height, across), at)

        out = call_by_half(
            place_kernel,
            (4,),
            [
                block(lambda i, t: (jnp.minimum(i, 1), 0, 0)),
                block(lambda i, t: (jnp.maximum(i - 2, 0), 0, 0)),
            ],
            block(lambda i, t: (2 * lax.rem(t[0] + i // 2, 2) + lax.rem(i, 2), 0, 0)),
            shaped((4, height, across), f32),
            (0.001, 7),
            bit_at,
            pieces,
        )
        return out.reshape(4 * height, across)

    sum_down = place(down_sums)
    sum_up = place(up_sums)
    sum_query, sum_key, sum_value, sum_attn = call(
        place_attend_kernel,
        (),
        [one_number()] + [full((2, model, width))] * 2,
        [full((model, width))] * 3 + [full((width, model))],
        [shaped((model, width), f32)] * 3 + [shaped((width, model), f32)],
        [],
        (0.001, 7, 0),
        (bit_at, *attend_sums),
    )
    return (
        output,
        grad_input,
        sum_query,
        done[0],
        sum_key,
        sum_value,
        done[1],
        sum_attn,
        done[2],
        done[3],
        done[4],
        sum_up,
        done[5],
        sum_down,
        *done[6:],
    )


def solution(mesh):
    in_specs = (
        P("rows", "hid"),
        P("rows", "hid"),
        P("rows"),
        P("rows"),
        P(None, "hid"),
        P("hid"),
        P(None, "hid"),
        P(None, "hid"),
        P("hid"),
        P("hid", None),
        P("hid"),
        P("hid"),
        P("hid"),
        P(None, "hid"),
        P("hid"),
        P("hid", None),
        P("hid"),
        P("hid"),
        P("hid"),
        P("hid"),
        P(),
        P("hid"),
        P(),
        P("hid"),
        P("hid"),
        P(),
        P("hid"),
        P(),
        P("hid"),
        P(),
    )
    out_specs = (
        P("rows", "hid"),
        P("rows", "hid"),
        P(None, "hid"),
        P("hid"),
        P(None, "hid"),
        P(None, "hid"),
        P("hid"),
        P("hid", None),
        P("hid"),
        P("hid"),
        P("hid"),
        P(None, "hid"),
        P("hid"),
        P("hid", None),
        P("hid"),
        P("hid"),
        P("hid"),
        P("hid"),
        P(),
        P("hid"),
        P(),
        P("hid"),
        P("hid"),
        P(),
        P("hid"),
        P(),
        P("hid"),
        P(),
        P(),
    )
    return jax.shard_map(body, mesh=mesh, in_specs=in_specs, out_specs=out_specs, check_vma=False)
```

time: 803 us -> 355 us (0.44)
  waiting for transfers between devices: 379 us -> 126 us
  matrix products: 159 us -> 0 us
  Pallas kernels: 0 us -> 122 us
  blocking collectives: 95.2 us -> 0 us
  local copies, waits for them, and re-layouts: 91.2 us -> 17.3 us
  starting transfers between devices: 0.99 us -> 42.8 us
  between operations: 29.7 us -> 4.12 us
    psum x1 -> x0, waiting for transfers between devices: 303 us -> none  [body(): lax.psum((grad_w_up, grad_w_down, grad_b_up, grad_b_down, grad_gain_two,...]
    dot_general x32 -> x0, matrix products: 159 us -> none  [the longest x12 40.8 us: contract(): lax.dot_general(first, second, (((first_dim,), (second_dim,)), ((), ())),...]
    ppermute x0 -> x41, waiting for transfers between devices: none -> 126 us  [the longest x22 117 us: swap(): return lax.ppermute(values_in, ('rows', 'hid'), swap_pairs(core_masks))]
    pallas_call x0 -> x15, Pallas kernels: none -> 122 us  [the longest x9 94 us: call(): pl.pallas_call(kernel, grid=grid, in_specs=in_specs, out_specs=out_specs,...]
    psum x6 -> x0, blocking collectives: 95.2 us -> none  [the longest x1 82.1 us: body(): lax.psum((grad_w_up, grad_w_down, grad_b_up, grad_b_down, grad_gain_two,...]
    ppermute x0 -> x41, starting transfers between devices: none -> 42.8 us  [the longest x22 38.2 us: swap(): return lax.ppermute(values_in, ('rows', 'hid'), swap_pairs(core_masks))]
    all_gather x4 -> x0, waiting for transfers between devices: 42.7 us -> none  [the longest x1 11 us: body(): lax.all_gather(to_low(grad_attn), 'hid', axis=1, tiled=True)]
    reduce_scatter x3 -> x0, waiting for transfers between devices: 32.1 us -> none  [the longest x1 12.2 us: body(): lax.psum_scatter(contract(grad_pre, w_up, 1, 1), 'hid', scatter_dimension...]
  transfers between devices with their start and end apart: 9 -> 41, of which waited for: 8 -> 20; matrix products, arithmetic and copies ran while one was open for 4% -> 14% of each run, Pallas kernels for 0% -> 24%
where the time goes in v1:
time: 355 us; the launch traced here: 348 us
  waiting for transfers between devices  126 us (35%)
  Pallas kernels  122 us (34%)
  starting transfers between devices  42.8 us (12%)
  other arithmetic  36 us (10%)
  local copies, waits for them, and re-layouts  17.3 us (5%)
  between operations  4.12 us (1%)
    ppermute x22, waiting for transfers between devices, swap(): return lax.ppermute(values_in, ('rows', 'hid'), swap_pairs(core_masks))  117 us
    pallas_call x9, Pallas kernels, call(): pl.pallas_call(kernel, grid=grid, in_specs=in_specs, out_specs=out_specs,...  94 us
    ppermute x22, starting transfers between devices, swap(): return lax.ppermute(values_in, ('rows', 'hid'), swap_pairs(core_masks))  38.2 us
    pallas_call x6, Pallas kernels, call_by_half(): pl.pallas_call(kernel, grid_spec=pltpu.PrefetchScalarGridSpec(num_scalar_...  28.4 us
    pallas_call x13, other arithmetic, call(): pl.pallas_call(kernel, grid=grid, in_specs=in_specs, out_specs=out_specs,...  16.6 us
    unnamed x73, local copies, waits for them, and re-layouts  16.5 us
    ppermute x19, waiting for transfers between devices, near(): return lax.ppermute(values_in, 'hid', [(0, 1), (1, 0)])  9.16 us
    convert_element_type x12, other arithmetic, to_low(): return values_in.astype(bf16)  9.04 us
  transfers between devices with their start and end apart: 41, of which 20 were waited for; matrix products, arithmetic and copies ran while one was open for 14% of the time, Pallas kernels for 24%

profile of v1, /device:TPU:0, one launch (start us, length us, event | category | flops | bytes accessed | tf_op | source)
XLA Modules:
  0.0 348.4 jit_solution(12650751261941980572)
XLA Ops:
  17.7 1.5 collective-permute-done.3.wv_peer
  19.5 1.3 collective-permute-done.4.wa_peer
  22.2 17.9 %shard_map.509 = (bf16[12,512,512]{2,1,0:T(8,128)(2,1)}, bf16[512,768]{1,0:T(8,128)(2,1)}, bf16[512,768]{1,0:T(8,128)(2,1)}, bf16[512,768]{1,0:T(8,128)(2,1)}, b...) custom-call(s32[1]{0:T(128)} %bitcast.core_ref, ...), custom_call_target="tpu_custom_call" | custom-call | flops 4000000000 | bytes 20000000 | tf_op jit(solution)/shard_map/pallas_call | solution.py:782
  40.1 1.4 copy-done.14
  41.5 19.8 %shard_map.510 = (bf16[512,1536]{1,0:T(8,128)(2,1)}, bf16[512,1536]{1,0:T(8,128)(2,1)}, bf16[512,3072]{1,0:T(8,128)(2,1)}, bf16[512,3072]{1,0:T(8,128)(2,1)}, bf...) custom-call(s32[1]{0:T(128)} %bitcast.core_ref, ...), custom_call_target="tpu_custom_call" | custom-call | flops 5000000000 | bytes 25000000 | tf_op jit(solution)/shard_map/pallas_call | solution.py:782
  61.3 15.9 %shard_map.511 = (bf16[512,1536]{1,0:T(8,128)(2,1)}, bf16[512,1536]{1,0:T(8,128)(2,1)}, f32[512,768]{1,0:T(8,128)}, bf16[512,768]{1,0:T(8,128)(2,1)}, f32[4,768]{1,0:T(4,128)}, /*index=5*/f32[2,3072]{1,0:T(2,128)}) custom-call(s32[1]{0:T(128)} %bitcast.core_ref, bf16[512,768]{1,0:T(8,128)(2,1)} %get-tuple-element.89.grad_ffn.grad, ...), custom_call_target="tpu_custom_call" | custom-call | flops 5000000000 | bytes 25000000 | tf_op jit(solution)/shard_map/pallas_call | solution.py:782
  77.7 16.4 %shard_map.512 = (bf16[512,1152]{1,0:T(8,128)(2,1)}, bf16[512,1152]{1,0:T(8,128)(2,1)}, f32[3,768]{1,0:T(4,128)}) custom-call(s32[1]{0:T(128)} %bitcast.core_ref, bf16[12,512,512]{2,1,0:T(8,128)(2,1)} %get-tuple-element.96.weights, bf16[512,768]{1,0:T(8,128)(2,1)} %get-tuple-element.97.query_ref, bf16[512,768]{1,0:T(8,128)(2,1)} %get-tuple-element.98.key_ref, ...), custom_call_target="tpu_custom_call" | custom-call | flops 4000000000 | bytes 20000000 | tf_op jit(solution)/shard_map/pallas_call | solution.py:782
  95.1 2.9 collective-permute-done.12.gated_near
  98.2 2.1 collective-permute-done.13.grad_attn_near
  102.4 5.5 %shard_map.515 = bf16[2,768,384]{2,1,0:T(8,128)(2,1)} custom-call(s32[1]{0:T(128)} %bitcast.4.half_ref, s32[1]{0:T(128)} %bitcast.core_ref, bf16[1024,384]{1,0:T(8,128)(2,1)} %x_own.5, bf16[1024,384]{1,0:T(8,128)(2,1)} %copy-done.9, bf16[512,1152]{1,0:T(8,128)(2,1)} %get-tuple-element.102.grad_own.grad, bf16[512,1152]{1,0:T(8,128)(2,1)} %copy-done.8, ...), custom_call_target="tpu_custom_call" | custom-call | flops 1200000000 | bytes 8000000 | tf_op jit(solution)/shard_map/pallas_call | solution.py:782
  107.8 2.5 collective-permute-start.14
  111.4 4.8 %shard_map.519 = bf16[384,1536]{1,0:T(8,128)(2,1)} custom-call(s32[1]{0:T(128)} %bitcast.4.half_ref, bf16[512,768]{1,0:T(8,128)(2,1)} %get-tuple-element.85.hidden, bf16[512,768]{1,0:T(8,128)(2,1)} %collective-permute-done.25.hidden_near, bf16[512,1536]{1,0:T(8,128)(2,1)} %get-tuple-element.121.grad, bf16[512,1536]{1,0:T(8,128)(2,1)} %copy-done.1), custom_call_target="tpu_custom_call" | custom-call | flops 1200000000 | bytes 5100000 | tf_op jit(solution)/shard_map/pallas_call | solution.py:797
  116.2 4.7 %shard_map.522 = bf16[768,768]{1,0:T(8,128)(2,1)} custom-call(s32[1]{0:T(128)} %bitcast.4.half_ref, bf16[512,1536]{1,0:T(8,128)(2,1)} %get-tuple-element.124.mixed, bf16[512,1536]{1,0:T(8,128)(2,1)} %collective-permute-done.33.mixed_near, bf16[512,768]{1,0:T(8,128)(2,1)} %get-tuple-element.89.grad_ffn.grad, bf16[512,768]{1,0:T(8,128)(2,1)} %collective-permute-done.34.grad_near), custom_call_target="tpu_custom_call" | custom-call | flops 1200000000 | bytes 4500000 | tf_op jit(solution)/shard_map/pallas_call | solution.py:797
  121.0 2.0 collective-permute-start.35
  123.0 5.5 %shard_map.514 = bf16[2,768,384]{2,1,0:T(8,128)(2,1)} custom-call(s32[1]{0:T(128)} %bitcast.3.half_ref.bit_ref, s32[1]{0:T(128)} %bitcast.core_ref, bf16[1024,384]{1,0:T(8,128)(2,1)} %x_own.5, bf16[1024,384]{1,0:T(8,128)(2,1)} %copy-done.9, bf16[512,1152]{1,0:T(8,128)(2,1)} %get-tuple-element.102.grad_own.grad, bf16[512,1152]{1,0:T(8,128)(2,1)} %copy-done.8, ...), custom_call_target="tpu_custom_call" | custom-call | flops 1200000000 | bytes 8000000 | tf_op jit(solution)/shard_map/pallas_call | solution.py:782
  128.4 2.0 fusion.4
  130.5 1.6 collective-permute-start.15
  132.1 4.8 %shard_map.518 = bf16[384,1536]{1,0:T(8,128)(2,1)} custom-call(s32[1]{0:T(128)} %bitcast.3.half_ref.bit_ref, bf16[512,768]{1,0:T(8,128)(2,1)} %get-tuple-element.85.hidden, bf16[512,768]{1,0:T(8,128)(2,1)} %collective-permute-done.25.hidden_near, bf16[512,1536]{1,0:T(8,128)(2,1)} %get-tuple-element.121.grad, bf16[512,1536]{1,0:T(8,128)(2,1)} %copy-done.1), custom_call_target="tpu_custom_call" | custom-call | flops 1200000000 | bytes 5100000 | tf_op jit(solution)/shard_map/pallas_call | solution.py:797
  136.8 5.2 %collective-permute-done.27 = bf16[2,192,1536]{2,1,0:T(8,128)(2,1)S(1)} collective-permute-done((bf16[2,192,1536]{2,1,0:T(8,128)(2,1)}, bf16[2,192,1536]{2,1,0:T(8,128)(2,1)S(1)}, u32[]{:S(2)}, u32[]{:S(2)}) %collective-permute-start.27) | collective-permute-done | bytes 1179680 | tf_op jit(solution)/shard_map/ppermute | solution.py:820
  142.0 2.0 fusion.6
  144.0 3.7 %collective-permute-start.28 = (bf16[192,1536]{1,0:T(8,128)(2,1)}, bf16[192,1536]{1,0:T(8,128)(2,1)}, u32[]{:S(2)}, u32[]{:S(2)}) collective-permute-start(bf16[192,1536]{1,0:T(8,128)(2,1)} %fusion.6), channel_id=1, source_target_pairs={{0,4},{1,3},{2,6},{3,1},{4,0},{5,7},{6,2},{7,5},{8,12},{9,11},{10,... | collective-permute-start | bytes 1769480 | tf_op jit(solution)/shard_map/ppermute | solution.py:820
  147.7 4.7 %shard_map.521 = bf16[768,768]{1,0:T(8,128)(2,1)} custom-call(s32[1]{0:T(128)} %bitcast.3.half_ref.bit_ref, bf16[512,1536]{1,0:T(8,128)(2,1)} %get-tuple-element.124.mixed, bf16[512,1536]{1,0:T(8,128)(2,1)} %collective-permute-done.33.mixed_near, bf16[512,768]{1,0:T(8,128)(2,1)} %get-tuple-element.89.grad_ffn.grad, ...), custom_call_target="tpu_custom_call" | custom-call | flops 1200000000 | bytes 4500000 | tf_op jit(solution)/shard_map/pallas_call | solution.py:797
  152.4 10.3 %collective-permute-done.35 = bf16[2,384,768]{2,1,0:T(8,128)(2,1)} collective-permute-done((bf16[2,384,768]{2,1,0:T(8,128)(2,1)}, bf16[2,384,768]{2,1,0:T(8,128)(2,1)}, u32[]{:S(2)}, u32[]{:S(2)}) %collective-permute-start.35) | collective-permute-done | bytes 1179680 | tf_op jit(solution)/shard_map/ppermute | solution.py:820
  162.7 1.4 fusion.8
  164.1 2.3 collective-permute-start.36
  166.7 1.7 collective-permute-start.16
  168.4 1.3 fusion.1
  170.1 4.2 %collective-permute-done.36 = bf16[384,768]{1,0:T(8,128)(2,1)S(1)} collective-permute-done((bf16[384,768]{1,0:T(8,128)(2,1)S(1)}, bf16[384,768]{1,0:T(8,128)(2,1)S(1)}, u32[]{:S(2)}, u32[]{:S(2)}) %collective-permute-start.36) | collective-permute-done | bytes 589856 | tf_op jit(solution)/shard_map/ppermute | solution.py:820
  174.3 1.3 fusion
  175.6 2.2 collective-permute-start.37
  177.8 7.2 %collective-permute-done.16 = bf16[768,384]{1,0:T(8,128)(2,1)S(1)} collective-permute-done((bf16[768,384]{1,0:T(8,128)(2,1)S(1)}, bf16[768,384]{1,0:T(8,128)(2,1)S(1)}, u32[]{:S(2)}, u32[]{:S(2)}) %collective-permute-start.16) | collective-permute-done | bytes 589856 | tf_op jit(solution)/shard_map/ppermute | solution.py:820
  185.1 1.7 collective-permute-start.17
  186.8 21.2 %collective-permute-done.29 = bf16[192,1536]{1,0:T(8,128)(2,1)S(1)} collective-permute-done((bf16[192,1536]{1,0:T(8,128)(2,1)S(1)}, bf16[192,1536]{1,0:T(8,128)(2,1)S(1)}, u32[]{:S(2)}, u32[]{:S(2)}) %collective-permute-start.29) | collective-permute-done | bytes 589856 | tf_op jit(solution)/shard_map/ppermute | solution.py:820
  209.5 21.6 %collective-permute-done.37 = bf16[384,768]{1,0:T(8,128)(2,1)S(1)} collective-permute-done((bf16[384,768]{1,0:T(8,128)(2,1)S(1)}, bf16[384,768]{1,0:T(8,128)(2,1)S(1)}, u32[]{:S(2)}, u32[]{:S(2)}) %collective-permute-start.37) | collective-permute-done | bytes 589856 | tf_op jit(solution)/shard_map/ppermute | solution.py:820
  231.2 3.8 %collective-permute-start.38 = (bf16[384,768]{1,0:T(8,128)(2,1)S(1)}, bf16[384,768]{1,0:T(8,128)(2,1)S(1)}, u32[]{:S(2)}, u32[]{:S(2)}) collective-permute-start(bf16[384,768]{1,0:T(8,128)(2,1)S(1)} %add_convert_fusion.1), channel_id=1, source_target_pairs={{0,24},{1,9},{2,26},{3,11},{4,28},{5,13},{6,30},{7,15},{8,16},{9,1... | collective-permute-start | bytes 1769480 | tf_op jit(solution)/shard_map/ppermute | solution.py:820
  235.9 1.6 collective-permute-start.31
  237.5 8.9 %collective-permute-done.38 = bf16[384,768]{1,0:T(8,128)(2,1)S(1)} collective-permute-done((bf16[384,768]{1,0:T(8,128)(2,1)S(1)}, bf16[384,768]{1,0:T(8,128)(2,1)S(1)}, u32[]{:S(2)}, u32[]{:S(2)}) %collective-permute-start.38) | collective-permute-done | bytes 589856 | tf_op jit(solution)/shard_map/ppermute | solution.py:820
  246.5 1.4 collective-permute-start.39
  248.8 1.5 maximum_select_fusion.1.half
  251.5 1.5 maximum_select_fusion.2.half
  253.0 1.4 collective-permute-start.32
  254.4 7.6 %collective-permute-done.39 = bf16[384,768]{1,0:T(8,128)(2,1)} collective-permute-done((bf16[384,768]{1,0:T(8,128)(2,1)S(1)}, bf16[384,768]{1,0:T(8,128)(2,1)}, u32[]{:S(2)}, u32[]{:S(2)}) %collective-permute-start.39) | collective-permute-done | bytes 589856 | tf_op jit(solution)/shard_map/ppermute | solution.py:820
  262.0 1.4 maximum_select_fusion.3.half
  263.4 2.2 collective-permute-start.40
  265.6 7.0 %shard_map.513 = (f32[512,384]{1,0:T(8,128)}, f32[512,384]{1,0:T(8,128)}) custom-call(s32[1]{0:T(128)} %bitcast.core_ref, f32[512,768]{1,0:T(8,128)} %get-tuple-element.95.grad_resid, bf16[512,1152]{1,0:T(8,128)(2,1)} %get-tuple-element.102.grad_own.grad, bf16[512,1152]{1,0:T(8,128)(2,1)} %get-tuple-element.103.grad_peer, bf16[768,384]{1,0:T(8,128)(2,1)} %wq_own.3, ...), custom_call_target="tpu_custom_call" | custom-call | flops 1800000000 | bytes 8000000 | tf_op jit(solution)/shard_map/pallas_call | solution.py:782
  273.1 19.5 %collective-permute-done.21 = f32[19,768]{1,0:T(8,128)S(1)} collective-permute-done((f32[19,768]{1,0:T(8,128)S(1)}, f32[19,768]{1,0:T(8,128)S(1)}, u32[]{:S(2)}, u32[]{:S(2)}) %collective-permute-start.21) | collective-permute-done | bytes 58400 | tf_op jit(solution)/shard_map/ppermute | solution.py:820
  293.5 3.7 %collective-permute-done.22 = f32[19,768]{1,0:T(8,128)S(1)} collective-permute-done((f32[19,768]{1,0:T(8,128)S(1)}, f32[19,768]{1,0:T(8,128)S(1)}, u32[]{:S(2)}, u32[]{:S(2)}) %collective-permute-start.22) | collective-permute-done | bytes 58400 | tf_op jit(solution)/shard_map/ppermute | solution.py:820
  297.9 3.8 %collective-permute-done.23 = f32[19,768]{1,0:T(8,128)S(1)} collective-permute-done((f32[19,768]{1,0:T(8,128)S(1)}, f32[19,768]{1,0:T(8,128)S(1)}, u32[]{:S(2)}, u32[]{:S(2)}) %collective-permute-start.23) | collective-permute-done | bytes 58400 | tf_op jit(solution)/shard_map/ppermute | solution.py:820
  301.7 5.9 %collective-permute-start.24 = (f32[19,768]{1,0:T(8,128)S(1)}, f32[19,768]{1,0:T(8,128)S(1)}, u32[]{:S(2)}, u32[]{:S(2)}) collective-permute-start(f32[19,768]{1,0:T(8,128)S(1)} %add.102), channel_id=1, source_target_pairs={{0,24},{1,9},{2,26},{3,11},{4,28},{5,13},{6,30},{7,15},{8,16},{9,1... | collective-permute-start | bytes 175112 | tf_op jit(solution)/shard_map/ppermute | solution.py:820
  307.6 2.3 collective-permute-done.24
  310.6 2.0 shard_map.517
  312.5 1.3 reduce
  313.8 1.3 reduce.1
  315.1 1.3 reduce.2
  316.4 1.3 reduce.3
  317.6 1.3 reduce.4
  318.9 1.3 reduce.5
  324.0 1.3 reduce.9
  326.6 1.3 reduce.11
  329.2 2.5 maximum_select_fusion.4
  331.7 2.8 maximum_select_fusion
  334.5 4.1 %shard_map.516 = (f32[768,384]{1,0:T(8,128)}, f32[768,384]{1,0:T(8,128)}, f32[768,384]{1,0:T(8,128)}, f32[384,768]{1,0:T(8,128)}) custom-call(s32[1]{0:T(128)} %bitcast.3.half_ref.bit_ref, bf16[2,768,384]{2,1,0:T(8,128)(2,1)} %copy-done.4, bf16[2,768,384]{2,1,0:T(8,128)(2,1)} %collective-permute-done.19.other), custom_call_target="tpu_custom_call" | custom-call | flops 1000000 | bytes 7000000 | tf_op jit(solution)/shard_map/pallas_call | solution.py:782
  338.6 4.7 %shard_map.520 = f32[4,192,1536]{2,1,0:T(8,128)} custom-call(s32[1]{0:T(128)} %bitcast.3.half_ref.bit_ref, bf16[2,192,1536]{2,1,0:T(8,128)(2,1)} %copy-done.2, bf16[2,192,1536]{2,1,0:T(8,128)(2,1)} %collective-permute-done.32.other), custom_call_target="tpu_custom_call" | custom-call | flops 1000000 | bytes 7000000 | tf_op jit(solution)/shard_map/pallas_call | solution.py:797
  343.3 4.7 %shard_map.523 = f32[4,384,768]{2,1,0:T(8,128)} custom-call(s32[1]{0:T(128)} %bitcast.3.half_ref.bit_ref, bf16[2,384,768]{2,1,0:T(8,128)(2,1)} %copy-done.3, bf16[2,384,768]{2,1,0:T(8,128)(2,1)} %collective-permute-done.40.other), custom_call_target="tpu_custom_call" | custom-call | flops 1000000 | bytes 7000000 | tf_op jit(solution)/shard_map/pallas_call | solution.py:797
  (147 shorter events, 35.4 us)
Async XLA Ops:
  0.7 16.5 %collective-permute-start.1 = (bf16[768,384]{1,0:T(8,128)(2,1)}, bf16[768,384]{1,0:T(8,128)(2,1)}, u32[]{:S(2)}, u32[]{:S(2)}) collective-permute-start(bf16[768,384]{1,0:T(8,128)(2,1)} %wq_own.3), channel_id=1, source_target_pairs={{0,1},{1,0},{2,3},{3,2},{4,5},{5,4},{6,7},{7,6},{8,9},{9,8},{10,11... | collective-permute-start | bytes 1769480 | tf_op jit(solution)/shard_map/ppermute | solution.py:824
  1.2 16.2 %collective-permute-start.2 = (bf16[768,384]{1,0:T(8,128)(2,1)}, bf16[768,384]{1,0:T(8,128)(2,1)}, u32[]{:S(2)}, u32[]{:S(2)}) collective-permute-start(bf16[768,384]{1,0:T(8,128)(2,1)} %wk_own.3), channel_id=1, source_target_pairs={{0,1},{1,0},{2,3},{3,2},{4,5},{5,4},{6,7},{7,6},{8,9},{9,8},{10,11... | collective-permute-start | bytes 1769480 | tf_op jit(solution)/shard_map/ppermute | solution.py:824
  1.3 38.8 %collective-permute-start.6 = (bf16[768,1536]{1,0:T(8,128)(2,1)}, bf16[768,1536]{1,0:T(8,128)(2,1)S(1)}, u32[]{:S(2)}, u32[]{:S(2)}) collective-permute-start(bf16[768,1536]{1,0:T(8,128)(2,1)} %up_own.3), channel_id=1, source_target_pairs={{0,1},{1,0},{2,3},{3,2},{4,5},{5,4},{6,7},{7,6},{8,9},{9,8},{10,11... | collective-permute-start | bytes 7077896 | tf_op jit(solution)/shard_map/ppermute | solution.py:824
  1.7 38.4 %collective-permute-start.7 = (bf16[1536,768]{1,0:T(8,128)(2,1)}, bf16[1536,768]{1,0:T(8,128)(2,1)}, u32[]{:S(2)}, u32[]{:S(2)}) collective-permute-start(bf16[1536,768]{1,0:T(8,128)(2,1)} %down_own.3), channel_id=1, source_target_pairs={{0,1},{1,0},{2,3},{3,2},{4,5},{5,4},{6,7},{7,6},{8,9},{9,8},{10,11... | collective-permute-start | bytes 7077896 | tf_op jit(solution)/shard_map/ppermute | solution.py:824
  15.5 5.8 %copy-start.20 = (f32[1,8832]{1,0:T(1,128)}, f32[1,8832]{1,0:T(1,128)S(1)}, u32[]{:S(2)}) copy-start(f32[1,8832]{1,0:T(1,128)S(1)} %reshape.196.pack_own) | copy-start | bytes 105988
  15.5 1.4 collective-permute-start.5
  16.8 4.5 %copy-start.26 = (f32[1,8832]{1,0:T(1,128)}, f32[1,8832]{1,0:T(1,128)S(1)}, u32[]{:S(2)}) copy-start(f32[1,8832]{1,0:T(1,128)S(1)} %collective-permute-done.5.pack_peer) | copy-start | bytes 105988
  16.8 2.3 collective-permute-start.3
  17.2 4.1 %collective-permute-start = (bf16[1024,384]{1,0:T(8,128)(2,1)}, bf16[1024,384]{1,0:T(8,128)(2,1)S(1)}, u32[]{:S(2)}, u32[]{:S(2)}) collective-permute-start(bf16[1024,384]{1,0:T(8,128)(2,1)} %x_own.5), channel_id=1, source_target_pairs={{0,1},{1,0},{2,3},{3,2},{4,5},{5,4},{6,7},{7,6},{8,9},{9,8},{10,11... | collective-permute-start | bytes 2359304 | tf_op jit(solution)/shard_map/ppermute | solution.py:824
  17.4 3.5 %collective-permute-start.4 = (bf16[384,768]{1,0:T(8,128)(2,1)}, bf16[384,768]{1,0:T(8,128)(2,1)}, u32[]{:S(2)}, u32[]{:S(2)}) collective-permute-start(bf16[384,768]{1,0:T(8,128)(2,1)} %wa_own.3), channel_id=1, source_target_pairs={{0,1},{1,0},{2,3},{3,2},{4,5},{5,4},{6,7},{7,6},{8,9},{9,8},{10,11... | collective-permute-start | bytes 1769480 | tf_op jit(solution)/shard_map/ppermute | solution.py:824
  19.2 20.9 %collective-permute-start.8 = (bf16[1024,384]{1,0:T(8,128)(2,1)}, bf16[1024,384]{1,0:T(8,128)(2,1)}, u32[]{:S(2)}, u32[]{:S(2)}) collective-permute-start(bf16[1024,384]{1,0:T(8,128)(2,1)} %teacher_own.1), channel_id=1, source_target_pairs={{0,1},{1,0},{2,3},{3,2},{4,5},{5,4},{6,7},{7,6},{8,9},{9,8},{10,11... | collective-permute-start | bytes 2359304 | tf_op jit(solution)/shard_map/ppermute | solution.py:824
  40.1 1.4 copy-start.14
  77.3 33.0 %collective-permute-start.26 = (bf16[512,1536]{1,0:T(8,128)(2,1)}, bf16[512,1536]{1,0:T(8,128)(2,1)S(1)}, u32[]{:S(2)}, u32[]{:S(2)}) collective-permute-start(bf16[512,1536]{1,0:T(8,128)(2,1)} %get-tuple-element.122), channel_id=1, source_target_pairs={{0,1},{1,0},{2,3},{3,2},{4,5},{5,4},{6,7},{7,6},{8,9},{9,8},{10,11... | collective-permute-start | bytes 4718600 | tf_op jit(solution)/shard_map/ppermute | solution.py:824
  77.7 16.6 %copy-start.28 = (bf16[512,384]{1,0:T(8,128)(2,1)S(1)}, bf16[512,384]{1,0:T(8,128)(2,1)}, u32[]{:S(2)}) copy-start(bf16[512,384]{1,0:T(8,128)(2,1)} %get-tuple-element.107) | copy-start | bytes 1179652
  77.7 16.9 %copy-start.10 = (bf16[512,768]{1,0:T(8,128)(2,1)S(1)}, bf16[512,768]{1,0:T(8,128)(2,1)}, u32[]{:S(2)}) copy-start(bf16[512,768]{1,0:T(8,128)(2,1)} %get-tuple-element.101.grad_attn) | copy-start | bytes 2359300
  77.7 23.5 %copy-start = (bf16[512,768]{1,0:T(8,128)(2,1)S(1)}, bf16[512,768]{1,0:T(8,128)(2,1)}, u32[]{:S(2)}) copy-start(bf16[512,768]{1,0:T(8,128)(2,1)} %get-tuple-element.89.grad_ffn.grad) | copy-start | bytes 2359300
  94.1 7.3 %collective-permute-start.11 = (bf16[512,1152]{1,0:T(8,128)(2,1)}, bf16[512,1152]{1,0:T(8,128)(2,1)S(1)}, u32[]{:S(2)}, u32[]{:S(2)}) collective-permute-start(bf16[512,1152]{1,0:T(8,128)(2,1)} %get-tuple-element.103.grad_peer), channel_id=1, source_target_pairs={{0,1},{1,0},{2,3},{3,2},{4,5},{5,4},{6,7},{7,6},{8,9},{9,8},{10,11... | collective-permute-start | bytes 3538952 | tf_op jit(solution)/shard_map/ppermute | solution.py:824
  94.2 3.8 %collective-permute-start.12 = (bf16[512,384]{1,0:T(8,128)(2,1)S(1)}, bf16[512,384]{1,0:T(8,128)(2,1)S(1)}, u32[]{:S(2)}, u32[]{:S(2)}) collective-permute-start(bf16[512,384]{1,0:T(8,128)(2,1)S(1)} %copy-done.28), channel_id=1, source_target_pairs={{0,1},{1,0},{2,3},{3,2},{4,5},{5,4},{6,7},{7,6},{8,9},{9,8},{10,11... | collective-permute-start | bytes 1179656 | tf_op jit(solution)/shard_map/ppermute | solution.py:824
  94.6 5.7 %collective-permute-start.13 = (bf16[512,768]{1,0:T(8,128)(2,1)S(1)}, bf16[512,768]{1,0:T(8,128)(2,1)S(1)}, u32[]{:S(2)}, u32[]{:S(2)}) collective-permute-start(bf16[512,768]{1,0:T(8,128)(2,1)S(1)} %copy-done.10), channel_id=1, source_target_pairs={{0,1},{1,0},{2,3},{3,2},{4,5},{5,4},{6,7},{7,6},{8,9},{9,8},{10,11... | collective-permute-start | bytes 2359304 | tf_op jit(solution)/shard_map/ppermute | solution.py:824
  94.8 21.5 %collective-permute-start.33 = (bf16[512,1536]{1,0:T(8,128)(2,1)}, bf16[512,1536]{1,0:T(8,128)(2,1)}, u32[]{:S(2)}, u32[]{:S(2)}) collective-permute-start(bf16[512,1536]{1,0:T(8,128)(2,1)} %get-tuple-element.125), channel_id=1, source_target_pairs={{0,1},{1,0},{2,3},{3,2},{4,5},{5,4},{6,7},{7,6},{8,9},{9,8},{10,11... | collective-permute-start | bytes 4718600 | tf_op jit(solution)/shard_map/ppermute | solution.py:824
  98.0 2.3 copy-start.15
  98.0 12.2 %collective-permute-start.25 = (bf16[512,768]{1,0:T(8,128)(2,1)}, bf16[512,768]{1,0:T(8,128)(2,1)}, u32[]{:S(2)}, u32[]{:S(2)}) collective-permute-start(bf16[512,768]{1,0:T(8,128)(2,1)} %get-tuple-element.85.hidden), channel_id=1, source_target_pairs={{0,1},{1,0},{2,3},{3,2},{4,5},{5,4},{6,7},{7,6},{8,9},{9,8},{10,11... | collective-permute-start | bytes 2359304 | tf_op jit(solution)/shard_map/ppermute | solution.py:824
  101.2 15.0 %collective-permute-start.34 = (bf16[512,768]{1,0:T(8,128)(2,1)S(1)}, bf16[512,768]{1,0:T(8,128)(2,1)}, u32[]{:S(2)}, u32[]{:S(2)}) collective-permute-start(bf16[512,768]{1,0:T(8,128)(2,1)S(1)} %copy-done), channel_id=1, source_target_pairs={{0,1},{1,0},{2,3},{3,2},{4,5},{5,4},{6,7},{7,6},{8,9},{9,8},{10,11... | collective-permute-start | bytes 2359304 | tf_op jit(solution)/shard_map/ppermute | solution.py:824
  107.8 20.6 %collective-permute-start.14 = (bf16[2,768,384]{2,1,0:T(8,128)(2,1)}, bf16[2,768,384]{2,1,0:T(8,128)(2,1)S(1)}, u32[]{:S(2)}, u32[]{:S(2)}) collective-permute-start(bf16[2,768,384]{2,1,0:T(8,128)(2,1)} %shard_map.515), channel_id=1, source_target_pairs={{0,2},{1,5},{2,0},{3,7},{4,6},{5,1},{6,4},{7,3},{8,10},{9,13},{10,... | collective-permute-start | bytes 3538952 | tf_op jit(solution)/shard_map/ppermute | solution.py:820
  116.2 25.8 %collective-permute-start.27 = (bf16[2,192,1536]{2,1,0:T(8,128)(2,1)}, bf16[2,192,1536]{2,1,0:T(8,128)(2,1)S(1)}, u32[]{:S(2)}, u32[]{:S(2)}) collective-permute-start(bf16[2,192,1536]{2,1,0:T(8,128)(2,1)} %bitcast.56), channel_id=1, source_target_pairs={{0,2},{1,5},{2,0},{3,7},{4,6},{5,1},{6,4},{7,3},{8,10},{9,13},{10,... | collective-permute-start | bytes 3538952 | tf_op jit(solution)/shard_map/ppermute | solution.py:820
  121.0 41.7 %collective-permute-start.35 = (bf16[2,384,768]{2,1,0:T(8,128)(2,1)}, bf16[2,384,768]{2,1,0:T(8,128)(2,1)}, u32[]{:S(2)}, u32[]{:S(2)}) collective-permute-start(bf16[2,384,768]{2,1,0:T(8,128)(2,1)} %bitcast.55), channel_id=1, source_target_pairs={{0,2},{1,5},{2,0},{3,7},{4,6},{5,1},{6,4},{7,3},{8,10},{9,13},{10,... | collective-permute-start | bytes 3538952 | tf_op jit(solution)/shard_map/ppermute | solution.py:820
  130.5 36.0 %collective-permute-start.15 = (bf16[768,384]{1,0:T(8,128)(2,1)}, bf16[768,384]{1,0:T(8,128)(2,1)S(1)}, u32[]{:S(2)}, u32[]{:S(2)}) collective-permute-start(bf16[768,384]{1,0:T(8,128)(2,1)} %fusion.4), channel_id=1, source_target_pairs={{0,4},{1,3},{2,6},{3,1},{4,0},{5,7},{6,2},{7,5},{8,12},{9,11},{10,... | collective-permute-start | bytes 1769480 | tf_op jit(solution)/shard_map/ppermute | solution.py:820
  144.0 24.4 %collective-permute-start.28 = (bf16[192,1536]{1,0:T(8,128)(2,1)}, bf16[192,1536]{1,0:T(8,128)(2,1)}, u32[]{:S(2)}, u32[]{:S(2)}) collective-permute-start(bf16[192,1536]{1,0:T(8,128)(2,1)} %fusion.6), channel_id=1, source_target_pairs={{0,4},{1,3},{2,6},{3,1},{4,0},{5,7},{6,2},{7,5},{8,12},{9,11},{10,... | collective-permute-start | bytes 1769480 | tf_op jit(solution)/shard_map/ppermute | solution.py:820
  152.4 14.0 %copy-start.5 = (bf16[2,768,384]{2,1,0:T(8,128)(2,1)S(1)}, bf16[2,768,384]{2,1,0:T(8,128)(2,1)}, u32[]{:S(2)}) copy-start(bf16[2,768,384]{2,1,0:T(8,128)(2,1)} %shard_map.514) | copy-start | bytes 3538948
  164.1 4.3 %copy-start.6 = (bf16[384,1536]{1,0:T(8,128)(2,1)S(1)}, bf16[384,1536]{1,0:T(8,128)(2,1)}, u32[]{:S(2)}) copy-start(bf16[384,1536]{1,0:T(8,128)(2,1)} %shard_map.518) | copy-start | bytes 3538948
  164.1 10.2 %collective-permute-start.36 = (bf16[384,768]{1,0:T(8,128)(2,1)S(1)}, bf16[384,768]{1,0:T(8,128)(2,1)S(1)}, u32[]{:S(2)}, u32[]{:S(2)}) collective-permute-start(bf16[384,768]{1,0:T(8,128)(2,1)S(1)} %fusion.8), channel_id=1, source_target_pairs={{0,4},{1,3},{2,6},{3,1},{4,0},{5,7},{6,2},{7,5},{8,12},{9,11},{10,... | collective-permute-start | bytes 1769480 | tf_op jit(solution)/shard_map/ppermute | solution.py:820
  166.7 7.6 %copy-start.7 = (bf16[768,768]{1,0:T(8,128)(2,1)S(1)}, bf16[768,768]{1,0:T(8,128)(2,1)}, u32[]{:S(2)}) copy-start(bf16[768,768]{1,0:T(8,128)(2,1)} %shard_map.521) | copy-start | bytes 3538948
  166.7 18.3 %collective-permute-start.16 = (bf16[768,384]{1,0:T(8,128)(2,1)S(1)}, bf16[768,384]{1,0:T(8,128)(2,1)S(1)}, u32[]{:S(2)}, u32[]{:S(2)}) collective-permute-start(bf16[768,384]{1,0:T(8,128)(2,1)S(1)} %fusion.2), channel_id=1, source_target_pairs={{0,8},{1,25},{2,10},{3,27},{4,12},{5,29},{6,14},{7,31},{8,0},{9,17... | collective-permute-start | bytes 1769480 | tf_op jit(solution)/shard_map/ppermute | solution.py:820
  169.7 38.4 %collective-permute-start.29 = (bf16[192,1536]{1,0:T(8,128)(2,1)S(1)}, bf16[192,1536]{1,0:T(8,128)(2,1)S(1)}, u32[]{:S(2)}, u32[]{:S(2)}) collective-permute-start(bf16[192,1536]{1,0:T(8,128)(2,1)S(1)} %fusion.1), channel_id=1, source_target_pairs={{0,8},{1,25},{2,10},{3,27},{4,12},{5,29},{6,14},{7,31},{8,0},{9,17... | collective-permute-start | bytes 1769480 | tf_op jit(solution)/shard_map/ppermute | solution.py:820
  175.6 55.4 %collective-permute-start.37 = (bf16[384,768]{1,0:T(8,128)(2,1)S(1)}, bf16[384,768]{1,0:T(8,128)(2,1)S(1)}, u32[]{:S(2)}, u32[]{:S(2)}) collective-permute-start(bf16[384,768]{1,0:T(8,128)(2,1)S(1)} %fusion), channel_id=1, source_target_pairs={{0,8},{1,25},{2,10},{3,27},{4,12},{5,29},{6,14},{7,31},{8,0},{9,17... | collective-permute-start | bytes 1769480 | tf_op jit(solution)/shard_map/ppermute | solution.py:820
  185.1 49.8 %collective-permute-start.17 = (bf16[768,384]{1,0:T(8,128)(2,1)S(1)}, bf16[768,384]{1,0:T(8,128)(2,1)S(1)}, u32[]{:S(2)}, u32[]{:S(2)}) collective-permute-start(bf16[768,384]{1,0:T(8,128)(2,1)S(1)} %add_convert_fusion.9), channel_id=1, source_target_pairs={{0,24},{1,9},{2,26},{3,11},{4,28},{5,13},{6,30},{7,15},{8,16},{9,1... | collective-permute-start | bytes 1769480 | tf_op jit(solution)/shard_map/ppermute | solution.py:820
  208.2 27.5 %collective-permute-start.30 = (bf16[192,1536]{1,0:T(8,128)(2,1)S(1)}, bf16[192,1536]{1,0:T(8,128)(2,1)S(1)}, u32[]{:S(2)}, u32[]{:S(2)}) collective-permute-start(bf16[192,1536]{1,0:T(8,128)(2,1)S(1)} %add_convert_fusion.5), channel_id=1, source_target_pairs={{0,24},{1,9},{2,26},{3,11},{4,28},{5,13},{6,30},{7,15},{8,16},{9,1... | collective-permute-start | bytes 1769480 | tf_op jit(solution)/shard_map/ppermute | solution.py:820
  231.2 15.2 %collective-permute-start.38 = (bf16[384,768]{1,0:T(8,128)(2,1)S(1)}, bf16[384,768]{1,0:T(8,128)(2,1)S(1)}, u32[]{:S(2)}, u32[]{:S(2)}) collective-permute-start(bf16[384,768]{1,0:T(8,128)(2,1)S(1)} %add_convert_fusion.1), channel_id=1, source_target_pairs={{0,24},{1,9},{2,26},{3,11},{4,28},{5,13},{6,30},{7,15},{8,16},{9,1... | collective-permute-start | bytes 1769480 | tf_op jit(solution)/shard_map/ppermute | solution.py:820
  235.1 12.9 %collective-permute-start.18 = (bf16[768,384]{1,0:T(8,128)(2,1)S(1)}, bf16[768,384]{1,0:T(8,128)(2,1)S(1)}, u32[]{:S(2)}, u32[]{:S(2)}) collective-permute-start(bf16[768,384]{1,0:T(8,128)(2,1)S(1)} %add_convert_fusion.8), channel_id=1, source_target_pairs={{0,4},{1,3},{2,6},{3,1},{4,0},{5,7},{6,2},{7,5},{8,12},{9,11},{10,... | collective-permute-start | bytes 1769480 | tf_op jit(solution)/shard_map/ppermute | solution.py:820
  235.8 12.0 %copy-start.27 = (f32[2,3072]{1,0:T(2,128)S(1)}, f32[2,3072]{1,0:T(2,128)}, u32[]{:S(2)}) copy-start(f32[2,3072]{1,0:T(2,128)} %get-tuple-element.112) | copy-start | bytes 73732
  235.8 12.0 %copy-start.21 = (f32[4,768]{1,0:T(4,128)S(1)}, f32[4,768]{1,0:T(4,128)}, u32[]{:S(2)}) copy-start(f32[4,768]{1,0:T(4,128)} %get-tuple-element.109) | copy-start | bytes 36868
  235.8 12.0 %copy-start.22 = (f32[4,768]{1,0:T(4,128)S(1)}, f32[4,768]{1,0:T(4,128)}, u32[]{:S(2)}) copy-start(f32[4,768]{1,0:T(4,128)} %get-tuple-element.110) | copy-start | bytes 36868
  235.9 12.0 %copy-start.24 = (f32[3,768]{1,0:T(4,128)S(1)}, f32[3,768]{1,0:T(4,128)}, u32[]{:S(2)}) copy-start(f32[3,768]{1,0:T(4,128)} %get-tuple-element.111) | copy-start | bytes 27652
  235.9 15.6 %collective-permute-start.31 = (bf16[192,1536]{1,0:T(8,128)(2,1)S(1)}, bf16[192,1536]{1,0:T(8,128)(2,1)}, u32[]{:S(2)}, u32[]{:S(2)}) collective-permute-start(bf16[192,1536]{1,0:T(8,128)(2,1)S(1)} %add_convert_fusion.4), channel_id=1, source_target_pairs={{0,4},{1,3},{2,6},{3,1},{4,0},{5,7},{6,2},{7,5},{8,12},{9,11},{10,... | collective-permute-start | bytes 1769480 | tf_op jit(solution)/shard_map/ppermute | solution.py:820
  246.5 3.8 %copy-start.12 = (bf16[384,768]{1,0:T(8,128)(2,1)}, bf16[384,768]{1,0:T(8,128)(2,1)S(1)}, u32[]{:S(2)}) copy-start(bf16[384,768]{1,0:T(8,128)(2,1)S(1)} %add_convert_fusion) | copy-start | bytes 1769476
  246.5 15.5 %collective-permute-start.39 = (bf16[384,768]{1,0:T(8,128)(2,1)S(1)}, bf16[384,768]{1,0:T(8,128)(2,1)}, u32[]{:S(2)}, u32[]{:S(2)}) collective-permute-start(bf16[384,768]{1,0:T(8,128)(2,1)S(1)} %add_convert_fusion), channel_id=1, source_target_pairs={{0,4},{1,3},{2,6},{3,1},{4,0},{5,7},{6,2},{7,5},{8,12},{9,11},{10,... | collective-permute-start | bytes 1769480 | tf_op jit(solution)/shard_map/ppermute | solution.py:820
  247.9 24.7 %collective-permute-start.20 = (f32[19,768]{1,0:T(8,128)S(1)}, f32[19,768]{1,0:T(8,128)S(1)}, u32[]{:S(2)}, u32[]{:S(2)}) collective-permute-start(f32[19,768]{1,0:T(8,128)S(1)} %pad_maximum_fusion), channel_id=1, source_target_pairs={{0,1},{1,0},{2,3},{3,2},{4,5},{5,4},{6,7},{7,6},{8,9},{9,8},{10,11... | collective-permute-start | bytes 175112 | tf_op jit(solution)/shard_map/ppermute | solution.py:824
  250.3 2.7 copy-start.4
  250.3 84.1 %collective-permute-start.19 = (bf16[2,768,384]{2,1,0:T(8,128)(2,1)S(1)}, bf16[2,768,384]{2,1,0:T(8,128)(2,1)}, u32[]{:S(2)}, u32[]{:S(2)}) collective-permute-start(bf16[2,768,384]{2,1,0:T(8,128)(2,1)S(1)} %maximum_select_fusion.1.half), channel_id=1, source_target_pairs={{0,2},{1,5},{2,0},{3,7},{4,6},{5,1},{6,4},{7,3},{8,10},{9,13},{10,... | collective-permute-start | bytes 3538952 | tf_op jit(solution)/shard_map/ppermute | solution.py:820
  251.5 10.5 %copy-start.13 = (bf16[384,768]{1,0:T(8,128)(2,1)S(1)}, bf16[384,768]{1,0:T(8,128)(2,1)}, u32[]{:S(2)}) copy-start(bf16[384,768]{1,0:T(8,128)(2,1)} %copy-done.12) | copy-start | bytes 1769476
  253.0 10.4 %copy-start.2 = (bf16[2,192,1536]{2,1,0:T(8,128)(2,1)}, bf16[2,192,1536]{2,1,0:T(8,128)(2,1)S(1)}, u32[]{:S(2)}) copy-start(bf16[2,192,1536]{2,1,0:T(8,128)(2,1)S(1)} %maximum_select_fusion.2.half) | copy-start | bytes 3538948
  253.0 85.6 %collective-permute-start.32 = (bf16[2,192,1536]{2,1,0:T(8,128)(2,1)S(1)}, bf16[2,192,1536]{2,1,0:T(8,128)(2,1)}, u32[]{:S(2)}, u32[]{:S(2)}) collective-permute-start(bf16[2,192,1536]{2,1,0:T(8,128)(2,1)S(1)} %maximum_select_fusion.2.half), channel_id=1, source_target_pairs={{0,2},{1,5},{2,0},{3,7},{4,6},{5,1},{6,4},{7,3},{8,10},{9,13},{10,... | collective-permute-start | bytes 3538952 | tf_op jit(solution)/shard_map/ppermute | solution.py:820
  263.4 9.2 %copy-start.3 = (bf16[2,384,768]{2,1,0:T(8,128)(2,1)}, bf16[2,384,768]{2,1,0:T(8,128)(2,1)S(1)}, u32[]{:S(2)}) copy-start(bf16[2,384,768]{2,1,0:T(8,128)(2,1)S(1)} %maximum_select_fusion.3.half) | copy-start | bytes 3538948
  263.4 79.8 %collective-permute-start.40 = (bf16[2,384,768]{2,1,0:T(8,128)(2,1)S(1)}, bf16[2,384,768]{2,1,0:T(8,128)(2,1)}, u32[]{:S(2)}, u32[]{:S(2)}) collective-permute-start(bf16[2,384,768]{2,1,0:T(8,128)(2,1)S(1)} %maximum_select_fusion.3.half), channel_id=1, source_target_pairs={{0,2},{1,5},{2,0},{3,7},{4,6},{5,1},{6,4},{7,3},{8,10},{9,13},{10,... | collective-permute-start | bytes 3538952 | tf_op jit(solution)/shard_map/ppermute | solution.py:820
  265.6 7.0 %copy-start.19 = (f32[8,768]{1,0:T(8,128)S(1)}, f32[8,768]{1,0:T(8,128)}, u32[]{:S(2)}) copy-start(f32[8,768]{1,0:T(8,128)} %copy-done.18) | copy-start | bytes 73732
  265.6 7.0 %copy-start.23 = (f32[4,768]{1,0:T(4,128)S(1)}, f32[4,768]{1,0:T(4,128)}, u32[]{:S(2)}) copy-start(f32[4,768]{1,0:T(4,128)} %get-tuple-element.110) | copy-start | bytes 36868
  265.6 7.0 %copy-start.25 = (f32[3,768]{1,0:T(4,128)S(1)}, f32[3,768]{1,0:T(4,128)}, u32[]{:S(2)}) copy-start(f32[3,768]{1,0:T(4,128)} %get-tuple-element.111) | copy-start | bytes 27652
  272.6 59.1 %collective-permute-start.10 = (f32[512,384]{1,0:T(8,128)}, f32[512,384]{1,0:T(8,128)}, u32[]{:S(2)}, u32[]{:S(2)}) collective-permute-start(f32[512,384]{1,0:T(8,128)} %get-tuple-element.105), channel_id=1, source_target_pairs={{0,1},{1,0},{2,3},{3,2},{4,5},{5,4},{6,7},{7,6},{8,9},{9,8},{10,11... | collective-permute-start | bytes 2359304 | tf_op jit(solution)/shard_map/ppermute | solution.py:824
  272.7 20.0 %collective-permute-start.21 = (f32[19,768]{1,0:T(8,128)S(1)}, f32[19,768]{1,0:T(8,128)S(1)}, u32[]{:S(2)}, u32[]{:S(2)}) collective-permute-start(f32[19,768]{1,0:T(8,128)S(1)} %fusion.9), channel_id=1, source_target_pairs={{0,2},{1,5},{2,0},{3,7},{4,6},{5,1},{6,4},{7,3},{8,10},{9,13},{10,... | collective-permute-start | bytes 175112 | tf_op jit(solution)/shard_map/ppermute | solution.py:820
  292.7 4.5 %collective-permute-start.22 = (f32[19,768]{1,0:T(8,128)S(1)}, f32[19,768]{1,0:T(8,128)S(1)}, u32[]{:S(2)}, u32[]{:S(2)}) collective-permute-start(f32[19,768]{1,0:T(8,128)S(1)} %add.100), channel_id=1, source_target_pairs={{0,4},{1,3},{2,6},{3,1},{4,0},{5,7},{6,2},{7,5},{8,12},{9,11},{10,... | collective-permute-start | bytes 175112 | tf_op jit(solution)/shard_map/ppermute | solution.py:820
  297.2 4.4 %collective-permute-start.23 = (f32[19,768]{1,0:T(8,128)S(1)}, f32[19,768]{1,0:T(8,128)S(1)}, u32[]{:S(2)}, u32[]{:S(2)}) collective-permute-start(f32[19,768]{1,0:T(8,128)S(1)} %add.101), channel_id=1, source_target_pairs={{0,8},{1,25},{2,10},{3,27},{4,12},{5,29},{6,14},{7,31},{8,0},{9,17... | collective-permute-start | bytes 175112 | tf_op jit(solution)/shard_map/ppermute | solution.py:820
  301.7 8.2 %collective-permute-start.24 = (f32[19,768]{1,0:T(8,128)S(1)}, f32[19,768]{1,0:T(8,128)S(1)}, u32[]{:S(2)}, u32[]{:S(2)}) collective-permute-start(f32[19,768]{1,0:T(8,128)S(1)} %add.102), channel_id=1, source_target_pairs={{0,24},{1,9},{2,26},{3,11},{4,28},{5,13},{6,30},{7,15},{8,16},{9,1... | collective-permute-start | bytes 175112 | tf_op jit(solution)/shard_map/ppermute | solution.py:820
  309.9 19.3 %collective-permute-start.9 = (bf16[512,384]{1,0:T(8,128)(2,1)}, bf16[512,384]{1,0:T(8,128)(2,1)}, u32[]{:S(2)}, u32[]{:S(2)}) collective-permute-start(bf16[512,384]{1,0:T(8,128)(2,1)} %get-tuple-element.88), channel_id=1, source_target_pairs={{0,1},{1,0},{2,3},{3,2},{4,5},{5,4},{6,7},{7,6},{8,9},{9,8},{10,11... | collective-permute-start | bytes 1179656 | tf_op jit(solution)/shard_map/ppermute | solution.py:824
  329.2 2.5 copy-start.16
  (6 other events, 5.3 us)

commit v2 on v1

v2 whole, which is shorter than its diff:
```python
from functools import partial
import math

import jax
import jax.numpy as jnp
from jax import lax
from jax.experimental import pallas as pl
from jax.experimental.pallas import tpu as pltpu
from jax.sharding import PartitionSpec as P

HD = 64
BLOCK = 512
LANES = 128
TILE = 512

norm_eps = 1e-05
gate_temper = 2.0 / 3.0
stretch_low = -0.1
stretch_high = 1.1
target_share = 0.4
masked_score = -1000000000.0
open_shift = gate_temper * math.log(-stretch_low / stretch_high)


f32 = jnp.float32
bf16 = jnp.bfloat16


def to_low(values_in):
    return values_in.astype(bf16)


def contract(first, second, first_dim, second_dim):
    return lax.dot_general(
        first, second, (((first_dim,), (second_dim,)), ((), ())), preferred_element_type=f32
    )


def column_sum(values_in):
    return jnp.sum(values_in, axis=0, keepdims=True)


def row_sum(values_in):
    return jnp.sum(values_in, axis=1, keepdims=True)


def sigmoid(values_in):
    return 1.0 / (1.0 + jnp.exp(-values_in))


def stretched(gate_noise, log_alpha):
    relaxed = sigmoid(
        (jnp.log(gate_noise) - jnp.log(1.0 - gate_noise) + log_alpha) / gate_temper
    )
    return relaxed, relaxed * (stretch_high - stretch_low) + stretch_low


def hard_concrete(gate_noise, log_alpha):
    return jnp.clip(stretched(gate_noise, log_alpha)[1], 0.0, 1.0)


def gate_slope(gate_noise, log_alpha):
    relaxed, wide = stretched(gate_noise, log_alpha)
    slope = relaxed * (1.0 - relaxed) * ((stretch_high - stretch_low) / gate_temper)
    return jnp.where((wide > 0.0) & (wide < 1.0), slope, 0.0)


def open_share(log_alpha):
    return sigmoid(log_alpha - open_shift)


class Pack:
    def __init__(self, width, units):
        self.width, self.units = width, units
        at = 0
        for name in ("b_query", "b_value", "b_attn_out", "gain_one", "shift_one"):
            setattr(self, name, (at, width))
            at += width
        for name in ("b_down", "gain_two", "shift_two", "hidden_alpha", "hidden_noise"):
            setattr(self, name, (at, width))
            at += width
        for name in ("b_up", "unit_alpha", "unit_noise"):
            setattr(self, name, (at, units))
            at += units
        for name in ("head_alpha", "head_noise", "scalars"):
            setattr(self, name, (at, LANES))
            at += LANES
        self.total = at


def pack_kernel(pack, counts, *refs):
    out_ref = refs[-1]
    out_ref[...] = jnp.full(out_ref.shape, 0.5, f32)
    for ref, (spot, lane) in zip(refs[:-1], counts):
        size = ref.shape[0]
        out_ref[:, spot[0] + lane : spot[0] + lane + size] = ref[...].reshape(1, size)


def take(pack_ref, spot):
    return pack_ref[:, spot[0] : spot[0] + spot[1]]


def natural(core, own, peer):
    at_peer = core.astype(f32)
    at_own = 1.0 - at_peer
    return jnp.concatenate((own * at_own + peer * at_peer, peer * at_own + own * at_peer), axis=1)


def both(core, own_ref, peer_ref, spot):
    return natural(core, take(own_ref, spot), take(peer_ref, spot))


def hidden_gates(core, pack, own_ref, peer_ref):
    return hard_concrete(
        both(core, own_ref, peer_ref, pack.hidden_noise),
        both(core, own_ref, peer_ref, pack.hidden_alpha),
    )


def head_row(pack, own_ref, peer_ref, heads):
    parts = []
    for ref in (own_ref, peer_ref):
        gates = hard_concrete(take(ref, pack.head_noise), take(ref, pack.head_alpha))
        for at in range(heads):
            parts.append(jnp.broadcast_to(gates[:, at : at + 1], (1, HD)))
    return jnp.concatenate(parts, axis=1)


def scalar_gate(pack, own_ref, at):
    numbers = take(own_ref, pack.scalars)
    return hard_concrete(numbers[:, at + 1 : at + 2], numbers[:, at : at + 1])


def half_mask(side, dtype):
    lane = lax.broadcasted_iota(jnp.int32, (1, LANES), 1)
    inside = (lane < HD) if side == 0 else (lane >= HD)
    return jnp.where(inside, 1.0, 0.0).astype(dtype)


def pick_half(first, second):
    lane = lax.broadcasted_iota(jnp.int32, (1, LANES), 1)
    return jnp.where(lane < HD, first, second)


def norm_back(grad_normed, normed, inv_scale):
    width = normed.shape[1]
    mean_grad = row_sum(grad_normed) * (1.0 / width)
    mean_both = row_sum(grad_normed * normed) * (1.0 / width)
    return inv_scale * (grad_normed - mean_grad - normed * mean_both)


def norm_forward(resid):
    width = resid.shape[1]
    row_mean = row_sum(resid) * (1.0 / width)
    row_var = row_sum(resid * resid) * (1.0 / width) - row_mean * row_mean
    inv_scale = lax.rsqrt(row_var + norm_eps)
    return (resid - row_mean) * inv_scale, inv_scale


def own_rows(ref, core):
    return ref[pl.ds(pl.multiple_of(core * BLOCK, BLOCK), BLOCK), :]


def token_line(ref, core):
    lanes_of = BLOCK // LANES
    rows = [ref[pl.ds(core * lanes_of + at, 1), :] for at in range(lanes_of)]
    return jnp.concatenate(rows, axis=1).astype(f32)


def to_side(line):
    return jnp.broadcast_to(line, (LANES, BLOCK)).T[:, 0:1]


def rows_in(core, width, own_ref, peer_ref, out_ref, sems):
    rows = pl.ds(pl.multiple_of(core * BLOCK, BLOCK), BLOCK)
    own_at = pl.multiple_of(core * width, LANES)
    peer_at = pl.multiple_of((1 - core) * width, LANES)
    return (
        pltpu.make_async_copy(own_ref.at[rows, :], out_ref.at[:, pl.ds(own_at, width)], sems.at[0]),
        pltpu.make_async_copy(
            peer_ref.at[rows, :], out_ref.at[:, pl.ds(peer_at, width)], sems.at[1]
        ),
    )


def attend_kernel(
    pack,
    core_ref,
    x_own,
    x_peer,
    wq_own,
    wk_own,
    wv_own,
    wq_peer,
    wk_peer,
    wv_peer,
    wa_own,
    wa_peer,
    pack_own,
    pack_peer,
    segments,
    valid,
    weights_out,
    query_out,
    key_out,
    value_out,
    context_out,
    gated_own_out,
    gated_peer_out,
    stats_out,
    biased_out,
    normed_out,
    hidden_out,
    x_nat,
    mask_bias,
    gate_row,
    weight_in,
    weight_out,
    biases,
    total,
    sems,
):
    pair = pl.program_id(0)
    core = core_ref[0]
    width = pack.width
    heads = width // HD
    own_pairs = pl.num_programs(0) // 2

    @pl.when(pair == 0)
    def _():
        copies = rows_in(core, width, x_own, x_peer, x_nat, sems)
        for copy in copies:
            copy.start()
        gate_row[...] = head_row(pack, pack_own, pack_peer, heads)
        segment_line, valid_line = token_line(segments, core), token_line(valid, core)
        segment_side, valid_side = to_side(segment_line), to_side(valid_line)
        allowed = (segment_side == segment_line) & ((valid_line == 1.0) | (valid_side == 0.0))
        mask_bias[...] = jnp.where(allowed, 0.0, masked_score)
        for copy in copies:
            copy.wait()

    def load(at, pack_ref, query_ref, key_ref, value_ref, out_ref):
        weight_in[:, :LANES] = query_ref[...]
        weight_in[:, LANES : 2 * LANES] = key_ref[...]
        weight_in[:, 2 * LANES :] = value_ref[...]
        weight_out[...] = out_ref[...]
        spot = pl.multiple_of(at * LANES, LANES)
        biases[0:1, :] = pack_ref[:, pl.ds(pack.b_query[0] + spot, LANES)]
        biases[1:2, :] = pack_ref[:, pl.ds(pack.b_value[0] + spot, LANES)]

    @pl.when(pair < own_pairs)
    def _():
        load(pair, pack_own, wq_own, wk_own, wv_own, wa_own)

    @pl.when(pair >= own_pairs)
    def _():
        load(pair - own_pairs, pack_peer, wq_peer, wk_peer, wv_peer, wa_peer)

    columns = pl.ds(pl.multiple_of(pair * LANES, LANES), LANES)
    projected = contract(x_nat[...], weight_in[...], 1, 0)
    query = to_low(projected[:, :LANES] + biases[0:1, :]) * jnp.asarray(HD ** (-0.5), bf16)
    key = to_low(projected[:, LANES : 2 * LANES])
    value = to_low(projected[:, 2 * LANES :] + biases[1:2, :])
    query_out[...] = query
    key_out[...] = key
    value_out[...] = value
    value_wide = jnp.concatenate((value, jnp.ones((BLOCK, LANES), bf16)), axis=1)
    contexts = []
    lane = lax.broadcasted_iota(jnp.int32, (1, LANES), 1)
    stats = stats_out[...]
    for side in range(2):
        scores = contract(query * half_mask(side, bf16), key, 1, 1) + mask_bias[...]
        row_top = jnp.max(scores, axis=1, keepdims=True)
        weights = to_low(jnp.exp(scores - row_top))
        weights_out[side] = weights
        summed = contract(weights, value_wide, 1, 0)
        inverse = 1.0 / summed[:, LANES : 2 * LANES]
        contexts.append(summed[:, :LANES] * inverse)
        stats = jnp.where(lane == 2 * pair + side, inverse, stats)
    stats_out[...] = stats
    context = pick_half(contexts[0], contexts[1])
    context_out[...] = to_low(context)
    gated = to_low(context * gate_row[:, columns])
    attn_part = contract(gated, weight_out[...], 1, 0)

    @pl.when(pair == 0)
    def _():
        total[...] = attn_part

    @pl.when(pair > 0)
    def _():
        total[...] += attn_part

    @pl.when(pair < own_pairs)
    def _():
        gated_own_out[...] = gated

    @pl.when(pair >= own_pairs)
    def _():
        gated_peer_out[...] = gated

    @pl.when(pair == pl.num_programs(0) - 1)
    def _():
        biased = total[...] + both(core, pack_own, pack_peer, pack.b_attn_out)
        biased_out[...] = biased
        gates = hidden_gates(core, pack, pack_own, pack_peer)
        mha_gate = scalar_gate(pack, pack_own, 0)
        resid = x_nat[...].astype(f32) + biased * (mha_gate * gates)
        normed, inv_scale = norm_forward(resid)
        normed_out[...] = normed
        gain = both(core, pack_own, pack_peer, pack.gain_one)
        shift = both(core, pack_own, pack_peer, pack.shift_one)
        hidden_out[...] = to_low((normed * gain + shift) * gates)
        stats_out[...] = jnp.where(lane == LANES - 1, inv_scale, stats)


def gelu_parts(pre_act):
    whole = 0.5 + 0.5 * lax.erf(pre_act * (0.5**0.5))
    return whole, jnp.exp(-0.5 * pre_act * pre_act) * (1.0 / math.sqrt(2.0 * math.pi))


def ffn_forward_kernel(
    pack,
    core_ref,
    hidden,
    normed,
    up_own,
    up_peer,
    down_own,
    down_peer,
    pack_own,
    pack_peer,
    teacher_own,
    teacher_peer,
    valid,
    mixed_own_out,
    mixed_peer_out,
    active_out,
    slope_out,
    output_own,
    output_peer,
    grad_resid_out,
    grad_ffn_out,
    sums_out,
    total,
    normed_in,
    target,
    sems,
):
    step = pl.program_id(0)
    core = core_ref[0]
    own_steps = pl.num_programs(0) // 2
    width = pack.width
    copies = (
        pltpu.make_async_copy(normed, normed_in, sems.at[2]),
        *rows_in(core, width, teacher_own, teacher_peer, target, sems),
    )

    def tile(at, up_ref, down_ref, pack_ref, mixed_ref):
        spot = pl.multiple_of(at * TILE, TILE)

        def cut(place):
            return pack_ref[:, pl.ds(place[0] + spot, TILE)]

        pre_act = contract(hidden[...], up_ref[...], 1, 0) + cut(pack.b_up)
        whole, density = gelu_parts(pre_act)
        active = pre_act * whole
        unit_gate = hard_concrete(cut(pack.unit_noise), cut(pack.unit_alpha))
        mixed = to_low(active * unit_gate)
        mixed_ref[...] = mixed
        active_out[...] = to_low(active)
        slope_out[...] = to_low((whole + pre_act * density) * unit_gate)
        return contract(mixed, down_ref[...], 1, 0)

    @pl.when(step == 0)
    def _():
        for copy in copies:
            copy.start()
        total[...] = tile(step, up_own, down_own, pack_own, mixed_own_out)

    @pl.when((step > 0) & (step < own_steps))
    def _():
        total[...] += tile(step, up_own, down_own, pack_own, mixed_own_out)

    @pl.when(step >= own_steps)
    def _():
        total[...] += tile(step - own_steps, up_peer, down_peer, pack_peer, mixed_peer_out)

    @pl.when(step == pl.num_programs(0) - 1)
    def _():
        gates = hidden_gates(core, pack, pack_own, pack_peer)
        ffn_gate = scalar_gate(pack, pack_own, 2)

        def vector(spot):
            return both(core, pack_own, pack_peer, spot)

        for copy in copies:
            copy.wait()
        biased = total[...] + vector(pack.b_down)
        hidden_one = (normed_in[...] * vector(pack.gain_one) + vector(pack.shift_one)) * gates
        normed_two, inv_two = norm_forward(hidden_one + biased * (ffn_gate * gates))
        gain = vector(pack.gain_two)
        final = (normed_two * gain + vector(pack.shift_two)) * gates
        final_low = to_low(final)

        def split(own_ref, peer_ref, values_in):
            @pl.when(core == 0)
            def _():
                own_ref[...] = values_in[:, :width]
                peer_ref[...] = values_in[:, width:]

            @pl.when(core == 1)
            def _():
                own_ref[...] = values_in[:, width:]
                peer_ref[...] = values_in[:, :width]

        split(output_own, output_peer, final_low)
        valid_side = to_side(token_line(valid, core))
        grad_final = (final - target[...].astype(f32)) * valid_side
        grad_resid = norm_back(grad_final * (gates * gain), normed_two, inv_two)
        grad_resid_out[...] = grad_resid
        grad_ffn_out[...] = to_low(grad_resid * (ffn_gate * gates))
        sums_out[0:1, :] = column_sum(grad_final * normed_two)
        sums_out[1:2, :] = column_sum(grad_final)
        sums_out[2:3, :] = column_sum(grad_resid * biased)
        sums_out[3:4, :] = column_sum(grad_resid)


def ffn_pre_kernel(
    pack,
    core_ref,
    grad_ffn,
    active,
    slope,
    down_own,
    down_peer,
    grad_pre_own,
    grad_pre_peer,
    unit_sums_out,
):
    step = pl.program_id(0)
    core = core_ref[0]
    own_steps = pl.num_programs(0) // 2
    units = pack.units

    def tile(at, side, down_ref, pre_ref):
        grad_mixed = contract(grad_ffn[...], down_ref[...], 1, 1)
        grad_pre = to_low(grad_mixed * slope[...].astype(f32))
        pre_ref[...] = grad_pre
        spot = pl.multiple_of(side * units + at * TILE, TILE)
        unit_sums_out[0:1, pl.ds(spot, TILE)] = column_sum(grad_mixed * active[...].astype(f32))
        unit_sums_out[1:2, pl.ds(spot, TILE)] = column_sum(grad_pre.astype(f32))

    @pl.when(step < own_steps)
    def _():
        tile(step, core, down_own, grad_pre_own)

    @pl.when(step >= own_steps)
    def _():
        tile(step - own_steps, 1 - core, down_peer, grad_pre_peer)


def ffn_backward_kernel(
    pack,
    core_ref,
    grad_pre_own,
    grad_pre_peer,
    grad_resid_two,
    normed,
    biased,
    stats,
    up_own,
    up_peer,
    pack_own,
    pack_peer,
    grad_resid_out,
    grad_attn_out,
    sums_out,
    total,
    resid_in,
    normed_in,
    biased_in,
    sems,
):
    step = pl.program_id(0)
    core = core_ref[0]
    own_steps = pl.num_programs(0) // 2
    copies = (
        pltpu.make_async_copy(grad_resid_two, resid_in, sems.at[0]),
        pltpu.make_async_copy(normed, normed_in, sems.at[1]),
        pltpu.make_async_copy(biased, biased_in, sems.at[2]),
    )

    @pl.when(step == 0)
    def _():
        for copy in copies:
            copy.start()
        total[...] = contract(grad_pre_own[...], up_own[...], 1, 1)

    @pl.when((step > 0) & (step < own_steps))
    def _():
        total[...] += contract(grad_pre_own[...], up_own[...], 1, 1)

    @pl.when(step >= own_steps)
    def _():
        total[...] += contract(grad_pre_peer[...], up_peer[...], 1, 1)

    @pl.when(step == pl.num_programs(0) - 1)
    def _():
        gates = hidden_gates(core, pack, pack_own, pack_peer)
        mha_gate = scalar_gate(pack, pack_own, 0)
        gain = both(core, pack_own, pack_peer, pack.gain_one)
        for copy in copies:
            copy.wait()
        grad_hidden = resid_in[...] + total[...]
        normed_one = normed_in[...]
        sums_out[0:1, :] = column_sum(grad_hidden * normed_one)
        sums_out[1:2, :] = column_sum(grad_hidden)
        inv_scale = stats[:, LANES - 1 : LANES]
        grad_resid = norm_back(grad_hidden * (gates * gain), normed_one, inv_scale)
        grad_resid_out[...] = grad_resid
        grad_attn_out[...] = to_low(grad_resid * (mha_gate * gates))
        sums_out[2:3, :] = column_sum(grad_resid * biased_in[...])
        sums_out[3:4, :] = column_sum(grad_resid)


def attend_back_kernel(
    pack,
    side_is_own,
    core_ref,
    weights,
    query_ref,
    key_ref,
    value_ref,
    context_ref,
    stats,
    grad_attn,
    wa_ref,
    pack_own,
    pack_peer,
    out_ref,
    sums_out,
    gate_row,
):
    at = pl.program_id(0)
    core = core_ref[0]
    width = pack.width
    pair = at if side_is_own else at + pl.num_programs(0)

    @pl.when(at == 0)
    def _():
        gate_row[...] = head_row(pack, pack_own, pack_peer, width // HD)

    columns = pl.ds(pl.multiple_of(pair * LANES, LANES), LANES)
    lane = lax.broadcasted_iota(jnp.int32, (1, LANES), 1)

    query, key, value = query_ref[...], key_ref[...], value_ref[...]
    context = context_ref[...].astype(f32)
    grad_context = contract(grad_attn[...], wa_ref[...], 1, 1)
    spot = pl.ds(pl.multiple_of(at * LANES, LANES), LANES)
    sums_out[0:1, spot] = column_sum(grad_context * context)
    inverses = [
        row_sum(jnp.where(lane == 2 * pair + side, stats[...], 0.0)) for side in range(2)
    ]
    grad_low = to_low(grad_context * gate_row[:, columns] * pick_half(inverses[0], inverses[1]))
    product = grad_low.astype(f32) * context
    found = []
    for side in range(2):
        mask = half_mask(side, f32)
        level = row_sum(product * mask)
        grad_probs = contract(grad_low * mask.astype(bf16), value, 1, 1)
        chosen = weights[side]
        grad_raw = to_low(chosen.astype(f32) * (grad_probs - level))
        found.append(
            (
                contract(grad_raw, key, 1, 0),
                contract(grad_raw, query, 0, 0),
                contract(chosen, grad_low, 0, 0),
            )
        )
    grad_query = to_low(pick_half(found[0][0], found[1][0]) * HD ** (-0.5))
    grad_key = to_low(pick_half(found[0][1], found[1][1]))
    grad_value = to_low(pick_half(found[0][2], found[1][2]))
    for place, grad in enumerate((grad_query, grad_key, grad_value)):
        at_lane = pl.multiple_of(place * width + at * LANES, LANES)
        out_ref[:, pl.ds(at_lane, LANES)] = grad
    sums_out[1:2, spot] = column_sum(grad_query.astype(f32))
    sums_out[2:3, spot] = column_sum(grad_value.astype(f32))


def down_grad_kernel(bit_ref, mixed, mixed_near, grad, grad_near, sent_out, kept_out):
    summed = to_low(
        contract(mixed[...], grad[...], 0, 0) + contract(mixed_near[...], grad_near[...], 0, 0)
    )
    first = pl.program_id(0) < pl.num_programs(0) // 2

    @pl.when(first)
    def _():
        sent_out[...] = summed

    @pl.when(jnp.logical_not(first))
    def _():
        kept_out[...] = summed


def attn_out_grad_kernel(bit_ref, gated, gated_near, grad, grad_near, sent_out, kept_out):
    width = gated.shape[1]
    part = width // 4
    summed = to_low(
        contract(gated[...], grad[...], 0, 0) + contract(gated_near[...], grad_near[...], 0, 0)
    )

    def put(ref):
        for at in range(4):
            ref[:, at * width : (at + 1) * width] = summed[at * part : (at + 1) * part]

    @pl.when(pl.program_id(0) == 0)
    def _():
        put(sent_out)

    @pl.when(pl.program_id(0) == 1)
    def _():
        put(kept_out)


def attend_grad_kernel(
    half_ref,
    core_ref,
    x_own,
    x_peer,
    grad,
    grad_near,
    out_ref,
    source,
    sem,
):
    core = core_ref[0]

    @pl.when(half_ref[0] == core)
    def _():
        copy = pltpu.make_async_copy(x_own, source, sem)
        copy.start()
        copy.wait()

    @pl.when(half_ref[0] != core)
    def _():
        copy = pltpu.make_async_copy(x_peer, source, sem)
        copy.start()
        copy.wait()

    summed = contract(own_rows(source, core), grad[...], 0, 0) + contract(
        own_rows(source, 1 - core), grad_near[...], 0, 0
    )
    out_ref[...] = to_low(summed)


def input_grad_kernel(
    width,
    core_ref,
    grad_resid,
    grad_own,
    grad_peer,
    wq_own,
    wk_own,
    wv_own,
    wq_peer,
    wk_peer,
    wv_peer,
    own_out,
    peer_out,
):
    core = core_ref[0]
    summed = grad_resid[...]
    for grad, weights in (
        (grad_own, (wq_own, wk_own, wv_own)),
        (grad_peer, (wq_peer, wk_peer, wv_peer)),
    ):
        for place, weight in enumerate(weights):
            summed = summed + contract(
                grad[:, place * width : (place + 1) * width], weight[...], 1, 1
            )

    @pl.when(core == 0)
    def _():
        own_out[...] = summed[:, :width]
        peer_out[...] = summed[:, width:]

    @pl.when(core == 1)
    def _():
        own_out[...] = summed[:, width:]
        peer_out[...] = summed[:, :width]


def place_kernel(bit_ref, half, other, out_ref):
    step = pl.program_id(0)

    @pl.when(step < 2)
    def _():
        out_ref[...] = half[...].astype(f32)

    @pl.when(step >= 2)
    def _():
        out_ref[...] = other[...].astype(f32)


def place_up_kernel(bit_ref, half, other, up_out, attn_out):
    width = attn_out.shape[1]
    rows = up_out.shape[0]
    part = width // 4

    def put(ref):
        up_out[...] = ref[:rows, :].astype(f32)
        for at in range(4):
            attn_out[at * part : (at + 1) * part, :] = ref[
                rows:, at * width : (at + 1) * width
            ].astype(f32)

    @pl.when(pl.program_id(0) == 0)
    def _():
        put(half)

    @pl.when(pl.program_id(0) == 1)
    def _():
        put(other)


def place_attend_kernel(bit_ref, half, other, query_out, key_out, value_out):
    width = query_out.shape[1]

    def put(ref):
        for at, out in enumerate((query_out, key_out, value_out)):
            out[...] = ref[:, at * width : (at + 1) * width].astype(f32)

    @pl.when(pl.program_id(0) == 0)
    def _():
        put(half)

    @pl.when(pl.program_id(0) == 1)
    def _():
        put(other)


def finish_kernel(
    pack,
    core_ref,
    sums,
    pack_own,
    pack_peer,
    b_query,
    b_value,
    b_attn_out,
    gain_one,
    shift_one,
    b_up,
    b_down,
    gain_two,
    shift_two,
    head_gate,
    mha_gate,
    unit_gate,
    ffn_gate,
    hidden_gate,
    head_alpha,
    mha_alpha,
    unit_alpha,
    ffn_alpha,
    hidden_alpha,
    share_out,
    penalty_out,
):
    core = core_ref[0]
    width, units = pack.width, pack.units
    columns = pl.ds(pl.multiple_of(core * width, LANES), width)
    heads = width // HD

    def put(out_ref, line):
        out_ref[...] = line.reshape(out_ref.shape)

    def own(row):
        return sums[row : row + 1, columns]

    def vector(spot):
        return take(pack_own, spot)

    gates = hard_concrete(vector(pack.hidden_noise), vector(pack.hidden_alpha))
    mha, ffn = scalar_gate(pack, pack_own, 0), scalar_gate(pack, pack_own, 2)
    put(gain_two, gates * own(0))
    put(shift_two, gates * own(1))
    put(b_down, (ffn * gates) * own(3))
    put(gain_one, gates * own(4))
    put(shift_one, gates * own(5))
    put(b_attn_out, (mha * gates) * own(7))
    put(b_query, own(9))
    put(b_value, own(10))
    grad_hidden = (
        vector(pack.gain_two) * own(0)
        + vector(pack.shift_two) * own(1)
        + ffn * own(2)
        + vector(pack.gain_one) * own(4)
        + vector(pack.shift_one) * own(5)
        + mha * own(6)
    )
    put(hidden_gate, grad_hidden)
    all_gates = hidden_gates(core, pack, pack_own, pack_peer)
    grad_ffn_gate = row_sum(all_gates * sums[2:3, :])
    grad_mha_gate = row_sum(all_gates * sums[6:7, :])
    put(ffn_gate, grad_ffn_gate)
    put(mha_gate, grad_mha_gate)

    unit_rows = units // (2 * width)

    def unit_line(first):
        at = first + core * unit_rows
        return jnp.concatenate([sums[pl.ds(at + k, 1), :] for k in range(unit_rows)], axis=1)

    grad_unit = unit_line(11)
    put(b_up, unit_line(11 + 2 * unit_rows))
    put(unit_gate, grad_unit)
    by_head = own(8)
    lane = lax.broadcasted_iota(jnp.int32, (1, LANES), 1)
    grad_head = jnp.zeros((1, LANES), f32)
    for at in range(heads):
        grad_head = jnp.where(
            lane == at, row_sum(by_head[:, at * HD : (at + 1) * HD]), grad_head
        )
    put(head_gate, grad_head[:, :heads])

    numbers = vector(pack.scalars)
    mha_open, ffn_open = open_share(numbers[:, 0:1]), open_share(numbers[:, 2:3])
    first_weight, second_weight = numbers[:, 4:5], numbers[:, 5:6]

    def open_total(spot, count):
        return row_sum(open_share(take(pack_own, spot)[:, :count])) + row_sum(
            open_share(take(pack_peer, spot)[:, :count])
        )

    head_sum = open_total(pack.head_alpha, heads)
    unit_sum = open_total(pack.unit_alpha, units)
    hidden_sum = open_total(pack.hidden_alpha, width)
    model, inner = 2.0 * width, 2.0 * units
    scale = 1.0 / ((4.0 * model + 2.0 * inner) * model)
    kept = 4.0 * HD * mha_open * head_sum + 2.0 * ffn_open * unit_sum
    share = kept * hidden_sum * scale
    gap = share - target_share
    put(share_out, share)
    put(penalty_out, first_weight * gap + second_weight * gap * gap)
    slope = (first_weight + 2.0 * second_weight * gap) * scale
    by_heads = slope * hidden_sum * (4.0 * HD)
    by_units = slope * hidden_sum * 2.0

    def alpha_grad(noise, alpha, grad_gate, grad_open):
        opened = open_share(alpha)
        return gate_slope(noise, alpha) * grad_gate + grad_open * (opened * (1.0 - opened))

    put(
        head_alpha,
        alpha_grad(
            vector(pack.head_noise), vector(pack.head_alpha), grad_head, by_heads * mha_open
        )[:, :heads],
    )
    put(
        unit_alpha,
        alpha_grad(
            vector(pack.unit_noise), vector(pack.unit_alpha), grad_unit, by_units * ffn_open
        ),
    )
    put(
        hidden_alpha,
        alpha_grad(
            vector(pack.hidden_noise), vector(pack.hidden_alpha), grad_hidden, slope * kept
        ),
    )
    put(
        mha_alpha,
        alpha_grad(numbers[:, 1:2], numbers[:, 0:1], grad_mha_gate, by_heads * head_sum),
    )
    put(
        ffn_alpha,
        alpha_grad(numbers[:, 3:4], numbers[:, 2:3], grad_ffn_gate, by_units * unit_sum),
    )


def full(shape):
    return pl.BlockSpec(shape, lambda *at: (0,) * len(shape), pipeline_mode=pl.Buffered(1))


def anywhere():
    return pl.BlockSpec(memory_space=pl.ANY)


def every(shape, dim):
    return pl.BlockSpec(shape, lambda i: tuple(i if d == dim else 0 for d in range(2)))


def sides(steps):
    def early(shape, dim):
        return pl.BlockSpec(
            shape, lambda i: tuple(jnp.minimum(i, steps - 1) if d == dim else 0 for d in range(2))
        )

    def late(shape, dim):
        return pl.BlockSpec(
            shape, lambda i: tuple(jnp.maximum(i - steps, 0) if d == dim else 0 for d in range(2))
        )

    return early, late


def one_number():
    return pl.BlockSpec(memory_space=pltpu.SMEM)


def shaped(shape, dtype):
    return jax.ShapeDtypeStruct(shape, dtype)


class Order:
    def __init__(self):
        self.last = ()
        self.share = 1.0

    def tie(self, values_in):
        if not self.last:
            return values_in
        return lax.optimization_barrier((values_in, *self.last))[0]

    def mark(self, *values_in):
        self.last = values_in


def call(order, kernel, grid, in_specs, out_specs, out_shape, scratch, cost, args, mib=62):
    out = pl.pallas_call(
        kernel,
        grid=grid,
        in_specs=in_specs,
        out_specs=out_specs,
        out_shape=out_shape,
        scratch_shapes=scratch,
        compiler_params=pltpu.CompilerParams(vmem_limit_bytes=mib * 2**20),
        cost_estimate=pl.CostEstimate(
            flops=int(cost[0] * 1e9 * order.share),
            bytes_accessed=int(cost[1] * 1e6 * order.share),
            transcendentals=0,
        ),
    )(order.tie(args[0]), *args[1:])
    order.mark(jax.tree.leaves(out)[-1])
    return out


def call_by_half(order, kernel, grid, in_specs, out_specs, out_shape, cost, half, args, mib=62):
    out = pl.pallas_call(
        kernel,
        grid_spec=pltpu.PrefetchScalarGridSpec(
            num_scalar_prefetch=1, grid=grid, in_specs=in_specs, out_specs=out_specs
        ),
        out_shape=out_shape,
        compiler_params=pltpu.CompilerParams(vmem_limit_bytes=mib * 2**20),
        cost_estimate=pl.CostEstimate(
            flops=int(cost[0] * 1e9 * order.share),
            bytes_accessed=int(cost[1] * 1e6 * order.share),
            transcendentals=0,
        ),
    )(order.tie(half), *args)
    order.mark(jax.tree.leaves(out)[-1])
    return out


def swap_pairs(core_masks):
    rows, cores = lax.axis_size("rows"), lax.axis_size("hid")
    return [
        (row * cores + core, (row ^ core_masks[core]) * cores + core)
        for row in range(rows)
        for core in range(cores)
    ]


def swap(values_in, core_masks):
    return lax.ppermute(values_in, ("rows", "hid"), swap_pairs(core_masks))


def along(values_in, steps):
    rows, cores = lax.axis_size("rows"), lax.axis_size("hid")
    pairs = [
        (row * cores + core, (row + 4 * (steps[row // 4 % 4] - row // 4 % 4)) * cores + core)
        for row in range(rows)
        if row // 4 % 4 in steps
        for core in range(cores)
    ]
    return lax.ppermute(values_in, ("rows", "hid"), pairs)


def near(values_in):
    return lax.ppermute(values_in, "hid", [(0, 1), (1, 0)])


def spread_masks():
    rest = lax.axis_size("rows") // 4
    masks = [4 * (2**k * 2 - 1) for k in range(rest.bit_length() - 1)]
    return [(masks[k], masks[len(masks) - 1 - k]) for k in range(len(masks))]


def add_low(first, second):
    return to_low(first.astype(f32) + second.astype(f32))


def pick(values_in, at):
    return lax.dynamic_index_in_dim(values_in, at, 0, keepdims=False)


class RowSum:
    def __init__(self, order, sent_half, first_bit, second_bit):
        self.order = order
        self.first_bit, self.second_bit = first_bit, second_bit
        self.near = swap(sent_half, (1, 2))

    def halve(self, kept):
        at = self.second_bit
        kept = self.order.tie(kept)
        to_send = add_low(pick(kept, 1 - at), pick(self.near, 1 - at))
        self.own = add_low(pick(kept, at), pick(self.near, at))
        self.near = swap(to_send, (2, 1))
        self.order.mark(to_send, self.own)

    def halve_with(self, kept, below, below_near):
        kept = add_low(self.order.tie(kept), self.near)
        below = add_low(self.order.tie(below), below_near)
        rows = (kept.shape[0] + below.shape[0]) // 2
        first, second = kept[:rows], jnp.concatenate((kept[rows:], below), axis=0)
        to_send = jnp.where(self.second_bit == 0, second, first)
        self.own = jnp.where(self.second_bit == 0, first, second)
        self.near = swap(to_send, (2, 1))
        self.order.mark(to_send, self.own)

    def quarter(self, path=False):
        self.own = add_low(self.order.tie(self.own), self.near)
        masks = spread_masks()
        self.left = [partial(swap, core_masks=pair) for pair in masks]
        self.inner = None
        if path:
            steps = [{0: 1, 3: 2}, {1: 2, 2: 1}, {1: 0, 2: 3}]
            self.left = [partial(along, steps=item) for item in steps] + self.left[2:]
            at = lax.rem(lax.axis_index("rows") // 4, 4)
            self.inner = (at == 1) | (at == 2)
            self.until_out = 3
        self.near = self.left.pop(0)(self.own)
        self.order.mark(self.own)

    def spread(self):
        own = self.order.tie(self.own)
        if self.inner is not None:
            self.until_out -= 1
        if self.inner is not None and self.until_out == 0:
            self.own = jnp.where(self.inner, own, self.near)
        else:
            self.own = add_low(own, self.near)
        self.near = self.left.pop(0)(self.own) if self.left else swap(self.own, (2, 1))
        self.order.mark(self.own)

    def spread_all(self):
        while self.left:
            self.spread()
        self.spread()

    def widen(self):
        own, near = self.order.tie(self.own), self.near
        self.half = jnp.where(
            self.second_bit == 0, jnp.stack((own, near)), jnp.stack((near, own))
        )
        self.order.mark(self.half)
        self.near = swap(self.half, (1, 2))

    def parts(self):
        return self.half, self.near


class SmallSum:
    def __init__(self, order, values_in):
        self.order, self.own = order, values_in
        self.left = [(1, 2), (2, 1)] + spread_masks()
        self.near = near(values_in)

    def step(self):
        self.own = self.order.tie(self.own) + self.near
        self.order.mark(self.own)
        if self.left:
            self.near = swap(self.own, self.left.pop(0))
            return True
        return False

    def rest(self):
        while self.step():
            pass
        return self.own


def body(
    hidden_in,
    teacher,
    segment_ids,
    valid_mask,
    w_query,
    b_query,
    w_key,
    w_value,
    b_value,
    w_attn_out,
    b_attn_out,
    gain_one,
    shift_one,
    w_up,
    b_up,
    w_down,
    b_down,
    gain_two,
    shift_two,
    head_alpha,
    mha_alpha,
    unit_alpha,
    ffn_alpha,
    hidden_alpha,
    head_noise,
    mha_noise,
    unit_noise,
    ffn_noise,
    hidden_noise,
    lagrange,
):
    model, width = w_query.shape
    units = w_up.shape[1]
    heads = width // HD
    pairs = model // LANES
    tokens = hidden_in.shape[0] // 2
    pack = Pack(width, units)
    order = Order()
    core = lax.axis_index("hid")
    row = lax.axis_index("rows")
    core_at = jnp.reshape(core, (1,)).astype(jnp.int32)
    low_bit, high_bit = row & 1, (row >> 1) & 1
    first_bit = jnp.where(core == 0, low_bit, high_bit).astype(jnp.int32)
    second_bit = jnp.where(core == 0, high_bit, low_bit).astype(jnp.int32)

    packed = (
        (b_query, pack.b_query, 0),
        (b_value, pack.b_value, 0),
        (b_attn_out, pack.b_attn_out, 0),
        (gain_one, pack.gain_one, 0),
        (shift_one, pack.shift_one, 0),
        (b_down, pack.b_down, 0),
        (gain_two, pack.gain_two, 0),
        (shift_two, pack.shift_two, 0),
        (hidden_alpha, pack.hidden_alpha, 0),
        (hidden_noise, pack.hidden_noise, 0),
        (b_up, pack.b_up, 0),
        (unit_alpha, pack.unit_alpha, 0),
        (unit_noise, pack.unit_noise, 0),
        (head_alpha, pack.head_alpha, 0),
        (head_noise, pack.head_noise, 0),
        (mha_alpha, pack.scalars, 0),
        (mha_noise, pack.scalars, 1),
        (ffn_alpha, pack.scalars, 2),
        (ffn_noise, pack.scalars, 3),
        (lagrange, pack.scalars, 4),
    )
    pack_own = call(
        order,
        partial(pack_kernel, pack, [item[1:] for item in packed]),
        (),
        [full(item[0].shape) for item in packed],
        full((1, pack.total)),
        shaped((1, pack.total), f32),
        [],
        (0.001, 0.1, 0),
        tuple(item[0] for item in packed),
    )
    x_peer = near(hidden_in)
    pack_peer = near(pack_own)
    wq_peer, wk_peer, wv_peer = near(w_query), near(w_key), near(w_value)
    wa_peer = near(w_attn_out)
    first_peers = (x_peer, pack_peer, wq_peer, wk_peer, wv_peer, wa_peer)
    *first_peers, up_sent, down_sent, teacher_sent = lax.optimization_barrier(
        (*first_peers, w_up, w_down, teacher)
    )
    x_peer, pack_peer, wq_peer, wk_peer, wv_peer, wa_peer = first_peers
    up_peer, down_peer, teacher_peer = near(up_sent), near(down_sent), near(teacher_sent)
    segments = segment_ids.reshape(-1, LANES)
    valid = valid_mask.reshape(-1, LANES)
    packs = [full((1, pack.total))] * 2
    pair_early, pair_late = sides(pairs // 2)
    token_low = shaped((tokens, model), bf16)
    token_wide = shaped((tokens, model), f32)
    token_half = shaped((tokens, width), bf16)

    (
        weights,
        query,
        key,
        value,
        context,
        gated_own,
        gated_peer,
        stats,
        biased,
        normed,
        hidden,
    ) = call(
        order,
        partial(attend_kernel, pack),
        (pairs,),
        [one_number()]
        + [anywhere()] * 2
        + [pair_early((model, LANES), 1)] * 3
        + [pair_late((model, LANES), 1)] * 3
        + [pair_early((LANES, model), 0), pair_late((LANES, model), 0)]
        + packs
        + [full(segments.shape)] * 2,
        [pl.BlockSpec((2, BLOCK, BLOCK), lambda i: (i, 0, 0))]
        + [every((tokens, LANES), 1)] * 4
        + [pair_early((tokens, LANES), 1), pair_late((tokens, LANES), 1)]
        + [full((tokens, LANES))]
        + [full((tokens, model))] * 3,
        [
            shaped((2 * pairs, BLOCK, BLOCK), bf16),
            token_low,
            token_low,
            token_low,
            token_low,
            token_half,
            token_half,
            shaped((tokens, LANES), f32),
            token_wide,
            token_wide,
            token_low,
        ],
        [
            pltpu.VMEM((tokens, model), bf16),
            pltpu.VMEM((BLOCK, BLOCK), f32),
            pltpu.VMEM((1, model), f32),
            pltpu.VMEM((model, 3 * LANES), bf16),
            pltpu.VMEM((LANES, model), bf16),
            pltpu.VMEM((8, LANES), f32),
            pltpu.VMEM((tokens, model), f32),
            pltpu.SemaphoreType.DMA((2,)),
        ],
        (4.0, 20, 3),
        (
            core_at,
            hidden_in,
            x_peer,
            w_query,
            w_key,
            w_value,
            wq_peer,
            wk_peer,
            wv_peer,
            w_attn_out,
            wa_peer,
            pack_own,
            pack_peer,
            segments,
            valid,
        ),
    )
    hidden_near = near(hidden)
    gated_near = near(gated_peer)

    tiles = units // TILE
    early, late = sides(tiles)

    (
        mixed_own,
        mixed_peer,
        active,
        slope,
        output_own,
        output_peer,
        grad_resid_two,
        grad_ffn,
        sums_two,
    ) = call(
        order,
        partial(ffn_forward_kernel, pack),
        (2 * tiles,),
        [one_number(), full((tokens, model)), anywhere()]
        + [early((model, TILE), 1), late((model, TILE), 1)]
        + [early((TILE, model), 0), late((TILE, model), 0)]
        + packs
        + [anywhere()] * 2
        + [full(valid.shape)],
        [early((tokens, TILE), 1), late((tokens, TILE), 1)]
        + [every((tokens, TILE), 1)] * 2
        + [full((tokens, width))] * 2
        + [full((tokens, model))] * 2
        + [full((4, model))],
        [
            shaped((tokens, units), bf16),
            shaped((tokens, units), bf16),
            shaped((tokens, 2 * units), bf16),
            shaped((tokens, 2 * units), bf16),
            token_half,
            token_half,
            token_wide,
            token_low,
            shaped((4, model), f32),
        ],
        [
            pltpu.VMEM((tokens, model), f32),
            pltpu.VMEM((tokens, model), f32),
            pltpu.VMEM((tokens, model), bf16),
            pltpu.SemaphoreType.DMA((3,)),
        ],
        (5.0, 25, 3),
        (
            core_at,
            hidden,
            normed,
            w_up,
            up_peer,
            w_down,
            down_peer,
            pack_own,
            pack_peer,
            teacher,
            teacher_peer,
            valid,
        ),
    )
    mixed_near = near(mixed_peer)
    grad_ffn_near = near(grad_ffn)
    output_near = near(output_peer)

    grad_pre_own, grad_pre_peer, unit_sums = call(
        order,
        partial(ffn_pre_kernel, pack),
        (2 * tiles,),
        [one_number(), full((tokens, model))]
        + [every((tokens, TILE), 1)] * 2
        + [early((TILE, model), 0), late((TILE, model), 0)],
        [early((tokens, TILE), 1), late((tokens, TILE), 1), full((2, 2 * units))],
        [
            shaped((tokens, units), bf16),
            shaped((tokens, units), bf16),
            shaped((2, 2 * units), f32),
        ],
        [],
        (50, 300, 0),
        (core_at, grad_ffn, active, slope, w_down, down_peer),
    )
    grad_pre_near = near(grad_pre_peer)

    bit_at = jnp.reshape(first_bit, (1,))

    def at_half(i, steps, bit):
        return jnp.where(i < steps, 1 - bit[0], bit[0])

    def sent_then_kept(shape, steps, dim):
        return [
            pl.BlockSpec(
                shape,
                lambda i, t, at=at: tuple(at(i) if d == dim else 0 for d in range(2)),
            )
            for at in (
                lambda i: jnp.minimum(i, steps - 1),
                lambda i: jnp.maximum(i - steps, 0),
            )
        ]

    half_units = units // 2
    step_units = half_units // 2
    by_units = pl.BlockSpec(
        (tokens, step_units), lambda i, t: (0, at_half(i, 2, t) * 2 + lax.rem(i, 2))
    )
    down_sent, down_kept = call_by_half(
        order,
        down_grad_kernel,
        (4,),
        [by_units, by_units] + [full((tokens, model))] * 2,
        sent_then_kept((step_units, model), 2, 0),
        [shaped((half_units, model), bf16)] * 2,
        (48, 180),
        bit_at,
        (mixed_own, mixed_near, grad_ffn, grad_ffn_near),
    )
    down_sent, down_kept = (
        item.reshape(2, half_units // 2, model) for item in (down_sent, down_kept)
    )
    down_chunk = RowSum(order, down_sent, first_bit, second_bit)

    up_rows = width + width // 4
    by_features = pl.BlockSpec((tokens, width), lambda i, t: (0, at_half(i, 2, t)))
    by_units = pl.BlockSpec((tokens, half_units), lambda i, t: (0, lax.rem(i, 2)))
    up_sent, up_kept = call_by_half(
        order,
        down_grad_kernel,
        (4,),
        [by_features, by_features, by_units, by_units],
        sent_then_kept((width, half_units), 2, 1),
        [shaped((width, units), bf16)] * 2,
        (2.4, 12),
        bit_at,
        (hidden, hidden_near, grad_pre_own, grad_pre_near),
    )
    up_chunk = RowSum(order, up_sent, first_bit, second_bit)

    grad_resid_one, grad_attn, sums_one = call(
        order,
        partial(ffn_backward_kernel, pack),
        (2 * tiles,),
        [one_number()]
        + [early((tokens, TILE), 1), late((tokens, TILE), 1)]
        + [anywhere()] * 3
        + [full((tokens, LANES))]
        + [early((model, TILE), 1), late((model, TILE), 1)]
        + packs,
        [full((tokens, model))] * 2 + [full((4, model))],
        [token_wide, token_low, shaped((4, model), f32)],
        [pltpu.VMEM((tokens, model), f32)] * 4 + [pltpu.SemaphoreType.DMA((3,))],
        (2.5, 15, 0),
        (
            core_at,
            grad_pre_own,
            grad_pre_peer,
            grad_resid_two,
            normed,
            biased,
            stats,
            w_up,
            up_peer,
            pack_own,
            pack_peer,
        ),
    )
    grad_attn_near = near(grad_attn)
    own_pairs = pairs // 2

    def attend_back(side_is_own, wa_ref):
        first = 0 if side_is_own else own_pairs
        return call(
            order,
            partial(attend_back_kernel, pack, side_is_own),
            (own_pairs,),
            [one_number(), pl.BlockSpec((2, BLOCK, BLOCK), lambda i: (i + first, 0, 0))]
            + [pl.BlockSpec((tokens, LANES), lambda i: (0, i + first))] * 4
            + [full((tokens, LANES)), full((tokens, model))]
            + [pl.BlockSpec((LANES, model), lambda i: (i, 0))]
            + packs,
            [full((tokens, 3 * width)), full((3, width))],
            [shaped((tokens, 3 * width), bf16), shaped((3, width), f32)],
            [pltpu.VMEM((1, model), f32)],
            (2.0, 10, 0),
            (
                core_at,
                weights,
                query,
                key,
                value,
                context,
                stats,
                grad_attn,
                wa_ref,
                pack_own,
                pack_peer,
            ),
        )

    grad_peer, sums_peer = attend_back(False, wa_peer)
    grad_near = near(grad_peer)
    down_chunk.halve(down_kept)
    by_columns = pl.BlockSpec((tokens, width), lambda i, t: (0, at_half(i, 1, t)))
    attn_sent, attn_kept = call_by_half(
        order,
        attn_out_grad_kernel,
        (2,),
        [full((tokens, width))] * 2 + [by_columns] * 2,
        [full((width // 4, units))] * 2,
        [shaped((width // 4, units), bf16)] * 2,
        (0.6, 3),
        bit_at,
        (gated_own, gated_near, grad_attn, grad_attn_near),
    )
    attn_near = swap(attn_sent, (1, 2))
    grad_own, sums_own = attend_back(True, w_attn_out)
    up_chunk.halve_with(up_kept, attn_kept, attn_near)
    down_chunk.quarter(path=True)
    sums_attn = jnp.where(
        core == 0,
        jnp.concatenate((sums_own, sums_peer), axis=1),
        jnp.concatenate((sums_peer, sums_own), axis=1),
    )

    def attend_half(half):
        out = call(
            order,
            attend_grad_kernel,
            (),
            [one_number()] * 2 + [anywhere()] * 2 + [full((tokens, 3 * width))] * 2,
            full((width, 3 * width)),
            shaped((width, 3 * width), bf16),
            [pltpu.VMEM(hidden_in.shape, bf16), pltpu.SemaphoreType.DMA],
            (24, 100, 0),
            (jnp.reshape(half, (1,)), core_at, hidden_in, x_peer, grad_own, grad_near),
        )
        return out.reshape(2, width // 2, 3 * width)

    attend_sent = attend_half(1 - first_bit)
    attend_chunk = RowSum(order, attend_sent, first_bit, second_bit)
    up_chunk.quarter()
    down_chunk.spread()
    small = SmallSum(
        order,
        jnp.concatenate((sums_two, sums_one, sums_attn, unit_sums.reshape(-1, model)), axis=0),
    )
    attend_kept = attend_half(first_bit)
    attend_chunk.halve(attend_kept)
    small.step()

    input_own, input_peer = call(
        order,
        partial(input_grad_kernel, width),
        (),
        [one_number(), full((tokens, model))]
        + [full((tokens, 3 * width))] * 2
        + [full((model, width))] * 6,
        [full((tokens, width))] * 2,
        [shaped((tokens, width), f32)] * 2,
        [],
        (1.8, 8, 0),
        (
            core_at,
            grad_resid_one,
            grad_own,
            grad_peer,
            w_query,
            w_key,
            w_value,
            wq_peer,
            wk_peer,
            wv_peer,
        ),
    )
    input_near = near(input_peer)

    def by_token(own, other):
        own = order.tie(own)
        out = jnp.where(
            core == 0, jnp.concatenate((own, other), axis=0), jnp.concatenate((other, own), axis=0)
        )
        order.mark(out)
        return out

    up_chunk.spread()
    down_chunk.spread()
    attend_chunk.quarter()
    small.step()
    output = by_token(output_own, output_near)
    grad_input = by_token(input_own, input_near)
    up_chunk.spread()
    down_chunk.spread()
    attend_chunk.spread()
    small.step()
    up_chunk.widen()
    down_chunk.widen()
    attend_chunk.spread()
    small.step()
    attend_chunk.widen()
    small_sums = small.rest()
    sizes = (width,) * 5 + (units,) + (width,) * 3 + (heads, 1, units, 1, width)
    sizes = sizes + (heads, 1, units, 1, width, 1, 1)
    finished = call(
        order,
        partial(finish_kernel, pack),
        (),
        [one_number(), full(small_sums.shape)] + packs,
        [full((size,)) for size in sizes],
        [shaped((size,), f32) for size in sizes],
        [],
        (0.01, 0.3, 0.1),
        (core_at, small_sums, pack_own, pack_peer),
    )

    def place(pieces):
        _, height, across = pieces[0].shape

        def block(at):
            return pl.BlockSpec((1, height, across), at)

        out = call_by_half(
            order,
            place_kernel,
            (4,),
            [
                block(lambda i, t: (jnp.minimum(i, 1), 0, 0)),
                block(lambda i, t: (jnp.maximum(i - 2, 0), 0, 0)),
            ],
            block(lambda i, t: (2 * lax.rem(t[0] + i // 2, 2) + lax.rem(i, 2), 0, 0)),
            shaped((4, height, across), f32),
            (0.001, 7),
            bit_at,
            pieces,
        )
        return out.reshape(4 * height, across)

    def by_half(pieces):
        return tuple(piece.reshape(-1, piece.shape[-1]) for piece in pieces)

    def own_half(shape, dim):
        return pl.BlockSpec(
            shape, lambda i, t: tuple(lax.rem(t[0] + i, 2) if d == dim else 0 for d in range(2))
        )

    sum_up, sum_attn = call_by_half(
        order,
        place_up_kernel,
        (2,),
        [full((up_rows, units))] * 2,
        [own_half((width, units), 0), own_half((width, width), 1)],
        [shaped((model, units), f32), shaped((width, model), f32)],
        (0.001, 10),
        bit_at,
        by_half(up_chunk.parts()),
    )
    sum_down = place(down_chunk.parts())
    sum_query, sum_key, sum_value = call_by_half(
        order,
        place_attend_kernel,
        (2,),
        [full((width, 3 * width))] * 2,
        [own_half((width, width), 0)] * 3,
        [shaped((model, width), f32)] * 3,
        (0.001, 7),
        bit_at,
        by_half(attend_chunk.parts()),
    )
    return (
        output,
        grad_input,
        sum_query,
        finished[0],
        sum_key,
        sum_value,
        finished[1],
        sum_attn,
        finished[2],
        finished[3],
        finished[4],
        sum_up,
        finished[5],
        sum_down,
        *finished[6:],
    )


def solution(mesh):
    in_specs = (
        P("rows", "hid"),
        P("rows", "hid"),
        P("rows"),
        P("rows"),
        P(None, "hid"),
        P("hid"),
        P(None, "hid"),
        P(None, "hid"),
        P("hid"),
        P("hid", None),
        P("hid"),
        P("hid"),
        P("hid"),
        P(None, "hid"),
        P("hid"),
        P("hid", None),
        P("hid"),
        P("hid"),
        P("hid"),
        P("hid"),
        P(),
        P("hid"),
        P(),
        P("hid"),
        P("hid"),
        P(),
        P("hid"),
        P(),
        P("hid"),
        P(),
    )
    out_specs = (
        P("rows", "hid"),
        P("rows", "hid"),
        P(None, "hid"),
        P("hid"),
        P(None, "hid"),
        P(None, "hid"),
        P("hid"),
        P("hid", None),
        P("hid"),
        P("hid"),
        P("hid"),
        P(None, "hid"),
        P("hid"),
        P("hid", None),
        P("hid"),
        P("hid"),
        P("hid"),
        P("hid"),
        P(),
        P("hid"),
        P(),
        P("hid"),
        P("hid"),
        P(),
        P("hid"),
        P(),
        P("hid"),
        P(),
        P(),
    )
    return jax.shard_map(body, mesh=mesh, in_specs=in_specs, out_specs=out_specs, check_vma=False)
```

time: 355 us -> 266 us (0.75); the launches traced: 348 us -> 265 us
  waiting for transfers between devices: 126 us -> 72.5 us
  local copies, waits for them, and re-layouts: 17.3 us -> 1.26 us
  other arithmetic: 36 us -> 24.1 us
  starting transfers between devices: 42.8 us -> 39 us
    ppermute x22 -> x21, waiting for transfers between devices: 117 us -> 50.6 us  [swap(): return lax.ppermute(values_in, ('rows', 'hid'), swap_pairs(core_masks))]
    ppermute x0 -> x3, waiting for transfers between devices: none -> 18.2 us  [along(): return lax.ppermute(values_in, ('rows', 'hid'), pairs)]
    pallas_call x13 -> x0, other arithmetic: 16.6 us -> none  [call(): pl.pallas_call(kernel, grid=grid, in_specs=in_specs, out_specs=out_specs,...]
    unnamed x73 -> x34, local copies, waits for them, and re-layouts: 16.5 us -> 1.21 us
    ppermute x22 -> x21, starting transfers between devices: 38.2 us -> 26.7 us  [swap(): return lax.ppermute(values_in, ('rows', 'hid'), swap_pairs(core_masks))]
    ppermute x0 -> x3, starting transfers between devices: none -> 7.19 us  [along(): return lax.ppermute(values_in, ('rows', 'hid'), pairs)]
    convert_element_type x12 -> x13, other arithmetic: 9.04 us -> 16 us  [to_low(): return values_in.astype(bf16)]
    ppermute x19, waiting for transfers between devices: 9.16 us -> 3.72 us  [near(): return lax.ppermute(values_in, 'hid', [(0, 1), (1, 0)])]
  transfers between devices with their start and end apart: 41 -> 43, of which waited for: 20 -> 15; matrix products, arithmetic and copies ran while one was open for 14% -> 9% of each run, Pallas kernels for 24% -> 46%
where the time goes in v2:
time: 266 us; the launch traced here: 265 us
  Pallas kernels  124 us (47%)
  waiting for transfers between devices  72.5 us (27%)
  starting transfers between devices  39 us (15%)
  other arithmetic  24.1 us (9%)
  between operations  3.67 us (1%)
    pallas_call x11, Pallas kernels, call(): pl.pallas_call(kernel, grid=grid, in_specs=in_specs, out_specs=out_specs,...  94.3 us
    ppermute x21, waiting for transfers between devices, swap(): return lax.ppermute(values_in, ('rows', 'hid'), swap_pairs(core_masks))  50.6 us
    pallas_call x6, Pallas kernels, call_by_half(): pl.pallas_call(kernel, grid_spec=pltpu.PrefetchScalarGridSpec(num_scalar_...  29.9 us
    ppermute x21, starting transfers between devices, swap(): return lax.ppermute(values_in, ('rows', 'hid'), swap_pairs(core_masks))  26.7 us
    ppermute x3, waiting for transfers between devices, along(): return lax.ppermute(values_in, ('rows', 'hid'), pairs)  18.2 us
    convert_element_type x13, other arithmetic, to_low(): return values_in.astype(bf16)  16 us
    ppermute x3, starting transfers between devices, along(): return lax.ppermute(values_in, ('rows', 'hid'), pairs)  7.19 us
  transfers between devices with their start and end apart: 43, of which 15 were waited for; matrix products, arithmetic and copies ran while one was open for 9% of the time, Pallas kernels for 46%

profile of v2, /device:TPU:0, one launch (start us, length us, event | category | flops | bytes accessed | tf_op | source)
XLA Modules:
  0.0 264.8 jit_solution(649322326030823318)
XLA Ops:
  3.8 1.5 shard_map.509.pack_own
  6.9 0.8 collective-permute-done.2.wq_peer
  7.7 0.8 collective-permute-done.3.wk_peer
  8.5 0.8 collective-permute-done.4.wv_peer
  9.4 0.8 collective-permute-done.5.wa_peer.wa_ref
  11.2 19.0 %shard_map.510 = (bf16[12,512,512]{2,1,0:T(8,128)(2,1)}, bf16[512,768]{1,0:T(8,128)(2,1)}, bf16[512,768]{1,0:T(8,128)(2,1)}, bf16[512,768]{1,0:T(8,128)(2,1)}, b...) custom-call(s32[1]{0:T(128)} %bitcast.core_ref, ...), custom_call_target="tpu_custom_call" | custom-call | flops 4000000000 | bytes 20000000 | tf_op jit(solution)/shard_map/pallas_call | solution.py:932
  30.5 16.6 %shard_map.511 = (bf16[512,1536]{1,0:T(8,128)(2,1)}, bf16[512,1536]{1,0:T(8,128)(2,1)}, bf16[512,3072]{1,0:T(8,128)(2,1)}, bf16[512,3072]{1,0:T(8,128)(2,1)}, bf...) custom-call(s32[1]{0:T(128)} %bitcast.core_ref, ...), custom_call_target="tpu_custom_call" | custom-call | flops 5000000000 | bytes 25000000 | tf_op jit(solution)/shard_map/pallas_call | solution.py:932
  47.7 9.9 %shard_map.512 = (bf16[512,1536]{1,0:T(8,128)(2,1)}, bf16[512,1536]{1,0:T(8,128)(2,1)}, f32[2,3072]{1,0:T(2,128)}) custom-call(s32[1]{0:T(128)} %bitcast.core_ref, bf16[512,768]{1,0:T(8,128)(2,1)} %get-tuple-element.158.grad_ffn.grad, bf16[512,3072]{1,0:T(8,128)(2,1)} %get-tuple-element.159.active, bf16[512,3072]{1,0:T(8,128)(2,1)} %get-tuple-element.160.slope, ...), custom_call_target="tpu_custom_call" | custom-call | flops 49999998976 | bytes 300000000 | tf_op jit(solution)/shard_map/pallas_call | solution.py:932
  57.9 6.7 %shard_map.513 = (bf16[768,768]{1,0:T(8,128)(2,1)}, bf16[768,768]{1,0:T(8,128)(2,1)}) custom-call(s32[1]{0:T(128)} %bitcast.3.bit_ref.half_ref, bf16[512,1536]{1,0:T(8,128)(2,1)} %get-tuple-element.163.mixed, bf16[512,1536]{1,0:T(8,128)(2,1)} %collective-permute-done.9.mixed_near, bf16[512,768]{1,0:T(8,128)(2,1)} %get-tuple-element.158.grad_ffn.grad, ...), custom_call_target="tpu_custom_call" | custom-call | flops 48000000000 | bytes 180000000 | tf_op jit(solution)/shard_map/pallas_call | solution.py:951
  64.5 2.7 %collective-permute-start.13 = (bf16[2,384,768]{2,1,0:T(8,128)(2,1)}, bf16[2,384,768]{2,1,0:T(8,128)(2,1)}, u32[]{:S(2)}, u32[]{:S(2)}) collective-permute-start(bf16[2,384,768]{2,1,0:T(8,128)(2,1)} %bitcast.38), channel_id=1, source_target_pairs={{0,2},{1,5},{2,0},{3,7},{4,6},{5,1},{6,4},{7,3},{8,10},{9,13},{10,... | collective-permute-start | bytes 3538952 | tf_op jit(solution)/shard_map/ppermute | solution.py:978
  67.2 1.1 copy-done.16
  68.4 7.1 %shard_map.514 = (bf16[384,1536]{1,0:T(8,128)(2,1)}, bf16[384,1536]{1,0:T(8,128)(2,1)}) custom-call(s32[1]{0:T(128)} %bitcast.3.bit_ref.half_ref, bf16[512,768]{1,0:T(8,128)(2,1)} %get-tuple-element.149.hidden.mixed, bf16[512,768]{1,0:T(8,128)(2,1)} %collective-permute-done.11.mixed_near, bf16[512,1536]{1,0:T(8,128)(2,1)} %get-tuple-element.167.grad.grad_pre_own, ...), custom_call_target="tpu_custom_call" | custom-call | flops 2400000000 | bytes 12000000 | tf_op jit(solution)/shard_map/pallas_call | solution.py:951
  75.5 10.7 %shard_map.515 = (f32[512,768]{1,0:T(8,128)}, bf16[512,768]{1,0:T(8,128)(2,1)}, f32[4,768]{1,0:T(4,128)}) custom-call(s32[1]{0:T(128)} %bitcast.core_ref, bf16[512,1536]{1,0:T(8,128)(2,1)} %get-tuple-element.167.grad.grad_pre_own, bf16[512,1536]{1,0:T(8,128)(2,1)} %get-tuple-element.168.grad_pre_peer, f32[512,768]{1,0:T(8,128)} %get-tuple-element.171.grad_resid_two, ...), custom_call_target="tpu_custom_call" | custom-call | flops 2500000000 | bytes 15000000 | tf_op jit(solution)/shard_map/pallas_call | solution.py:932
  87.0 9.0 %shard_map.516 = (bf16[512,1152]{1,0:T(8,128)(2,1)}, f32[3,384]{1,0:T(4,128)}) custom-call(s32[1]{0:T(128)} %bitcast.core_ref, bf16[12,512,512]{2,1,0:T(8,128)(2,1)} %get-tuple-element.176.weights, bf16[512,768]{1,0:T(8,128)(2,1)} %get-tuple-element.177.query_ref, bf16[512,768]{1,0:T(8,128)(2,1)} %get-tuple-element.178.key_ref, ...), custom_call_target="tpu_custom_call" | custom-call | flops 2000000000 | bytes 10000000 | tf_op jit(solution)/shard_map/pallas_call | solution.py:932
  96.5 2.3 fusion.1
  98.8 2.0 collective-permute-start.18
  100.9 3.5 %shard_map.517 = (bf16[96,1536]{1,0:T(8,128)(2,1)}, bf16[96,1536]{1,0:T(8,128)(2,1)}) custom-call(s32[1]{0:T(128)} %bitcast.3.bit_ref.half_ref, bf16[512,384]{1,0:T(8,128)(2,1)} %get-tuple-element.186.gated, bf16[512,384]{1,0:T(8,128)(2,1)} %collective-permute-done.14.gated_near, bf16[512,768]{1,0:T(8,128)(2,1)} %get-tuple-element.181.grad_attn.grad, ...), custom_call_target="tpu_custom_call" | custom-call | flops 600000000 | bytes 3000000 | tf_op jit(solution)/shard_map/pallas_call | solution.py:951
  104.3 1.5 collective-permute-start.17
  105.8 8.9 %shard_map.518 = (bf16[512,1152]{1,0:T(8,128)(2,1)}, f32[3,384]{1,0:T(4,128)}) custom-call(s32[1]{0:T(128)} %bitcast.core_ref, bf16[12,512,512]{2,1,0:T(8,128)(2,1)} %get-tuple-element.176.weights, bf16[512,768]{1,0:T(8,128)(2,1)} %get-tuple-element.177.query_ref, bf16[512,768]{1,0:T(8,128)(2,1)} %get-tuple-element.178.key_ref, ...), custom_call_target="tpu_custom_call" | custom-call | flops 2000000000 | bytes 10000000 | tf_op jit(solution)/shard_map/pallas_call | solution.py:932
  114.8 1.6 add_convert_fusion
  116.6 1.0 add_convert_fusion.14
  117.7 1.1 broadcast_select_fusion
  119.3 2.0 add_convert_fusion.6
  121.3 4.3 %collective-permute-start.21 = (bf16[384,768]{1,0:T(8,128)(2,1)}, bf16[384,768]{1,0:T(8,128)(2,1)}, u32[]{:S(2)}, u32[]{:S(2)}) collective-permute-start(bf16[384,768]{1,0:T(8,128)(2,1)} %add_convert_fusion.6), channel_id=1, source_target_pairs={{0,8},{1,9},{2,10},{3,11},{4,12},{5,13},{6,14},{7,15},{24,16},{25,... | collective-permute-start | bytes 1769480 | tf_op jit(solution)/shard_map/ppermute | solution.py:989
  125.6 4.9 %shard_map.519 = bf16[384,1152]{1,0:T(8,128)(2,1)} custom-call(s32[1]{0:T(128)} %bitcast.8.half_ref, s32[1]{0:T(128)} %bitcast.core_ref, bf16[1024,384]{1,0:T(8,128)(2,1)} %x_own.5, bf16[1024,384]{1,0:T(8,128)(2,1)} %collective-permute-done.x_peer, bf16[512,1152]{1,0:T(8,128)(2,1)} %get-tuple-element.197.grad.grad_own, ...), custom_call_target="tpu_custom_call" | custom-call | flops 24000000000 | bytes 100000000 | tf_op jit(solution)/shard_map/pallas_call | solution.py:932
  130.5 0.6 collective-permute-start.22
  131.1 1.3 add_convert_fusion.3
  132.4 1.1 collective-permute-start.24
  133.5 5.3 %collective-permute-done.21 = bf16[384,768]{1,0:T(8,128)(2,1)} collective-permute-done((bf16[384,768]{1,0:T(8,128)(2,1)}, bf16[384,768]{1,0:T(8,128)(2,1)}, u32[]{:S(2)}, u32[]{:S(2)}) %collective-permute-start.21) | collective-permute-done | bytes 589856 | tf_op jit(solution)/shard_map/ppermute | solution.py:989
  138.8 1.4 add_convert_fusion.5
  140.1 1.5 collective-permute-start.25
  141.6 4.9 %shard_map.520 = bf16[384,1152]{1,0:T(8,128)(2,1)} custom-call(s32[1]{0:T(128)} %bitcast.3.bit_ref.half_ref, s32[1]{0:T(128)} %bitcast.core_ref, bf16[1024,384]{1,0:T(8,128)(2,1)} %x_own.5, bf16[1024,384]{1,0:T(8,128)(2,1)} %collective-permute-done.x_peer, bf16[512,1152]{1,0:T(8,128)(2,1)} %get-tuple-element.197.grad.grad_own, ...), custom_call_target="tpu_custom_call" | custom-call | flops 24000000000 | bytes 100000000 | tf_op jit(solution)/shard_map/pallas_call | solution.py:932
  146.5 2.4 fusion.3
  148.9 1.6 collective-permute-start.26
  151.1 6.9 %shard_map.521 = (f32[512,384]{1,0:T(8,128)}, f32[512,384]{1,0:T(8,128)}) custom-call(s32[1]{0:T(128)} %bitcast.core_ref, f32[512,768]{1,0:T(8,128)} %get-tuple-element.205.grad_resid, bf16[512,1152]{1,0:T(8,128)(2,1)} %get-tuple-element.197.grad.grad_own, bf16[512,1152]{1,0:T(8,128)(2,1)} %get-tuple-element.198.grad_peer, bf16[768,384]{1,0:T(8,128)(2,1)} %wq_own.3, ...), custom_call_target="tpu_custom_call" | custom-call | flops 1800000000 | bytes 8000000 | tf_op jit(solution)/shard_map/pallas_call | solution.py:932
  158.0 1.3 add_convert_fusion.2
  159.3 2.5 collective-permute-start.30
  161.9 1.2 add_convert_fusion.4
  163.1 1.4 collective-permute-start.31
  164.5 1.1 add_convert_fusion.11
  165.7 4.0 %collective-permute-start.32 = (bf16[192,1152]{1,0:T(8,128)(2,1)S(1)}, bf16[192,1152]{1,0:T(8,128)(2,1)S(1)}, u32[]{:S(2)}, u32[]{:S(2)}) collective-permute-start(bf16[192,1152]{1,0:T(8,128)(2,1)S(1)} %add_convert_fusion.11), channel_id=1, source_target_pairs={{0,8},{1,25},{2,10},{3,27},{4,12},{5,29},{6,14},{7,31},{8,0},{9,17... | collective-permute-start | bytes 1327112 | tf_op jit(solution)/shard_map/ppermute | solution.py:978
  170.3 2.3 maximum_select_fusion.4
  172.6 1.2 maximum_select_fusion
  173.8 4.4 %collective-permute-done.30 = bf16[240,1536]{1,0:T(8,128)(2,1)S(1)} collective-permute-done((bf16[240,1536]{1,0:T(8,128)(2,1)S(1)}, bf16[240,1536]{1,0:T(8,128)(2,1)S(1)}, u32[]{:S(2)}, u32[]{:S(2)}) %collective-permute-start.30) | collective-permute-done | bytes 737312 | tf_op jit(solution)/shard_map/ppermute | solution.py:978
  178.6 13.0 %collective-permute-done.31 = bf16[384,768]{1,0:T(8,128)(2,1)S(1)} collective-permute-done((bf16[384,768]{1,0:T(8,128)(2,1)S(1)}, bf16[384,768]{1,0:T(8,128)(2,1)S(1)}, u32[]{:S(2)}, u32[]{:S(2)}) %collective-permute-start.31) | collective-permute-done | bytes 589856 | tf_op jit(solution)/shard_map/ppermute | solution.py:989
  192.0 9.0 %collective-permute-done.32 = bf16[192,1152]{1,0:T(8,128)(2,1)S(1)} collective-permute-done((bf16[192,1152]{1,0:T(8,128)(2,1)S(1)}, bf16[192,1152]{1,0:T(8,128)(2,1)S(1)}, u32[]{:S(2)}, u32[]{:S(2)}) %collective-permute-start.32) | collective-permute-done | bytes 442400 | tf_op jit(solution)/shard_map/ppermute | solution.py:978
  201.1 2.2 collective-permute-start.36
  203.7 1.4 maximum_select_fusion.2.half
  205.1 10.1 %collective-permute-done.36 = bf16[192,1152]{1,0:T(8,128)(2,1)S(1)} collective-permute-done((bf16[192,1152]{1,0:T(8,128)(2,1)S(1)}, bf16[192,1152]{1,0:T(8,128)(2,1)S(1)}, u32[]{:S(2)}, u32[]{:S(2)}) %collective-permute-start.36) | collective-permute-done | bytes 442400 | tf_op jit(solution)/shard_map/ppermute | solution.py:978
  215.3 0.7 collective-permute-start.38
  216.1 1.8 collective-permute-start.40
  218.1 4.5 %collective-permute-done.37 = f32[19,768]{1,0:T(8,128)S(1)} collective-permute-done((f32[19,768]{1,0:T(8,128)S(1)}, f32[19,768]{1,0:T(8,128)S(1)}, u32[]{:S(2)}, u32[]{:S(2)}) %collective-permute-start.37) | collective-permute-done | bytes 58400 | tf_op jit(solution)/shard_map/ppermute | solution.py:978
  222.6 5.8 %collective-permute-done.38 = bf16[192,1152]{1,0:T(8,128)(2,1)S(1)} collective-permute-done((bf16[192,1152]{1,0:T(8,128)(2,1)S(1)}, bf16[192,1152]{1,0:T(8,128)(2,1)S(1)}, u32[]{:S(2)}, u32[]{:S(2)}) %collective-permute-start.38) | collective-permute-done | bytes 442400 | tf_op jit(solution)/shard_map/ppermute | solution.py:978
  228.4 1.1 maximum_select_fusion.3
  229.5 2.1 collective-permute-start.42
  231.6 1.2 collective-permute-start.39
  232.8 4.9 %collective-permute-done.39 = f32[19,768]{1,0:T(8,128)S(1)} collective-permute-done((f32[19,768]{1,0:T(8,128)S(1)}, f32[19,768]{1,0:T(8,128)S(1)}, u32[]{:S(2)}, u32[]{:S(2)}) %collective-permute-start.39) | collective-permute-done | bytes 58400 | tf_op jit(solution)/shard_map/ppermute | solution.py:978
  237.8 0.6 add.101.sums
  238.4 2.0 shard_map.522
  240.4 4.6 %shard_map.523 = (f32[768,1536]{1,0:T(8,128)}, f32[384,768]{1,0:T(8,128)}) custom-call(s32[1]{0:T(128)} %bitcast.3.bit_ref.half_ref, bf16[480,1536]{1,0:T(8,128)(2,1)} %bitcast.28, bf16[480,1536]{1,0:T(8,128)(2,1)} %bitcast.20.other), custom_call_target="tpu_custom_call" | custom-call | flops 1000000 | bytes 10000000 | tf_op jit(solution)/shard_map/pallas_call | solution.py:951
  245.0 7.0 %collective-permute-done.41.other = bf16[2,384,768]{2,1,0:T(8,128)(2,1)} collective-permute-done((bf16[2,384,768]{2,1,0:T(8,128)(2,1)}, bf16[2,384,768]{2,1,0:T(8,128)(2,1)}, u32[]{:S(2)}, u32[]{:S(2)}) %collective-permute-start.41) | collective-permute-done | bytes 1179680 | tf_op jit(solution)/shard_map/ppermute | solution.py:978
  252.0 4.7 %shard_map.524 = f32[4,384,768]{2,1,0:T(8,128)} custom-call(s32[1]{0:T(128)} %bitcast.3.bit_ref.half_ref, bf16[2,384,768]{2,1,0:T(8,128)(2,1)} %maximum_select_fusion.2.half, bf16[2,384,768]{2,1,0:T(8,128)(2,1)} %collective-permute-done.41.other), custom_call_target="tpu_custom_call" | custom-call | flops 1000000 | bytes 7000000 | tf_op jit(solution)/shard_map/pallas_call | solution.py:951
  256.7 4.8 %collective-permute-done.42 = bf16[2,192,1152]{2,1,0:T(8,128)(2,1)} collective-permute-done((bf16[2,192,1152]{2,1,0:T(8,128)(2,1)}, bf16[2,192,1152]{2,1,0:T(8,128)(2,1)}, u32[]{:S(2)}, u32[]{:S(2)}) %collective-permute-start.42) | collective-permute-done | bytes 884768 | tf_op jit(solution)/shard_map/ppermute | solution.py:978
  261.5 3.3 %shard_map.525 = (f32[768,384]{1,0:T(8,128)}, f32[768,384]{1,0:T(8,128)}, f32[768,384]{1,0:T(8,128)}) custom-call(s32[1]{0:T(128)} %bitcast.3.bit_ref.half_ref, bf16[384,1152]{1,0:T(8,128)(2,1)} %bitcast.21.half, bf16[384,1152]{1,0:T(8,128)(2,1)} %bitcast.22.other), custom_call_target="tpu_custom_call" | custom-call | flops 1000000 | bytes 7000000 | tf_op jit(solution)/shard_map/pallas_call | solution.py:951
  (102 shorter events, 8.9 us)
Async XLA Ops:
  0.7 9.5 %collective-permute-start = (bf16[1024,384]{1,0:T(8,128)(2,1)}, bf16[1024,384]{1,0:T(8,128)(2,1)}, u32[]{:S(2)}, u32[]{:S(2)}) collective-permute-start(bf16[1024,384]{1,0:T(8,128)(2,1)} %x_own.5), channel_id=1, source_target_pairs={{0,1},{1,0},{2,3},{3,2},{4,5},{5,4},{6,7},{7,6},{8,9},{9,8},{10,11... | collective-permute-start | bytes 2359304 | tf_op jit(solution)/shard_map/ppermute | solution.py:993
  5.3 1.4 collective-permute-start.1
  5.4 2.3 collective-permute-start.2
  5.8 2.7 %collective-permute-start.3 = (bf16[768,384]{1,0:T(8,128)(2,1)}, bf16[768,384]{1,0:T(8,128)(2,1)S(1)}, u32[]{:S(2)}, u32[]{:S(2)}) collective-permute-start(bf16[768,384]{1,0:T(8,128)(2,1)} %wk_own.3), channel_id=1, source_target_pairs={{0,1},{1,0},{2,3},{3,2},{4,5},{5,4},{6,7},{7,6},{8,9},{9,8},{10,11... | collective-permute-start | bytes 1769480 | tf_op jit(solution)/shard_map/ppermute | solution.py:993
  5.9 3.5 %collective-permute-start.4 = (bf16[768,384]{1,0:T(8,128)(2,1)}, bf16[768,384]{1,0:T(8,128)(2,1)S(1)}, u32[]{:S(2)}, u32[]{:S(2)}) collective-permute-start(bf16[768,384]{1,0:T(8,128)(2,1)} %wv_own.3), channel_id=1, source_target_pairs={{0,1},{1,0},{2,3},{3,2},{4,5},{5,4},{6,7},{7,6},{8,9},{9,8},{10,11... | collective-permute-start | bytes 1769480 | tf_op jit(solution)/shard_map/ppermute | solution.py:993
  6.7 4.4 %copy-start.8 = (f32[1,8832]{1,0:T(1,128)}, f32[1,8832]{1,0:T(1,128)S(1)}, u32[]{:S(2)}) copy-start(f32[1,8832]{1,0:T(1,128)S(1)} %collective-permute-done.1.pack_peer) | copy-start | bytes 105988
  6.7 3.5 %collective-permute-start.5 = (bf16[384,768]{1,0:T(8,128)(2,1)}, bf16[384,768]{1,0:T(8,128)(2,1)S(1)}, u32[]{:S(2)}, u32[]{:S(2)}) collective-permute-start(bf16[384,768]{1,0:T(8,128)(2,1)} %wa_ref.1), channel_id=1, source_target_pairs={{0,1},{1,0},{2,3},{3,2},{4,5},{5,4},{6,7},{7,6},{8,9},{9,8},{10,11... | collective-permute-start | bytes 1769480 | tf_op jit(solution)/shard_map/ppermute | solution.py:993
  7.7 3.5 %copy-start.5 = (bf16[768,384]{1,0:T(8,128)(2,1)}, bf16[768,384]{1,0:T(8,128)(2,1)S(1)}, u32[]{:S(2)}) copy-start(bf16[768,384]{1,0:T(8,128)(2,1)S(1)} %collective-permute-done.2.wq_peer) | copy-start | bytes 1769476
  8.5 2.7 %copy-start.6 = (bf16[768,384]{1,0:T(8,128)(2,1)}, bf16[768,384]{1,0:T(8,128)(2,1)S(1)}, u32[]{:S(2)}) copy-start(bf16[768,384]{1,0:T(8,128)(2,1)S(1)} %collective-permute-done.3.wk_peer) | copy-start | bytes 1769476
  9.4 0.8 copy-start.7
  10.2 1.0 copy-start.4
  10.2 20.3 %collective-permute-start.6 = (bf16[768,1536]{1,0:T(8,128)(2,1)}, bf16[768,1536]{1,0:T(8,128)(2,1)}, u32[]{:S(2)}, u32[]{:S(2)}) collective-permute-start(bf16[768,1536]{1,0:T(8,128)(2,1)} %up_own.3), channel_id=1, source_target_pairs={{0,1},{1,0},{2,3},{3,2},{4,5},{5,4},{6,7},{7,6},{8,9},{9,8},{10,11... | collective-permute-start | bytes 7077896 | tf_op jit(solution)/shard_map/ppermute | solution.py:993
  10.6 19.9 %collective-permute-start.7 = (bf16[1536,768]{1,0:T(8,128)(2,1)}, bf16[1536,768]{1,0:T(8,128)(2,1)}, u32[]{:S(2)}, u32[]{:S(2)}) collective-permute-start(bf16[1536,768]{1,0:T(8,128)(2,1)} %down_own.3), channel_id=1, source_target_pairs={{0,1},{1,0},{2,3},{3,2},{4,5},{5,4},{6,7},{7,6},{8,9},{9,8},{10,11... | collective-permute-start | bytes 7077896 | tf_op jit(solution)/shard_map/ppermute | solution.py:993
  10.8 19.8 %collective-permute-start.8 = (bf16[1024,384]{1,0:T(8,128)(2,1)}, bf16[1024,384]{1,0:T(8,128)(2,1)}, u32[]{:S(2)}, u32[]{:S(2)}) collective-permute-start(bf16[1024,384]{1,0:T(8,128)(2,1)} %teacher_own.1), channel_id=1, source_target_pairs={{0,1},{1,0},{2,3},{3,2},{4,5},{5,4},{6,7},{7,6},{8,9},{9,8},{10,11... | collective-permute-start | bytes 2359304 | tf_op jit(solution)/shard_map/ppermute | solution.py:993
  30.2 37.0 %collective-permute-start.11 = (bf16[512,768]{1,0:T(8,128)(2,1)}, bf16[512,768]{1,0:T(8,128)(2,1)}, u32[]{:S(2)}, u32[]{:S(2)}) collective-permute-start(bf16[512,768]{1,0:T(8,128)(2,1)} %get-tuple-element.149.hidden.mixed), channel_id=1, source_target_pairs={{0,1},{1,0},{2,3},{3,2},{4,5},{5,4},{6,7},{7,6},{8,9},{9,8},{10,11... | collective-permute-start | bytes 2359304 | tf_op jit(solution)/shard_map/ppermute | solution.py:993
  47.1 10.8 %collective-permute-start.9 = (bf16[512,1536]{1,0:T(8,128)(2,1)}, bf16[512,1536]{1,0:T(8,128)(2,1)}, u32[]{:S(2)}, u32[]{:S(2)}) collective-permute-start(bf16[512,1536]{1,0:T(8,128)(2,1)} %get-tuple-element.164), channel_id=1, source_target_pairs={{0,1},{1,0},{2,3},{3,2},{4,5},{5,4},{6,7},{7,6},{8,9},{9,8},{10,11... | collective-permute-start | bytes 4718600 | tf_op jit(solution)/shard_map/ppermute | solution.py:993
  47.4 10.4 %collective-permute-start.10 = (bf16[512,768]{1,0:T(8,128)(2,1)}, bf16[512,768]{1,0:T(8,128)(2,1)}, u32[]{:S(2)}, u32[]{:S(2)}) collective-permute-start(bf16[512,768]{1,0:T(8,128)(2,1)} %get-tuple-element.158.grad_ffn.grad), channel_id=1, source_target_pairs={{0,1},{1,0},{2,3},{3,2},{4,5},{5,4},{6,7},{7,6},{8,9},{9,8},{10,11... | collective-permute-start | bytes 2359304 | tf_op jit(solution)/shard_map/ppermute | solution.py:993
  57.5 9.7 %collective-permute-start.12 = (bf16[512,1536]{1,0:T(8,128)(2,1)}, bf16[512,1536]{1,0:T(8,128)(2,1)S(1)}, u32[]{:S(2)}, u32[]{:S(2)}) collective-permute-start(bf16[512,1536]{1,0:T(8,128)(2,1)} %get-tuple-element.168.grad_pre_peer), channel_id=1, source_target_pairs={{0,1},{1,0},{2,3},{3,2},{4,5},{5,4},{6,7},{7,6},{8,9},{9,8},{10,11... | collective-permute-start | bytes 4718600 | tf_op jit(solution)/shard_map/ppermute | solution.py:993
  64.5 31.5 %collective-permute-start.13 = (bf16[2,384,768]{2,1,0:T(8,128)(2,1)}, bf16[2,384,768]{2,1,0:T(8,128)(2,1)}, u32[]{:S(2)}, u32[]{:S(2)}) collective-permute-start(bf16[2,384,768]{2,1,0:T(8,128)(2,1)} %bitcast.38), channel_id=1, source_target_pairs={{0,2},{1,5},{2,0},{3,7},{4,6},{5,1},{6,4},{7,3},{8,10},{9,13},{10,... | collective-permute-start | bytes 3538952 | tf_op jit(solution)/shard_map/ppermute | solution.py:978
  67.2 1.1 copy-start.16
  75.5 39.3 %collective-permute-start.16 = (bf16[384,1536]{1,0:T(8,128)(2,1)}, bf16[384,1536]{1,0:T(8,128)(2,1)}, u32[]{:S(2)}, u32[]{:S(2)}) collective-permute-start(bf16[384,1536]{1,0:T(8,128)(2,1)} %get-tuple-element.192), channel_id=1, source_target_pairs={{0,2},{1,5},{2,0},{3,7},{4,6},{5,1},{6,4},{7,3},{8,10},{9,13},{10,... | collective-permute-start | bytes 3538952 | tf_op jit(solution)/shard_map/ppermute | solution.py:978
  75.5 11.3 %copy-start.11 = (f32[2,3072]{1,0:T(2,128)S(1)}, f32[2,3072]{1,0:T(2,128)}, u32[]{:S(2)}) copy-start(f32[2,3072]{1,0:T(2,128)} %get-tuple-element.161) | copy-start | bytes 73732
  86.2 14.6 %collective-permute-start.15 = (bf16[512,768]{1,0:T(8,128)(2,1)}, bf16[512,768]{1,0:T(8,128)(2,1)}, u32[]{:S(2)}, u32[]{:S(2)}) collective-permute-start(bf16[512,768]{1,0:T(8,128)(2,1)} %get-tuple-element.181.grad_attn.grad), channel_id=1, source_target_pairs={{0,1},{1,0},{2,3},{3,2},{4,5},{5,4},{6,7},{7,6},{8,9},{9,8},{10,11... | collective-permute-start | bytes 2359304 | tf_op jit(solution)/shard_map/ppermute | solution.py:993
  86.3 12.5 %collective-permute-start.14 = (bf16[512,384]{1,0:T(8,128)(2,1)}, bf16[512,384]{1,0:T(8,128)(2,1)}, u32[]{:S(2)}, u32[]{:S(2)}) collective-permute-start(bf16[512,384]{1,0:T(8,128)(2,1)} %get-tuple-element.187), channel_id=1, source_target_pairs={{0,1},{1,0},{2,3},{3,2},{4,5},{5,4},{6,7},{7,6},{8,9},{9,8},{10,11... | collective-permute-start | bytes 1179656 | tf_op jit(solution)/shard_map/ppermute | solution.py:993
  86.8 82.9 %collective-permute-start.28 = (bf16[512,384]{1,0:T(8,128)(2,1)}, bf16[512,384]{1,0:T(8,128)(2,1)}, u32[]{:S(2)}, u32[]{:S(2)}) collective-permute-start(bf16[512,384]{1,0:T(8,128)(2,1)} %get-tuple-element.212), channel_id=1, source_target_pairs={{0,1},{1,0},{2,3},{3,2},{4,5},{5,4},{6,7},{7,6},{8,9},{9,8},{10,11... | collective-permute-start | bytes 1179656 | tf_op jit(solution)/shard_map/ppermute | solution.py:993
  87.0 9.5 %copy-start.2 = (bf16[768,768]{1,0:T(8,128)(2,1)S(1)}, bf16[768,768]{1,0:T(8,128)(2,1)}, u32[]{:S(2)}) copy-start(bf16[768,768]{1,0:T(8,128)(2,1)} %get-tuple-element.165) | copy-start | bytes 3538948
  96.0 29.6 %collective-permute-start.19 = (bf16[512,1152]{1,0:T(8,128)(2,1)}, bf16[512,1152]{1,0:T(8,128)(2,1)}, u32[]{:S(2)}, u32[]{:S(2)}) collective-permute-start(bf16[512,1152]{1,0:T(8,128)(2,1)} %get-tuple-element.198.grad_peer), channel_id=1, source_target_pairs={{0,1},{1,0},{2,3},{3,2},{4,5},{5,4},{6,7},{7,6},{8,9},{9,8},{10,11... | collective-permute-start | bytes 3538952 | tf_op jit(solution)/shard_map/ppermute | solution.py:993
  98.8 20.5 %collective-permute-start.18 = (bf16[384,768]{1,0:T(8,128)(2,1)}, bf16[384,768]{1,0:T(8,128)(2,1)}, u32[]{:S(2)}, u32[]{:S(2)}) collective-permute-start(bf16[384,768]{1,0:T(8,128)(2,1)} %get-tuple-element.256), channel_id=1, source_target_pairs={{0,4},{1,3},{2,6},{3,1},{4,0},{5,7},{6,2},{7,5},{8,12},{9,11},{10,... | collective-permute-start | bytes 1769480 | tf_op jit(solution)/shard_map/ppermute | solution.py:978
  104.3 10.5 %copy-start.1 = (bf16[384,1536]{1,0:T(8,128)(2,1)S(1)}, bf16[384,1536]{1,0:T(8,128)(2,1)}, u32[]{:S(2)}) copy-start(bf16[384,1536]{1,0:T(8,128)(2,1)} %get-tuple-element.191) | copy-start | bytes 3538948
  104.3 12.3 %collective-permute-start.17 = (bf16[96,1536]{1,0:T(8,128)(2,1)}, bf16[96,1536]{1,0:T(8,128)(2,1)}, u32[]{:S(2)}, u32[]{:S(2)}) collective-permute-start(bf16[96,1536]{1,0:T(8,128)(2,1)} %get-tuple-element.194), channel_id=1, source_target_pairs={{0,2},{1,5},{2,0},{3,7},{4,6},{5,1},{6,4},{7,3},{8,10},{9,13},{10,... | collective-permute-start | bytes 884744 | tf_op jit(solution)/shard_map/ppermute | solution.py:978
  114.7 1.7 copy-start.14
  114.8 1.7 copy-start.15
  114.8 1.7 copy-start.12
  114.8 1.7 copy-start.13
  114.8 1.8 copy-start.10
  116.5 34.0 %collective-permute-start.23 = (f32[19,768]{1,0:T(8,128)S(1)}, f32[19,768]{1,0:T(8,128)S(1)}, u32[]{:S(2)}, u32[]{:S(2)}) collective-permute-start(f32[19,768]{1,0:T(8,128)S(1)} %pad_maximum_fusion.1), channel_id=1, source_target_pairs={{0,1},{1,0},{2,3},{3,2},{4,5},{5,4},{6,7},{7,6},{8,9},{9,8},{10,11... | collective-permute-start | bytes 175112 | tf_op jit(solution)/shard_map/ppermute | solution.py:993
  118.8 12.3 %collective-permute-start.20 = (bf16[240,1536]{1,0:T(8,128)(2,1)}, bf16[240,1536]{1,0:T(8,128)(2,1)}, u32[]{:S(2)}, u32[]{:S(2)}) collective-permute-start(bf16[240,1536]{1,0:T(8,128)(2,1)} %get-tuple-element.258), channel_id=1, source_target_pairs={{0,4},{1,3},{2,6},{3,1},{4,0},{5,7},{6,2},{7,5},{8,12},{9,11},{10,... | collective-permute-start | bytes 2211848 | tf_op jit(solution)/shard_map/ppermute | solution.py:978
  121.3 17.5 %collective-permute-start.21 = (bf16[384,768]{1,0:T(8,128)(2,1)}, bf16[384,768]{1,0:T(8,128)(2,1)}, u32[]{:S(2)}, u32[]{:S(2)}) collective-permute-start(bf16[384,768]{1,0:T(8,128)(2,1)} %add_convert_fusion.6), channel_id=1, source_target_pairs={{0,8},{1,9},{2,10},{3,11},{4,12},{5,13},{6,14},{7,15},{24,16},{25,... | collective-permute-start | bytes 1769480 | tf_op jit(solution)/shard_map/ppermute | solution.py:989
  130.5 16.0 %collective-permute-start.22 = (bf16[2,192,1152]{2,1,0:T(8,128)(2,1)}, bf16[2,192,1152]{2,1,0:T(8,128)(2,1)}, u32[]{:S(2)}, u32[]{:S(2)}) collective-permute-start(bf16[2,192,1152]{2,1,0:T(8,128)(2,1)} %bitcast.39), channel_id=1, source_target_pairs={{0,2},{1,5},{2,0},{3,7},{4,6},{5,1},{6,4},{7,3},{8,10},{9,13},{10,... | collective-permute-start | bytes 2654216 | tf_op jit(solution)/shard_map/ppermute | solution.py:978
  132.4 25.6 %collective-permute-start.24 = (bf16[240,1536]{1,0:T(8,128)(2,1)S(1)}, bf16[240,1536]{1,0:T(8,128)(2,1)}, u32[]{:S(2)}, u32[]{:S(2)}) collective-permute-start(bf16[240,1536]{1,0:T(8,128)(2,1)S(1)} %add_convert_fusion.3), channel_id=1, source_target_pairs={{0,8},{1,25},{2,10},{3,27},{4,12},{5,29},{6,14},{7,31},{8,0},{9,17... | collective-permute-start | bytes 2211848 | tf_op jit(solution)/shard_map/ppermute | solution.py:978
  140.1 19.2 %collective-permute-start.25 = (bf16[384,768]{1,0:T(8,128)(2,1)S(1)}, bf16[384,768]{1,0:T(8,128)(2,1)}, u32[]{:S(2)}, u32[]{:S(2)}) collective-permute-start(bf16[384,768]{1,0:T(8,128)(2,1)S(1)} %add_convert_fusion.5), channel_id=1, source_target_pairs={{8,16},{9,17},{10,18},{11,19},{12,20},{13,21},{14,22},{15,23},{16,... | collective-permute-start | bytes 1769480 | tf_op jit(solution)/shard_map/ppermute | solution.py:989
  148.9 14.2 %collective-permute-start.26 = (bf16[192,1152]{1,0:T(8,128)(2,1)}, bf16[192,1152]{1,0:T(8,128)(2,1)}, u32[]{:S(2)}, u32[]{:S(2)}) collective-permute-start(bf16[192,1152]{1,0:T(8,128)(2,1)} %get-tuple-element.260), channel_id=1, source_target_pairs={{0,4},{1,3},{2,6},{3,1},{4,0},{5,7},{6,2},{7,5},{8,12},{9,11},{10,... | collective-permute-start | bytes 1327112 | tf_op jit(solution)/shard_map/ppermute | solution.py:978
  150.6 15.1 %collective-permute-start.27 = (f32[19,768]{1,0:T(8,128)S(1)}, f32[19,768]{1,0:T(8,128)S(1)}, u32[]{:S(2)}, u32[]{:S(2)}) collective-permute-start(f32[19,768]{1,0:T(8,128)S(1)} %add.91), channel_id=1, source_target_pairs={{0,2},{1,5},{2,0},{3,7},{4,6},{5,1},{6,4},{7,3},{8,10},{9,13},{10,... | collective-permute-start | bytes 175112 | tf_op jit(solution)/shard_map/ppermute | solution.py:978
  158.0 14.6 %collective-permute-start.29 = (f32[512,384]{1,0:T(8,128)}, f32[512,384]{1,0:T(8,128)S(1)}, u32[]{:S(2)}, u32[]{:S(2)}) collective-permute-start(f32[512,384]{1,0:T(8,128)} %get-tuple-element.206), channel_id=1, source_target_pairs={{0,1},{1,0},{2,3},{3,2},{4,5},{5,4},{6,7},{7,6},{8,9},{9,8},{10,11... | collective-permute-start | bytes 2359304 | tf_op jit(solution)/shard_map/ppermute | solution.py:993
  159.3 11.0 %copy-start.9 = (bf16[512,384]{1,0:T(8,128)(2,1)S(1)}, bf16[512,384]{1,0:T(8,128)(2,1)}, u32[]{:S(2)}) copy-start(bf16[512,384]{1,0:T(8,128)(2,1)} %get-tuple-element.211) | copy-start | bytes 1179652
  159.3 18.8 %collective-permute-start.30 = (bf16[240,1536]{1,0:T(8,128)(2,1)S(1)}, bf16[240,1536]{1,0:T(8,128)(2,1)S(1)}, u32[]{:S(2)}, u32[]{:S(2)}) collective-permute-start(bf16[240,1536]{1,0:T(8,128)(2,1)S(1)} %add_convert_fusion.2), channel_id=1, source_target_pairs={{0,24},{1,9},{2,26},{3,11},{4,28},{5,13},{6,30},{7,15},{8,16},{9,1... | collective-permute-start | bytes 2211848 | tf_op jit(solution)/shard_map/ppermute | solution.py:978
  163.1 9.5 %copy-start.3 = (f32[512,384]{1,0:T(8,128)S(1)}, f32[512,384]{1,0:T(8,128)}, u32[]{:S(2)}) copy-start(f32[512,384]{1,0:T(8,128)} %get-tuple-element.214) | copy-start | bytes 2359300
  163.1 28.4 %collective-permute-start.31 = (bf16[384,768]{1,0:T(8,128)(2,1)S(1)}, bf16[384,768]{1,0:T(8,128)(2,1)S(1)}, u32[]{:S(2)}, u32[]{:S(2)}) collective-permute-start(bf16[384,768]{1,0:T(8,128)(2,1)S(1)} %add_convert_fusion.4), channel_id=1, source_target_pairs={{8,0},{9,1},{10,2},{11,3},{12,4},{13,5},{14,6},{15,7},{16,24},{17,... | collective-permute-start | bytes 1769480 | tf_op jit(solution)/shard_map/ppermute | solution.py:989
  165.7 35.3 %collective-permute-start.32 = (bf16[192,1152]{1,0:T(8,128)(2,1)S(1)}, bf16[192,1152]{1,0:T(8,128)(2,1)S(1)}, u32[]{:S(2)}, u32[]{:S(2)}) collective-permute-start(bf16[192,1152]{1,0:T(8,128)(2,1)S(1)} %add_convert_fusion.11), channel_id=1, source_target_pairs={{0,8},{1,25},{2,10},{3,27},{4,12},{5,29},{6,14},{7,31},{8,0},{9,17... | collective-permute-start | bytes 1327112 | tf_op jit(solution)/shard_map/ppermute | solution.py:978
  169.7 33.6 %collective-permute-start.33 = (f32[19,768]{1,0:T(8,128)S(1)}, f32[19,768]{1,0:T(8,128)S(1)}, u32[]{:S(2)}, u32[]{:S(2)}) collective-permute-start(f32[19,768]{1,0:T(8,128)S(1)} %add.95), channel_id=1, source_target_pairs={{0,4},{1,3},{2,6},{3,1},{4,0},{5,7},{6,2},{7,5},{8,12},{9,11},{10,... | collective-permute-start | bytes 175112 | tf_op jit(solution)/shard_map/ppermute | solution.py:978
  178.4 25.0 %collective-permute-start.34 = (bf16[240,1536]{1,0:T(8,128)(2,1)S(1)}, bf16[240,1536]{1,0:T(8,128)(2,1)S(1)}, u32[]{:S(2)}, u32[]{:S(2)}) collective-permute-start(bf16[240,1536]{1,0:T(8,128)(2,1)S(1)} %add_convert_fusion.1), channel_id=1, source_target_pairs={{0,4},{1,3},{2,6},{3,1},{4,0},{5,7},{6,2},{7,5},{8,12},{9,11},{10,... | collective-permute-start | bytes 2211848 | tf_op jit(solution)/shard_map/ppermute | solution.py:978
  191.6 12.1 %collective-permute-start.35 = (bf16[384,768]{1,0:T(8,128)(2,1)S(1)}, bf16[384,768]{1,0:T(8,128)(2,1)S(1)}, u32[]{:S(2)}, u32[]{:S(2)}) collective-permute-start(bf16[384,768]{1,0:T(8,128)(2,1)S(1)} %broadcast_select_fusion.2), channel_id=1, source_target_pairs={{0,4},{1,3},{2,6},{3,1},{4,0},{5,7},{6,2},{7,5},{8,12},{9,11},{10,... | collective-permute-start | bytes 1769480 | tf_op jit(solution)/shard_map/ppermute | solution.py:978
  201.1 14.1 %collective-permute-start.36 = (bf16[192,1152]{1,0:T(8,128)(2,1)S(1)}, bf16[192,1152]{1,0:T(8,128)(2,1)S(1)}, u32[]{:S(2)}, u32[]{:S(2)}) collective-permute-start(bf16[192,1152]{1,0:T(8,128)(2,1)S(1)} %add_convert_fusion.10), channel_id=1, source_target_pairs={{0,24},{1,9},{2,26},{3,11},{4,28},{5,13},{6,30},{7,15},{8,16},{9,1... | collective-permute-start | bytes 1327112 | tf_op jit(solution)/shard_map/ppermute | solution.py:978
  203.6 12.4 %copy-start = (bf16[2,240,1536]{2,1,0:T(8,128)(2,1)}, bf16[2,240,1536]{2,1,0:T(8,128)(2,1)S(1)}, u32[]{:S(2)}) copy-start(bf16[2,240,1536]{2,1,0:T(8,128)(2,1)S(1)} %maximum_select_fusion.1) | copy-start | bytes 4423684
  215.3 13.1 %collective-permute-start.38 = (bf16[192,1152]{1,0:T(8,128)(2,1)S(1)}, bf16[192,1152]{1,0:T(8,128)(2,1)S(1)}, u32[]{:S(2)}, u32[]{:S(2)}) collective-permute-start(bf16[192,1152]{1,0:T(8,128)(2,1)S(1)} %add_convert_fusion.9), channel_id=1, source_target_pairs={{0,4},{1,3},{2,6},{3,1},{4,0},{5,7},{6,2},{7,5},{8,12},{9,11},{10,... | collective-permute-start | bytes 1327112 | tf_op jit(solution)/shard_map/ppermute | solution.py:978
  216.1 24.3 %collective-permute-start.40 = (bf16[2,240,1536]{2,1,0:T(8,128)(2,1)S(1)}, bf16[2,240,1536]{2,1,0:T(8,128)(2,1)}, u32[]{:S(2)}, u32[]{:S(2)}) collective-permute-start(bf16[2,240,1536]{2,1,0:T(8,128)(2,1)S(1)} %maximum_select_fusion.1), channel_id=1, source_target_pairs={{0,2},{1,5},{2,0},{3,7},{4,6},{5,1},{6,4},{7,3},{8,10},{9,13},{10,... | collective-permute-start | bytes 4423688 | tf_op jit(solution)/shard_map/ppermute | solution.py:978
  217.9 4.7 %collective-permute-start.37 = (f32[19,768]{1,0:T(8,128)S(1)}, f32[19,768]{1,0:T(8,128)S(1)}, u32[]{:S(2)}, u32[]{:S(2)}) collective-permute-start(f32[19,768]{1,0:T(8,128)S(1)} %add.98), channel_id=1, source_target_pairs={{0,8},{1,25},{2,10},{3,27},{4,12},{5,29},{6,14},{7,31},{8,0},{9,17... | collective-permute-start | bytes 175112 | tf_op jit(solution)/shard_map/ppermute | solution.py:978
  217.9 34.1 %collective-permute-start.41 = (bf16[2,384,768]{2,1,0:T(8,128)(2,1)}, bf16[2,384,768]{2,1,0:T(8,128)(2,1)}, u32[]{:S(2)}, u32[]{:S(2)}) collective-permute-start(bf16[2,384,768]{2,1,0:T(8,128)(2,1)} %maximum_select_fusion.2.half), channel_id=1, source_target_pairs={{0,2},{1,5},{2,0},{3,7},{4,6},{5,1},{6,4},{7,3},{8,10},{9,13},{10,... | collective-permute-start | bytes 3538952 | tf_op jit(solution)/shard_map/ppermute | solution.py:978
  229.5 32.0 %collective-permute-start.42 = (bf16[2,192,1152]{2,1,0:T(8,128)(2,1)}, bf16[2,192,1152]{2,1,0:T(8,128)(2,1)}, u32[]{:S(2)}, u32[]{:S(2)}) collective-permute-start(bf16[2,192,1152]{2,1,0:T(8,128)(2,1)} %maximum_select_fusion.3), channel_id=1, source_target_pairs={{0,2},{1,5},{2,0},{3,7},{4,6},{5,1},{6,4},{7,3},{8,10},{9,13},{10,... | collective-permute-start | bytes 2654216 | tf_op jit(solution)/shard_map/ppermute | solution.py:978
  231.6 6.2 %collective-permute-start.39 = (f32[19,768]{1,0:T(8,128)S(1)}, f32[19,768]{1,0:T(8,128)S(1)}, u32[]{:S(2)}, u32[]{:S(2)}) collective-permute-start(f32[19,768]{1,0:T(8,128)S(1)} %add.100), channel_id=1, source_target_pairs={{0,24},{1,9},{2,26},{3,11},{4,28},{5,13},{6,30},{7,15},{8,16},{9,1... | collective-permute-start | bytes 175112 | tf_op jit(solution)/shard_map/ppermute | solution.py:978

commit v3 on v2

--- a/solution.py
+++ b/solution.py
@@ -11,7 +11,7 @@
 HD = 64
 BLOCK = 512
 LANES = 128
-TILE = 512
+TILE = 768
 
 norm_eps = 1e-05
 gate_temper = 2.0 / 3.0
@@ -93,7 +93,11 @@
     out_ref[...] = jnp.full(out_ref.shape, 0.5, f32)
     for ref, (spot, lane) in zip(refs[:-1], counts):
         size = ref.shape[0]
-        out_ref[:, spot[0] + lane : spot[0] + lane + size] = ref[...].reshape(1, size)
+        at = slice(spot[0] + lane, spot[0] + lane + size)
+        if size > 1:
+            out_ref[:, at] = ref[...].reshape(1, size)
+        else:
+            out_ref[:, at] = jnp.full((1, 1), ref[0], f32)
 
 
 def take(pack_ref, spot):
@@ -914,6 +918,18 @@
     return jax.ShapeDtypeStruct(shape, dtype)
 
 
+def far(struct):
+    return pltpu.HBM(struct.shape, struct.dtype)
+
+
+ORDER = (
+    *("K3a", "KD", "K3b", "KU", "hD", "K4a", "Kao", "qD", "K4b", "hU", "KAs", "sD", "qU", "KAk"),
+    *("S0", "hA", "sD", "S", "K6", "sU", "qA", "sD", "S", "O", "sU", "sA", "wD", "S", "sU", "sA"),
+    *("sA", "pD", "S", "wU", "wA", "F", "pU", "pA"),
+)
+ON_PATH = ("D", "U", "A")
+
+
 class Order:
     def __init__(self):
         self.last = ()
@@ -928,7 +944,7 @@
         self.last = values_in
 
 
-def call(order, kernel, grid, in_specs, out_specs, out_shape, scratch, cost, args, mib=62):
+def call(order, kernel, grid, in_specs, out_specs, out_shape, scratch, cost, args, mib=34):
     out = pl.pallas_call(
         kernel,
         grid=grid,
@@ -947,7 +963,7 @@
     return out
 
 
-def call_by_half(order, kernel, grid, in_specs, out_specs, out_shape, cost, half, args, mib=62):
+def call_by_half(order, kernel, grid, in_specs, out_specs, out_shape, cost, half, args, mib=34):
     out = pl.pallas_call(
         kernel,
         grid_spec=pltpu.PrefetchScalarGridSpec(
@@ -987,6 +1003,10 @@
         for core in range(cores)
     ]
     return lax.ppermute(values_in, ("rows", "hid"), pairs)
+
+
+def in_hbm(values_in):
+    return pltpu.with_memory_space_constraint(values_in, pltpu.HBM)
 
 
 def near(values_in):
@@ -1165,12 +1185,13 @@
         order,
         partial(pack_kernel, pack, [item[1:] for item in packed]),
         (),
-        [full(item[0].shape) for item in packed],
+        [full(item[0].shape) if item[0].shape[0] > 1 else one_number() for item in packed],
         full((1, pack.total)),
         shaped((1, pack.total), f32),
         [],
         (0.001, 0.1, 0),
-        tuple(item[0] for item in packed),
+        tuple(in_hbm(item[0]) if item[0].shape[0] > 1 else item[0] for item in packed),
+        mib=4,
     )
     x_peer = near(hidden_in)
     pack_peer = near(pack_own)
@@ -1182,8 +1203,17 @@
     )
     x_peer, pack_peer, wq_peer, wk_peer, wv_peer, wa_peer = first_peers
     up_peer, down_peer, teacher_peer = near(up_sent), near(down_sent), near(teacher_sent)
-    segments = segment_ids.reshape(-1, LANES)
-    valid = valid_mask.reshape(-1, LANES)
+    hidden_in, x_peer, teacher, teacher_peer = (
+        in_hbm(item) for item in (hidden_in, x_peer, teacher, teacher_peer)
+    )
+    w_query, w_key, w_value, w_attn_out, w_up, w_down = (
+        in_hbm(item) for item in (w_query, w_key, w_value, w_attn_out, w_up, w_down)
+    )
+    wq_peer, wk_peer, wv_peer, wa_peer, up_peer, down_peer = (
+        in_hbm(item) for item in (wq_peer, wk_peer, wv_peer, wa_peer, up_peer, down_peer)
+    )
+    segments = in_hbm(segment_ids.reshape(-1, LANES))
+    valid = in_hbm(valid_mask.reshape(-1, LANES))
     packs = [full((1, pack.total))] * 2
     pair_early, pair_late = sides(pairs // 2)
     token_low = shaped((tokens, model), bf16)
@@ -1219,16 +1249,16 @@
         + [full((tokens, LANES))]
         + [full((tokens, model))] * 3,
         [
-            shaped((2 * pairs, BLOCK, BLOCK), bf16),
-            token_low,
-            token_low,
-            token_low,
-            token_low,
-            token_half,
-            token_half,
+            far(shaped((2 * pairs, BLOCK, BLOCK), bf16)),
+            far(token_low),
+            far(token_low),
+            far(token_low),
+            far(token_low),
+            far(token_half),
+            far(token_half),
             shaped((tokens, LANES), f32),
-            token_wide,
-            token_wide,
+            far(token_wide),
+            far(token_wide),
             token_low,
         ],
         [
@@ -1260,6 +1290,7 @@
             valid,
         ),
     )
+    normed, biased = in_hbm(normed), in_hbm(biased)
     hidden_near = near(hidden)
     gated_near = near(gated_peer)
 
@@ -1296,9 +1327,9 @@
             shaped((tokens, units), bf16),
             shaped((tokens, 2 * units), bf16),
             shaped((tokens, 2 * units), bf16),
-            token_half,
-            token_half,
-            token_wide,
+            far(token_half),
+            far(token_half),
+            far(token_wide),
             token_low,
             shaped((4, model), f32),
         ],
@@ -1324,28 +1355,13 @@
             valid,
         ),
     )
+    grad_resid_two = in_hbm(grad_resid_two)
     mixed_near = near(mixed_peer)
     grad_ffn_near = near(grad_ffn)
     output_near = near(output_peer)
-
-    grad_pre_own, grad_pre_peer, unit_sums = call(
-        order,
-        partial(ffn_pre_kernel, pack),
-        (2 * tiles,),
-        [one_number(), full((tokens, model))]
-        + [every((tokens, TILE), 1)] * 2
-        + [early((TILE, model), 0), late((TILE, model), 0)],
-        [early((tokens, TILE), 1), late((tokens, TILE), 1), full((2, 2 * units))],
-        [
-            shaped((tokens, units), bf16),
-            shaped((tokens, units), bf16),
-            shaped((2, 2 * units), f32),
-        ],
-        [],
-        (50, 300, 0),
-        (core_at, grad_ffn, active, slope, w_down, down_peer),
-    )
-    grad_pre_near = near(grad_pre_peer)
+    up_rows = width + width // 4
+    half_units = units // 2
+    step_units = half_units // 2
 
     bit_at = jnp.reshape(first_bit, (1,))
 
@@ -1364,73 +1380,10 @@
             )
         ]
 
-    half_units = units // 2
-    step_units = half_units // 2
-    by_units = pl.BlockSpec(
-        (tokens, step_units), lambda i, t: (0, at_half(i, 2, t) * 2 + lax.rem(i, 2))
-    )
-    down_sent, down_kept = call_by_half(
-        order,
-        down_grad_kernel,
-        (4,),
-        [by_units, by_units] + [full((tokens, model))] * 2,
-        sent_then_kept((step_units, model), 2, 0),
-        [shaped((half_units, model), bf16)] * 2,
-        (48, 180),
-        bit_at,
-        (mixed_own, mixed_near, grad_ffn, grad_ffn_near),
-    )
-    down_sent, down_kept = (
-        item.reshape(2, half_units // 2, model) for item in (down_sent, down_kept)
-    )
-    down_chunk = RowSum(order, down_sent, first_bit, second_bit)
-
-    up_rows = width + width // 4
-    by_features = pl.BlockSpec((tokens, width), lambda i, t: (0, at_half(i, 2, t)))
-    by_units = pl.BlockSpec((tokens, half_units), lambda i, t: (0, lax.rem(i, 2)))
-    up_sent, up_kept = call_by_half(
-        order,
-        down_grad_kernel,
-        (4,),
-        [by_features, by_features, by_units, by_units],
-        sent_then_kept((width, half_units), 2, 1),
-        [shaped((width, units), bf16)] * 2,
-        (2.4, 12),
-        bit_at,
-        (hidden, hidden_near, grad_pre_own, grad_pre_near),
-    )
-    up_chunk = RowSum(order, up_sent, first_bit, second_bit)
-
-    grad_resid_one, grad_attn, sums_one = call(
-        order,
-        partial(ffn_backward_kernel, pack),
-        (2 * tiles,),
-        [one_number()]
-        + [early((tokens, TILE), 1), late((tokens, TILE), 1)]
-        + [anywhere()] * 3
-        + [full((tokens, LANES))]
-        + [early((model, TILE), 1), late((model, TILE), 1)]
-        + packs,
-        [full((tokens, model))] * 2 + [full((4, model))],
-        [token_wide, token_low, shaped((4, model), f32)],
-        [pltpu.VMEM((tokens, model), f32)] * 4 + [pltpu.SemaphoreType.DMA((3,))],
-        (2.5, 15, 0),
-        (
-            core_at,
-            grad_pre_own,
-            grad_pre_peer,
-            grad_resid_two,
-            normed,
-            biased,
-            stats,
-            w_up,
-            up_peer,
-            pack_own,
-            pack_peer,
-        ),
-    )
-    grad_attn_near = near(grad_attn)
     own_pairs = pairs // 2
+    weights, query, key, value, context = (
+        in_hbm(item) for item in (weights, query, key, value, context)
+    )
 
     def attend_back(side_is_own, wa_ref):
         first = 0 if side_is_own else own_pairs
@@ -1460,32 +1413,8 @@
                 pack_own,
                 pack_peer,
             ),
-        )
-
-    grad_peer, sums_peer = attend_back(False, wa_peer)
-    grad_near = near(grad_peer)
-    down_chunk.halve(down_kept)
-    by_columns = pl.BlockSpec((tokens, width), lambda i, t: (0, at_half(i, 1, t)))
-    attn_sent, attn_kept = call_by_half(
-        order,
-        attn_out_grad_kernel,
-        (2,),
-        [full((tokens, width))] * 2 + [by_columns] * 2,
-        [full((width // 4, units))] * 2,
-        [shaped((width // 4, units), bf16)] * 2,
-        (0.6, 3),
-        bit_at,
-        (gated_own, gated_near, grad_attn, grad_attn_near),
-    )
-    attn_near = swap(attn_sent, (1, 2))
-    grad_own, sums_own = attend_back(True, w_attn_out)
-    up_chunk.halve_with(up_kept, attn_kept, attn_near)
-    down_chunk.quarter(path=True)
-    sums_attn = jnp.where(
-        core == 0,
-        jnp.concatenate((sums_own, sums_peer), axis=1),
-        jnp.concatenate((sums_peer, sums_own), axis=1),
-    )
+            mib=18,
+        )
 
     def attend_half(half):
         out = call(
@@ -1498,84 +1427,9 @@
             [pltpu.VMEM(hidden_in.shape, bf16), pltpu.SemaphoreType.DMA],
             (24, 100, 0),
             (jnp.reshape(half, (1,)), core_at, hidden_in, x_peer, grad_own, grad_near),
+            mib=12,
         )
         return out.reshape(2, width // 2, 3 * width)
-
-    attend_sent = attend_half(1 - first_bit)
-    attend_chunk = RowSum(order, attend_sent, first_bit, second_bit)
-    up_chunk.quarter()
-    down_chunk.spread()
-    small = SmallSum(
-        order,
-        jnp.concatenate((sums_two, sums_one, sums_attn, unit_sums.reshape(-1, model)), axis=0),
-    )
-    attend_kept = attend_half(first_bit)
-    attend_chunk.halve(attend_kept)
-    small.step()
-
-    input_own, input_peer = call(
-        order,
-        partial(input_grad_kernel, width),
-        (),
-        [one_number(), full((tokens, model))]
-        + [full((tokens, 3 * width))] * 2
-        + [full((model, width))] * 6,
-        [full((tokens, width))] * 2,
-        [shaped((tokens, width), f32)] * 2,
-        [],
-        (1.8, 8, 0),
-        (
-            core_at,
-            grad_resid_one,
-            grad_own,
-            grad_peer,
-            w_query,
-            w_key,
-            w_value,
-            wq_peer,
-            wk_peer,
-            wv_peer,
-        ),
-    )
-    input_near = near(input_peer)
-
-    def by_token(own, other):
-        own = order.tie(own)
-        out = jnp.where(
-            core == 0, jnp.concatenate((own, other), axis=0), jnp.concatenate((other, own), axis=0)
-        )
-        order.mark(out)
-        return out
-
-    up_chunk.spread()
-    down_chunk.spread()
-    attend_chunk.quarter()
-    small.step()
-    output = by_token(output_own, output_near)
-    grad_input = by_token(input_own, input_near)
-    up_chunk.spread()
-    down_chunk.spread()
-    attend_chunk.spread()
-    small.step()
-    up_chunk.widen()
-    down_chunk.widen()
-    attend_chunk.spread()
-    small.step()
-    attend_chunk.widen()
-    small_sums = small.rest()
-    sizes = (width,) * 5 + (units,) + (width,) * 3 + (heads, 1, units, 1, width)
-    sizes = sizes + (heads, 1, units, 1, width, 1, 1)
-    finished = call(
-        order,
-        partial(finish_kernel, pack),
-        (),
-        [one_number(), full(small_sums.shape)] + packs,
-        [full((size,)) for size in sizes],
-        [shaped((size,), f32) for size in sizes],
-        [],
-        (0.01, 0.3, 0.1),
-        (core_at, small_sums, pack_own, pack_peer),
-    )
 
     def place(pieces):
         _, height, across = pieces[0].shape
@@ -1596,8 +1450,17 @@
             (0.001, 7),
             bit_at,
             pieces,
+            mib=18,
         )
         return out.reshape(4 * height, across)
+
+    def by_token(own, other):
+        own = order.tie(own)
+        out = jnp.where(
+            core == 0, jnp.concatenate((own, other), axis=0), jnp.concatenate((other, own), axis=0)
+        )
+        order.mark(out)
+        return out
 
     def by_half(pieces):
         return tuple(piece.reshape(-1, piece.shape[-1]) for piece in pieces)
@@ -1607,29 +1470,273 @@
             shape, lambda i, t: tuple(lax.rem(t[0] + i, 2) if d == dim else 0 for d in range(2))
         )
 
-    sum_up, sum_attn = call_by_half(
-        order,
-        place_up_kernel,
-        (2,),
-        [full((up_rows, units))] * 2,
-        [own_half((width, units), 0), own_half((width, width), 1)],
-        [shaped((model, units), f32), shaped((width, model), f32)],
-        (0.001, 10),
-        bit_at,
-        by_half(up_chunk.parts()),
-    )
-    sum_down = place(down_chunk.parts())
-    sum_query, sum_key, sum_value = call_by_half(
-        order,
-        place_attend_kernel,
-        (2,),
-        [full((width, 3 * width))] * 2,
-        [own_half((width, width), 0)] * 3,
-        [shaped((model, width), f32)] * 3,
-        (0.001, 7),
-        bit_at,
-        by_half(attend_chunk.parts()),
-    )
+    grad_pre_own = grad_pre_peer = unit_sums = grad_pre_near = down_kept = down_chunk = None
+    grad_resid_one = grad_attn = sums_one = grad_attn_near = up_kept = up_chunk = None
+    grad_peer = sums_peer = grad_near = attn_kept = attn_near = grad_own = None
+    sums_own = attend_chunk = attend_kept = small = input_own = input_peer = None
+    input_near = output = grad_input = sum_down = finished = sum_up = None
+    sum_attn = sum_query = sum_key = sum_value = None
+
+    def units_back():
+        nonlocal grad_pre_own, grad_pre_peer, unit_sums, grad_pre_near
+        grad_pre_own, grad_pre_peer, unit_sums = call(
+            order,
+            partial(ffn_pre_kernel, pack),
+            (2 * tiles,),
+            [one_number(), full((tokens, model))]
+            + [every((tokens, TILE), 1)] * 2
+            + [early((TILE, model), 0), late((TILE, model), 0)],
+            [early((tokens, TILE), 1), late((tokens, TILE), 1), full((2, 2 * units))],
+            [
+                shaped((tokens, units), bf16),
+                shaped((tokens, units), bf16),
+                shaped((2, 2 * units), f32),
+            ],
+            [],
+            (50, 300, 0),
+            (core_at, grad_ffn, active, slope, w_down, down_peer),
+            mib=18,
+        )
+        grad_pre_near = near(grad_pre_peer)
+
+    def down_grads():
+        nonlocal down_kept, down_chunk
+        by_units = pl.BlockSpec(
+            (tokens, step_units), lambda i, t: (0, at_half(i, 2, t) * 2 + lax.rem(i, 2))
+        )
+        down_sent, down_kept = call_by_half(
+            order,
+            down_grad_kernel,
+            (4,),
+            [by_units, by_units] + [full((tokens, model))] * 2,
+            sent_then_kept((step_units, model), 2, 0),
+            [shaped((half_units, model), bf16)] * 2,
+            (48, 180),
+            bit_at,
+            (mixed_own, mixed_near, grad_ffn, grad_ffn_near),
+            mib=12,
+        )
+        down_sent, down_kept = (
+            item.reshape(2, half_units // 2, model) for item in (down_sent, down_kept)
+        )
+        down_chunk = RowSum(order, down_sent, first_bit, second_bit)
+
+    def ffn_back():
+        nonlocal grad_resid_one, grad_attn, sums_one, grad_attn_near
+        grad_resid_one, grad_attn, sums_one = call(
+            order,
+            partial(ffn_backward_kernel, pack),
+            (2 * tiles,),
+            [one_number()]
+            + [early((tokens, TILE), 1), late((tokens, TILE), 1)]
+            + [anywhere()] * 3
+            + [full((tokens, LANES))]
+            + [early((model, TILE), 1), late((model, TILE), 1)]
+            + packs,
+            [full((tokens, model))] * 2 + [full((4, model))],
+            [far(token_wide), token_low, shaped((4, model), f32)],
+            [pltpu.VMEM((tokens, model), f32)] * 4 + [pltpu.SemaphoreType.DMA((3,))],
+            (2.5, 15, 0),
+            (
+                core_at,
+                grad_pre_own,
+                grad_pre_peer,
+                grad_resid_two,
+                normed,
+                biased,
+                stats,
+                w_up,
+                up_peer,
+                pack_own,
+                pack_peer,
+            ),
+            mib=20,
+        )
+        grad_attn_near = near(grad_attn)
+
+    def up_grads():
+        nonlocal up_kept, up_chunk
+        by_features = pl.BlockSpec((tokens, width), lambda i, t: (0, at_half(i, 2, t)))
+        by_units = pl.BlockSpec((tokens, half_units), lambda i, t: (0, lax.rem(i, 2)))
+        up_sent, up_kept = call_by_half(
+            order,
+            down_grad_kernel,
+            (4,),
+            [by_features, by_features, by_units, by_units],
+            sent_then_kept((width, half_units), 2, 1),
+            [shaped((width, units), bf16)] * 2,
+            (2.4, 12),
+            bit_at,
+            (hidden, hidden_near, grad_pre_own, grad_pre_near),
+            mib=18,
+        )
+        up_chunk = RowSum(order, up_sent, first_bit, second_bit)
+
+    def peer_heads():
+        nonlocal grad_peer, sums_peer, grad_near
+        grad_peer, sums_peer = attend_back(False, wa_peer)
+        grad_near = near(grad_peer)
+
+    def own_heads():
+        nonlocal grad_own, sums_own
+        grad_own, sums_own = attend_back(True, w_attn_out)
+
+    def out_grads():
+        nonlocal attn_kept, attn_near
+        by_columns = pl.BlockSpec((tokens, width), lambda i, t: (0, at_half(i, 1, t)))
+        attn_sent, attn_kept = call_by_half(
+            order,
+            attn_out_grad_kernel,
+            (2,),
+            [full((tokens, width))] * 2 + [by_columns] * 2,
+            [full((width // 4, units))] * 2,
+            [shaped((width // 4, units), bf16)] * 2,
+            (0.6, 3),
+            bit_at,
+            (gated_own, gated_near, grad_attn, grad_attn_near),
+            mib=8,
+        )
+        attn_near = swap(attn_sent, (1, 2))
+
+    def send_attend():
+        nonlocal attend_chunk
+        attend_sent = attend_half(1 - first_bit)
+        attend_chunk = RowSum(order, attend_sent, first_bit, second_bit)
+
+    def keep_attend():
+        nonlocal attend_kept
+        attend_kept = attend_half(first_bit)
+
+    def start_small():
+        nonlocal small
+        sums_attn = jnp.where(
+            core == 0,
+            jnp.concatenate((sums_own, sums_peer), axis=1),
+            jnp.concatenate((sums_peer, sums_own), axis=1),
+        )
+        small = SmallSum(
+            order,
+            jnp.concatenate((sums_two, sums_one, sums_attn, unit_sums.reshape(-1, model)), axis=0),
+        )
+
+    def inputs_back():
+        nonlocal input_own, input_peer, input_near
+        input_own, input_peer = call(
+            order,
+            partial(input_grad_kernel, width),
+            (),
+            [one_number(), full((tokens, model))]
+            + [full((tokens, 3 * width))] * 2
+            + [full((model, width))] * 6,
+            [full((tokens, width))] * 2,
+            [shaped((tokens, width), f32)] * 2,
+            [],
+            (1.8, 8, 0),
+            (
+                core_at,
+                in_hbm(grad_resid_one),
+                grad_own,
+                grad_peer,
+                w_query,
+                w_key,
+                w_value,
+                wq_peer,
+                wk_peer,
+                wv_peer,
+            ),
+            mib=16,
+        )
+        input_near = near(input_peer)
+
+    def put_output():
+        nonlocal output, grad_input
+        output = by_token(output_own, output_near)
+        grad_input = by_token(input_own, input_near)
+
+    def finish_small():
+        nonlocal finished
+        small_sums = small.rest()
+        sizes = (width,) * 5 + (units,) + (width,) * 3 + (heads, 1, units, 1, width)
+        sizes = sizes + (heads, 1, units, 1, width, 1, 1)
+        finished = call(
+            order,
+            partial(finish_kernel, pack),
+            (),
+            [one_number(), full(small_sums.shape)] + packs,
+            [full((size,)) for size in sizes],
+            [shaped((size,), f32) for size in sizes],
+            [],
+            (0.01, 0.3, 0.1),
+            (core_at, small_sums, pack_own, pack_peer),
+        )
+
+    def place_down():
+        nonlocal sum_down
+        sum_down = place(down_chunk.parts())
+
+    def place_up():
+        nonlocal sum_up, sum_attn
+        sum_up, sum_attn = call_by_half(
+            order,
+            place_up_kernel,
+            (2,),
+            [full((up_rows, units))] * 2,
+            [own_half((width, units), 0), own_half((width, width), 1)],
+            [shaped((model, units), f32), shaped((width, model), f32)],
+            (0.001, 10),
+            bit_at,
+            by_half(up_chunk.parts()),
+            mib=18,
+        )
+
+    def place_attend():
+        nonlocal sum_query, sum_key, sum_value
+        sum_query, sum_key, sum_value = call_by_half(
+            order,
+            place_attend_kernel,
+            (2,),
+            [full((width, 3 * width))] * 2,
+            [own_half((width, width), 0)] * 3,
+            [shaped((model, width), f32)] * 3,
+            (0.001, 7),
+            bit_at,
+            by_half(attend_chunk.parts()),
+            mib=18,
+        )
+
+    steps = dict(
+        K3a=units_back,
+        KD=down_grads,
+        K3b=ffn_back,
+        KU=up_grads,
+        K4a=peer_heads,
+        K4b=own_heads,
+        Kao=out_grads,
+        KAs=send_attend,
+        KAk=keep_attend,
+        S0=start_small,
+        S=lambda: small.step(),
+        K6=inputs_back,
+        O=put_output,
+        F=finish_small,
+        hD=lambda: down_chunk.halve(down_kept),
+        qD=lambda: down_chunk.quarter("D" in ON_PATH),
+        sD=lambda: down_chunk.spread(),
+        wD=lambda: down_chunk.widen(),
+        pD=place_down,
+        hU=lambda: up_chunk.halve_with(up_kept, attn_kept, attn_near),
+        qU=lambda: up_chunk.quarter("U" in ON_PATH),
+        sU=lambda: up_chunk.spread(),
+        wU=lambda: up_chunk.widen(),
+        pU=place_up,
+        hA=lambda: attend_chunk.halve(attend_kept),
+        qA=lambda: attend_chunk.quarter("A" in ON_PATH),
+        sA=lambda: attend_chunk.spread(),
+        wA=lambda: attend_chunk.widen(),
+        pA=place_attend,
+    )
+    for name in ORDER:
+        steps[name]()
     return (
         output,
         grad_input,

time: 266 us -> 236 us (0.89)
  Pallas kernels: 124 us -> 97 us
  other arithmetic: 24.1 us -> 10.2 us
  waiting for transfers between devices: 72.5 us -> 78.7 us
  starting transfers between devices: 39 us -> 43.7 us
    ppermute x3 -> x9, waiting for transfers between devices: 18.2 us -> 43.1 us  [along(): return lax.ppermute(values_in, ('rows', 'hid'), pairs)]
    ppermute x21 -> x17, waiting for transfers between devices: 50.6 us -> 31.9 us  [swap(): return lax.ppermute(values_in, ('rows', 'hid'), swap_pairs(core_masks))]
    pallas_call x11, Pallas kernels: 94.3 us -> 77 us  [call(): pl.pallas_call(kernel, grid=grid, in_specs=in_specs, out_specs=out_specs,...]
    pallas_call x6, Pallas kernels: 29.9 us -> 20.1 us  [call_by_half(): pl.pallas_call(kernel, grid_spec=pltpu.PrefetchScalarGridSpec(num_scalar_...]
    convert_element_type x13, other arithmetic: 16 us -> 6.64 us  [to_low(): return values_in.astype(bf16)]
    ppermute x3 -> x9, starting transfers between devices: 7.19 us -> 13 us  [along(): return lax.ppermute(values_in, ('rows', 'hid'), pairs)]
    ppermute x21 -> x17, starting transfers between devices: 26.7 us -> 26 us  [swap(): return lax.ppermute(values_in, ('rows', 'hid'), swap_pairs(core_masks))]
  transfers between devices with their start and end apart: 43 -> 45, of which waited for: 15 -> 18; matrix products, arithmetic and copies ran while one was open for 9% -> 4% of each run, Pallas kernels for 46% -> 34%
where the time goes in v3:
time: 236 us; the launch traced here: 235 us
  Pallas kernels  97 us (41%)
  waiting for transfers between devices  78.7 us (33%)
  starting transfers between devices  43.7 us (19%)
  other arithmetic  10.2 us (4%)
  between operations  3.76 us (2%)
    pallas_call x11, Pallas kernels, call(): pl.pallas_call(kernel, grid=grid, in_specs=in_specs, out_specs=out_specs,...  77 us
    ppermute x9, waiting for transfers between devices, along(): return lax.ppermute(values_in, ('rows', 'hid'), pairs)  43.1 us
    ppermute x17, waiting for transfers between devices, swap(): return lax.ppermute(values_in, ('rows', 'hid'), swap_pairs(core_masks))  31.9 us
    ppermute x17, starting transfers between devices, swap(): return lax.ppermute(values_in, ('rows', 'hid'), swap_pairs(core_masks))  26 us
    pallas_call x6, Pallas kernels, call_by_half(): pl.pallas_call(kernel, grid_spec=pltpu.PrefetchScalarGridSpec(num_scalar_...  20.1 us
    ppermute x9, starting transfers between devices, along(): return lax.ppermute(values_in, ('rows', 'hid'), pairs)  13 us
    convert_element_type x13, other arithmetic, to_low(): return values_in.astype(bf16)  6.64 us
  transfers between devices with their start and end apart: 45, of which 18 were waited for; matrix products, arithmetic and copies ran while one was open for 4% of the time, Pallas kernels for 34%

profile of v3, /device:TPU:0, one launch (start us, length us, event | category | flops | bytes accessed | tf_op | source)
XLA Modules:
  0.0 234.6 jit_solution(7081918865225218087)
XLA Ops:
  3.8 0.9 shard_map.509.pack_own
  6.1 1.0 collective-permute-done.2.wq_peer
  7.1 0.8 collective-permute-done.3.wk_peer
  7.9 0.8 collective-permute-done.4.wv_peer
  8.8 0.8 collective-permute-done.5.wa_peer.wa_ref
  10.5 19.0 %shard_map.510 = (bf16[12,512,512]{2,1,0:T(8,128)(2,1)}, bf16[512,768]{1,0:T(8,128)(2,1)}, bf16[512,768]{1,0:T(8,128)(2,1)}, bf16[512,768]{1,0:T(8,128)(2,1)}, b...) custom-call(s32[1]{0:T(128)} %bitcast.core_ref, ...), custom_call_target="tpu_custom_call" | custom-call | flops 4000000000 | bytes 20000000 | tf_op jit(solution)/shard_map/pallas_call | solution.py:948
  29.5 15.0 %shard_map.511 = (bf16[512,1536]{1,0:T(8,128)(2,1)S(1)}, bf16[512,1536]{1,0:T(8,128)(2,1)S(1)}, bf16[512,3072]{1,0:T(8,128)(2,1)S(1)}, bf16[512,3072]{1,0:T(8,12...) custom-call(s32[1]{0:T(128)} %bitcast.core_ref, ...), custom_call_target="tpu_custom_call" | custom-call | flops 5000000000 | bytes 25000000 | tf_op jit(solution)/shard_map/pallas_call | solution.py:948
  45.1 7.4 %shard_map.512 = (bf16[512,1536]{1,0:T(8,128)(2,1)S(1)}, bf16[512,1536]{1,0:T(8,128)(2,1)}, f32[2,3072]{1,0:T(2,128)S(1)}) custom-call(s32[1]{0:T(128)} %bitcast.core_ref, bf16[512,768]{1,0:T(8,128)(2,1)S(1)} %get-tuple-element.160.grad_ffn.grad, bf16[512,3072]{1,0:T(8,128)(2,1)S(1)} %get-tuple-element.161.active, ...), custom_call_target="tpu_custom_call" | custom-call | flops 49999998976 | bytes 300000000 | tf_op jit(solution)/shard_map/pallas_call | solution.py:948
  52.8 4.8 %shard_map.513 = (bf16[768,768]{1,0:T(8,128)(2,1)}, bf16[768,768]{1,0:T(8,128)(2,1)S(1)}) custom-call(s32[1]{0:T(128)} %bitcast.3.bit_ref.half_ref, bf16[512,1536]{1,0:T(8,128)(2,1)S(1)} %get-tuple-element.165.mixed, bf16[512,1536]{1,0:T(8,128)(2,1)S(1)} %collective-permute-done.9.mixed_near, bf16[512,768]{1,0:T(8,128)(2,1)S(1)} %get-tuple-element.160.grad_ffn.grad, ...), custom_call_target="tpu_custom_call" | custom-call | flops 48000000000 | bytes 180000000 | tf_op jit(solution)/shard_map/pallas_call | solution.py:967
  57.5 1.0 copy-done.2
  58.5 2.7 %collective-permute-start.13 = (bf16[2,384,768]{2,1,0:T(8,128)(2,1)}, bf16[2,384,768]{2,1,0:T(8,128)(2,1)}, u32[]{:S(2)}, u32[]{:S(2)}) collective-permute-start(bf16[2,384,768]{2,1,0:T(8,128)(2,1)} %bitcast.5), channel_id=1, source_target_pairs={{0,2},{1,5},{2,0},{3,7},{4,6},{5,1},{6,4},{7,3},{8,10},{9,13},{10,... | collective-permute-start | bytes 3538952 | tf_op jit(solution)/shard_map/ppermute | solution.py:994
  61.3 8.6 %shard_map.514 = (f32[512,768]{1,0:T(8,128)}, bf16[512,768]{1,0:T(8,128)(2,1)S(1)}, f32[4,768]{1,0:T(4,128)S(1)}) custom-call(s32[1]{0:T(128)} %bitcast.core_ref, bf16[512,1536]{1,0:T(8,128)(2,1)S(1)} %get-tuple-element.169.grad_pre_own.grad, bf16[512,1536]{1,0:T(8,128)(2,1)} %get-tuple-element.170.grad_pre_peer, ...), custom_call_target="tpu_custom_call" | custom-call | flops 2500000000 | bytes 15000000 | tf_op jit(solution)/shard_map/pallas_call | solution.py:948
  70.4 6.5 %shard_map.515 = (bf16[384,1536]{1,0:T(8,128)(2,1)}, bf16[384,1536]{1,0:T(8,128)(2,1)S(1)}) custom-call(s32[1]{0:T(128)} %bitcast.3.bit_ref.half_ref, bf16[512,768]{1,0:T(8,128)(2,1)} %get-tuple-element.151.hidden.mixed, bf16[512,768]{1,0:T(8,128)(2,1)} %collective-permute-done.11.mixed_near, bf16[512,1536]{1,0:T(8,128)(2,1)S(1)} %get-tuple-element.169.grad_pre_own.grad, ...), custom_call_target="tpu_custom_call" | custom-call | flops 2400000000 | bytes 12000000 | tf_op jit(solution)/shard_map/pallas_call | solution.py:967
  77.0 1.1 collective-permute-start.17
  78.1 2.4 %fusion = (bf16[384,768]{1,0:T(8,128)(2,1)}, bf16[384,768]{1,0:T(8,128)(2,1)S(1)}) fusion(bf16[2,384,768]{2,1,0:T(8,128)(2,1)} %collective-permute-done.13, s32[]{:T(128)S(6)} %select_n.119, bf16[2,384,768]{2,1,0:T(8,128)(2,1)S(1)} %bitcast.31, s32[]{:T(128)S(6)} %select_n.120), kind=kLoop, calls=%fused_computation.23 | loop fusion | flops 2359296 | bytes 3538952 | tf_op jit(solution)/shard_map/convert_element_type | solution.py:30
  80.4 1.0 collective-permute-start.16
  82.0 7.5 %shard_map.516 = (bf16[512,1152]{1,0:T(8,128)(2,1)S(1)}, f32[3,384]{1,0:T(4,128)S(1)}) custom-call(s32[1]{0:T(128)} %bitcast.core_ref, bf16[12,512,512]{2,1,0:T(8,128)(2,1)} %get-tuple-element.180.weights, bf16[512,768]{1,0:T(8,128)(2,1)} %get-tuple-element.181.query_ref, bf16[512,768]{1,0:T(8,128)(2,1)} %get-tuple-element.182.key_ref, ...), custom_call_target="tpu_custom_call" | custom-call | flops 2000000000 | bytes 10000000 | tf_op jit(solution)/shard_map/pallas_call | solution.py:948
  89.6 1.5 shard_map.517
  91.1 1.5 collective-permute-start.18
  92.7 4.2 %collective-permute-done.16 = bf16[384,768]{1,0:T(8,128)(2,1)} collective-permute-done((bf16[384,768]{1,0:T(8,128)(2,1)S(1)}, bf16[384,768]{1,0:T(8,128)(2,1)}, u32[]{:S(2)}, u32[]{:S(2)}) %collective-permute-start.16) | collective-permute-done | bytes 589856 | tf_op jit(solution)/shard_map/ppermute | solution.py:994
  96.8 1.2 add_convert_fusion.6
  98.1 7.6 %shard_map.518 = (bf16[512,1152]{1,0:T(8,128)(2,1)S(1)}, f32[3,384]{1,0:T(4,128)S(1)}) custom-call(s32[1]{0:T(128)} %bitcast.core_ref, bf16[12,512,512]{2,1,0:T(8,128)(2,1)} %get-tuple-element.180.weights, bf16[512,768]{1,0:T(8,128)(2,1)} %get-tuple-element.181.query_ref, bf16[512,768]{1,0:T(8,128)(2,1)} %get-tuple-element.182.key_ref, ...), custom_call_target="tpu_custom_call" | custom-call | flops 2000000000 | bytes 10000000 | tf_op jit(solution)/shard_map/pallas_call | solution.py:948
  105.7 3.7 %collective-permute-start.20 = (bf16[384,768]{1,0:T(8,128)(2,1)S(1)}, bf16[384,768]{1,0:T(8,128)(2,1)S(1)}, u32[]{:S(2)}, u32[]{:S(2)}) collective-permute-start(bf16[384,768]{1,0:T(8,128)(2,1)S(1)} %add_convert_fusion.6), channel_id=1, source_target_pairs={{0,8},{1,9},{2,10},{3,11},{4,12},{5,13},{6,14},{7,15},{24,16},{25,... | collective-permute-start | bytes 1769480 | tf_op jit(solution)/shard_map/ppermute | solution.py:1005
  109.4 1.6 add_convert_fusion
  111.4 1.0 collective-permute-start.21
  112.5 2.4 %shard_map.519 = bf16[384,1152]{1,0:T(8,128)(2,1)S(1)} custom-call(s32[1]{0:T(128)} %bitcast.8.half_ref, s32[1]{0:T(128)} %bitcast.core_ref, bf16[1024,384]{1,0:T(8,128)(2,1)} %x_own.5, bf16[1024,384]{1,0:T(8,128)(2,1)} %collective-permute-done.x_peer, bf16[512,1152]{1,0:T(8,128)(2,1)S(1)} %get-tuple-element.199.grad.grad_own, ...), custom_call_target="tpu_custom_call" | custom-call | flops 24000000000 | bytes 100000000 | tf_op jit(solution)/shard_map/pallas_call | solution.py:948
  114.9 1.5 collective-permute-start.22
  116.5 4.8 %collective-permute-done.20 = bf16[384,768]{1,0:T(8,128)(2,1)S(1)} collective-permute-done((bf16[384,768]{1,0:T(8,128)(2,1)S(1)}, bf16[384,768]{1,0:T(8,128)(2,1)S(1)}, u32[]{:S(2)}, u32[]{:S(2)}) %collective-permute-start.20) | collective-permute-done | bytes 589856 | tf_op jit(solution)/shard_map/ppermute | solution.py:1005
  121.4 0.7 collective-permute-start.23
  122.1 5.5 %collective-permute-done.21 = bf16[240,1536]{1,0:T(8,128)(2,1)S(1)} collective-permute-done((bf16[240,1536]{1,0:T(8,128)(2,1)S(1)}, bf16[240,1536]{1,0:T(8,128)(2,1)S(1)}, u32[]{:S(2)}, u32[]{:S(2)}) %collective-permute-start.21) | collective-permute-done | bytes 737312 | tf_op jit(solution)/shard_map/ppermute | solution.py:994
  127.8 1.7 collective-permute-start.25
  129.5 2.4 %shard_map.520 = bf16[384,1152]{1,0:T(8,128)(2,1)S(1)} custom-call(s32[1]{0:T(128)} %bitcast.3.bit_ref.half_ref, s32[1]{0:T(128)} %bitcast.core_ref, bf16[1024,384]{1,0:T(8,128)(2,1)} %x_own.5, bf16[1024,384]{1,0:T(8,128)(2,1)} %collective-permute-done.x_peer, bf16[512,1152]{1,0:T(8,128)(2,1)S(1)} %get-tuple-element.199.grad.grad_own, ...), custom_call_target="tpu_custom_call" | custom-call | flops 24000000000 | bytes 100000000 | tf_op jit(solution)/shard_map/pallas_call | solution.py:948
  132.2 0.9 collective-permute-start.26
  133.2 1.3 collective-permute-start.27
  134.6 1.8 collective-permute-start.28
  136.4 5.1 %shard_map.521 = (f32[512,384]{1,0:T(8,128)S(1)}, f32[512,384]{1,0:T(8,128)S(1)}) custom-call(s32[1]{0:T(128)} %bitcast.core_ref, f32[512,768]{1,0:T(8,128)} %get-tuple-element.208.grad_resid, bf16[512,1152]{1,0:T(8,128)(2,1)S(1)} %get-tuple-element.199.grad.grad_own, bf16[512,1152]{1,0:T(8,128)(2,1)S(1)} %get-tuple-element.200.grad_peer, ...), custom_call_target="tpu_custom_call" | custom-call | flops 1800000000 | bytes 8000000 | tf_op jit(solution)/shard_map/pallas_call | solution.py:948
  141.5 2.1 collective-permute-done.25
  143.8 0.8 collective-permute-start.31
  144.8 7.2 %collective-permute-done.27 = bf16[384,768]{1,0:T(8,128)(2,1)S(1)} collective-permute-done((bf16[384,768]{1,0:T(8,128)(2,1)S(1)}, bf16[384,768]{1,0:T(8,128)(2,1)S(1)}, u32[]{:S(2)}, u32[]{:S(2)}) %collective-permute-start.27) | collective-permute-done | bytes 589856 | tf_op jit(solution)/shard_map/ppermute | solution.py:1005
  152.0 1.5 collective-permute-start.32
  153.6 1.2 maximum_select_fusion.4
  154.8 1.2 maximum_select_fusion
  156.2 1.3 collective-permute-start.35
  158.0 1.5 collective-permute-start.34
  159.6 2.9 %collective-permute-done.32 = bf16[192,1152]{1,0:T(8,128)(2,1)S(1)} collective-permute-done((bf16[192,1152]{1,0:T(8,128)(2,1)S(1)}, bf16[192,1152]{1,0:T(8,128)(2,1)S(1)}, u32[]{:S(2)}, u32[]{:S(2)}) %collective-permute-start.32) | collective-permute-done | bytes 442400 | tf_op jit(solution)/shard_map/ppermute | solution.py:1005
  163.2 4.2 %collective-permute-done.33 = bf16[384,768]{1,0:T(8,128)(2,1)S(1)} collective-permute-done((bf16[384,768]{1,0:T(8,128)(2,1)S(1)}, bf16[384,768]{1,0:T(8,128)(2,1)S(1)}, u32[]{:S(2)}, u32[]{:S(2)}) %collective-permute-start.33) | collective-permute-done | bytes 589856 | tf_op jit(solution)/shard_map/ppermute | solution.py:994
  167.6 0.9 collective-permute-start.38
  168.5 17.2 %collective-permute-done.35 = bf16[240,1536]{1,0:T(8,128)(2,1)S(1)} collective-permute-done((bf16[240,1536]{1,0:T(8,128)(2,1)S(1)}, bf16[240,1536]{1,0:T(8,128)(2,1)S(1)}, u32[]{:S(2)}, u32[]{:S(2)}) %collective-permute-start.35) | collective-permute-done | bytes 737312 | tf_op jit(solution)/shard_map/ppermute | solution.py:1005
  186.0 1.3 collective-permute-start.37
  187.3 1.0 collective-permute-start.40
  188.2 2.7 %collective-permute-start.39 = (f32[19,768]{1,0:T(8,128)S(1)}, f32[19,768]{1,0:T(8,128)S(1)}, u32[]{:S(2)}, u32[]{:S(2)}) collective-permute-start(f32[19,768]{1,0:T(8,128)S(1)} %add.98), channel_id=1, source_target_pairs={{0,8},{1,25},{2,10},{3,27},{4,12},{5,29},{6,14},{7,31},{8,0},{9,17... | collective-permute-start | bytes 175112 | tf_op jit(solution)/shard_map/ppermute | solution.py:994
  190.9 9.0 %collective-permute-done.37 = bf16[192,1152]{1,0:T(8,128)(2,1)S(1)} collective-permute-done((bf16[192,1152]{1,0:T(8,128)(2,1)S(1)}, bf16[192,1152]{1,0:T(8,128)(2,1)S(1)}, u32[]{:S(2)}, u32[]{:S(2)}) %collective-permute-start.37) | collective-permute-done | bytes 442400 | tf_op jit(solution)/shard_map/ppermute | solution.py:1005
  199.9 1.0 collective-permute-start.41
  200.9 2.6 %shard_map.522 = f32[4,384,768]{2,1,0:T(8,128)} custom-call(s32[1]{0:T(128)} %bitcast.3.bit_ref.half_ref, bf16[2,384,768]{2,1,0:T(8,128)(2,1)S(1)} %maximum_select_fusion.2.half, bf16[2,384,768]{2,1,0:T(8,128)(2,1)S(1)} %collective-permute-done.38.other), custom_call_target="tpu_custom_call" | custom-call | flops 1000000 | bytes 7000000 | tf_op jit(solution)/shard_map/pallas_call | solution.py:967
  203.8 1.4 collective-permute-start.43
  205.1 6.0 %collective-permute-done.41 = bf16[192,1152]{1,0:T(8,128)(2,1)S(1)} collective-permute-done((bf16[192,1152]{1,0:T(8,128)(2,1)S(1)}, bf16[192,1152]{1,0:T(8,128)(2,1)S(1)}, u32[]{:S(2)}, u32[]{:S(2)}) %collective-permute-start.41) | collective-permute-done | bytes 442400 | tf_op jit(solution)/shard_map/ppermute | solution.py:994
  211.3 3.0 %collective-permute-start.44 = (bf16[2,192,1152]{2,1,0:T(8,128)(2,1)S(1)}, bf16[2,192,1152]{2,1,0:T(8,128)(2,1)S(1)}, u32[]{:S(2)}, u32[]{:S(2)}) collective-permute-start(bf16[2,192,1152]{2,1,0:T(8,128)(2,1)S(1)} %maximum_select_fusion.3), channel_id=1, source_target_pairs={{0,2},{1,5},{2,0},{3,7},{4,6},{5,1},{6,4},{7,3},{8,10},{9,13},{10,... | collective-permute-start | bytes 2654216 | tf_op jit(solution)/shard_map/ppermute | solution.py:994
  214.3 2.5 %collective-permute-start.42 = (f32[19,768]{1,0:T(8,128)S(1)}, f32[19,768]{1,0:T(8,128)S(1)}, u32[]{:S(2)}, u32[]{:S(2)}) collective-permute-start(f32[19,768]{1,0:T(8,128)S(1)} %add.100), channel_id=1, source_target_pairs={{0,24},{1,9},{2,26},{3,11},{4,28},{5,13},{6,30},{7,15},{8,16},{9,1... | collective-permute-start | bytes 175112 | tf_op jit(solution)/shard_map/ppermute | solution.py:994
  216.8 3.7 %collective-permute-done.42 = f32[19,768]{1,0:T(8,128)S(1)} collective-permute-done((f32[19,768]{1,0:T(8,128)S(1)}, f32[19,768]{1,0:T(8,128)S(1)}, u32[]{:S(2)}, u32[]{:S(2)}) %collective-permute-start.42) | collective-permute-done | bytes 58400 | tf_op jit(solution)/shard_map/ppermute | solution.py:994
  220.5 1.1 shard_map.523
  221.6 1.6 collective-permute-done.43
  223.2 2.8 %shard_map.524 = (f32[768,1536]{1,0:T(8,128)}, f32[384,768]{1,0:T(8,128)}) custom-call(s32[1]{0:T(128)} %bitcast.3.bit_ref.half_ref, bf16[480,1536]{1,0:T(8,128)(2,1)S(1)} %bitcast.28, bf16[480,1536]{1,0:T(8,128)(2,1)S(1)} %bitcast.30), custom_call_target="tpu_custom_call" | custom-call | flops 1000000 | bytes 10000000 | tf_op jit(solution)/shard_map/pallas_call | solution.py:967
  226.0 6.7 %collective-permute-done.44 = bf16[2,192,1152]{2,1,0:T(8,128)(2,1)S(1)} collective-permute-done((bf16[2,192,1152]{2,1,0:T(8,128)(2,1)S(1)}, bf16[2,192,1152]{2,1,0:T(8,128)(2,1)S(1)}, u32[]{:S(2)}, u32[]{:S(2)}) %collective-permute-start.44) | collective-permute-done | bytes 884768 | tf_op jit(solution)/shard_map/ppermute | solution.py:994
  232.7 1.9 shard_map.525
  (98 shorter events, 8.9 us)
Async XLA Ops:
  0.7 8.9 %collective-permute-start = (bf16[1024,384]{1,0:T(8,128)(2,1)}, bf16[1024,384]{1,0:T(8,128)(2,1)}, u32[]{:S(2)}, u32[]{:S(2)}) collective-permute-start(bf16[1024,384]{1,0:T(8,128)(2,1)} %x_own.5), channel_id=1, source_target_pairs={{0,1},{1,0},{2,3},{3,2},{4,5},{5,4},{6,7},{7,6},{8,9},{9,8},{10,11... | collective-permute-start | bytes 2359304 | tf_op jit(solution)/shard_map/ppermute | solution.py:1013
  4.7 1.2 collective-permute-start.1
  4.8 2.3 collective-permute-start.2
  5.2 2.7 %collective-permute-start.3 = (bf16[768,384]{1,0:T(8,128)(2,1)}, bf16[768,384]{1,0:T(8,128)(2,1)S(1)}, u32[]{:S(2)}, u32[]{:S(2)}) collective-permute-start(bf16[768,384]{1,0:T(8,128)(2,1)} %wk_own.3), channel_id=1, source_target_pairs={{0,1},{1,0},{2,3},{3,2},{4,5},{5,4},{6,7},{7,6},{8,9},{9,8},{10,11... | collective-permute-start | bytes 1769480 | tf_op jit(solution)/shard_map/ppermute | solution.py:1013
  5.3 3.4 %collective-permute-start.4 = (bf16[768,384]{1,0:T(8,128)(2,1)}, bf16[768,384]{1,0:T(8,128)(2,1)S(1)}, u32[]{:S(2)}, u32[]{:S(2)}) collective-permute-start(bf16[768,384]{1,0:T(8,128)(2,1)} %wv_own.3), channel_id=1, source_target_pairs={{0,1},{1,0},{2,3},{3,2},{4,5},{5,4},{6,7},{7,6},{8,9},{9,8},{10,11... | collective-permute-start | bytes 1769480 | tf_op jit(solution)/shard_map/ppermute | solution.py:1013
  5.9 3.7 %collective-permute-start.5 = (bf16[384,768]{1,0:T(8,128)(2,1)}, bf16[384,768]{1,0:T(8,128)(2,1)S(1)}, u32[]{:S(2)}, u32[]{:S(2)}) collective-permute-start(bf16[384,768]{1,0:T(8,128)(2,1)} %wa_ref.1), channel_id=1, source_target_pairs={{0,1},{1,0},{2,3},{3,2},{4,5},{5,4},{6,7},{7,6},{8,9},{9,8},{10,11... | collective-permute-start | bytes 1769480 | tf_op jit(solution)/shard_map/ppermute | solution.py:1013
  7.1 3.4 %copy-start.7 = (bf16[768,384]{1,0:T(8,128)(2,1)}, bf16[768,384]{1,0:T(8,128)(2,1)S(1)}, u32[]{:S(2)}) copy-start(bf16[768,384]{1,0:T(8,128)(2,1)S(1)} %collective-permute-done.2.wq_peer) | copy-start | bytes 1769476
  7.9 2.6 %copy-start.8 = (bf16[768,384]{1,0:T(8,128)(2,1)}, bf16[768,384]{1,0:T(8,128)(2,1)S(1)}, u32[]{:S(2)}) copy-start(bf16[768,384]{1,0:T(8,128)(2,1)S(1)} %collective-permute-done.3.wk_peer) | copy-start | bytes 1769476
  8.8 1.7 copy-start.9
  9.6 0.9 copy-start.6
  9.6 19.9 %collective-permute-start.6 = (bf16[768,1536]{1,0:T(8,128)(2,1)}, bf16[768,1536]{1,0:T(8,128)(2,1)}, u32[]{:S(2)}, u32[]{:S(2)}) collective-permute-start(bf16[768,1536]{1,0:T(8,128)(2,1)} %up_own.3), channel_id=1, source_target_pairs={{0,1},{1,0},{2,3},{3,2},{4,5},{5,4},{6,7},{7,6},{8,9},{9,8},{10,11... | collective-permute-start | bytes 7077896 | tf_op jit(solution)/shard_map/ppermute | solution.py:1013
  10.0 19.5 %collective-permute-start.7 = (bf16[1536,768]{1,0:T(8,128)(2,1)}, bf16[1536,768]{1,0:T(8,128)(2,1)}, u32[]{:S(2)}, u32[]{:S(2)}) collective-permute-start(bf16[1536,768]{1,0:T(8,128)(2,1)} %down_own.3), channel_id=1, source_target_pairs={{0,1},{1,0},{2,3},{3,2},{4,5},{5,4},{6,7},{7,6},{8,9},{9,8},{10,11... | collective-permute-start | bytes 7077896 | tf_op jit(solution)/shard_map/ppermute | solution.py:1013
  10.1 19.4 %collective-permute-start.8 = (bf16[1024,384]{1,0:T(8,128)(2,1)}, bf16[1024,384]{1,0:T(8,128)(2,1)}, u32[]{:S(2)}, u32[]{:S(2)}) collective-permute-start(bf16[1024,384]{1,0:T(8,128)(2,1)} %teacher_own.1), channel_id=1, source_target_pairs={{0,1},{1,0},{2,3},{3,2},{4,5},{5,4},{6,7},{7,6},{8,9},{9,8},{10,11... | collective-permute-start | bytes 2359304 | tf_op jit(solution)/shard_map/ppermute | solution.py:1013
  44.5 8.2 %collective-permute-start.9 = (bf16[512,1536]{1,0:T(8,128)(2,1)S(1)}, bf16[512,1536]{1,0:T(8,128)(2,1)S(1)}, u32[]{:S(2)}, u32[]{:S(2)}) collective-permute-start(bf16[512,1536]{1,0:T(8,128)(2,1)S(1)} %get-tuple-element.166), channel_id=1, source_target_pairs={{0,1},{1,0},{2,3},{3,2},{4,5},{5,4},{6,7},{7,6},{8,9},{9,8},{10,11... | collective-permute-start | bytes 4718600 | tf_op jit(solution)/shard_map/ppermute | solution.py:1013
  44.9 7.9 %collective-permute-start.10 = (bf16[512,768]{1,0:T(8,128)(2,1)S(1)}, bf16[512,768]{1,0:T(8,128)(2,1)S(1)}, u32[]{:S(2)}, u32[]{:S(2)}) collective-permute-start(bf16[512,768]{1,0:T(8,128)(2,1)S(1)} %get-tuple-element.160.grad_ffn.grad), channel_id=1, source_target_pairs={{0,1},{1,0},{2,3},{3,2},{4,5},{5,4},{6,7},{7,6},{8,9},{9,8},{10,11... | collective-permute-start | bytes 2359304 | tf_op jit(solution)/shard_map/ppermute | solution.py:1013
  52.5 18.0 %collective-permute-start.12 = (bf16[512,1536]{1,0:T(8,128)(2,1)}, bf16[512,1536]{1,0:T(8,128)(2,1)}, u32[]{:S(2)}, u32[]{:S(2)}) collective-permute-start(bf16[512,1536]{1,0:T(8,128)(2,1)} %get-tuple-element.170.grad_pre_peer), channel_id=1, source_target_pairs={{0,1},{1,0},{2,3},{3,2},{4,5},{5,4},{6,7},{7,6},{8,9},{9,8},{10,11... | collective-permute-start | bytes 4718600 | tf_op jit(solution)/shard_map/ppermute | solution.py:1013
  57.5 1.0 copy-start.2
  58.5 19.5 %collective-permute-start.13 = (bf16[2,384,768]{2,1,0:T(8,128)(2,1)}, bf16[2,384,768]{2,1,0:T(8,128)(2,1)}, u32[]{:S(2)}, u32[]{:S(2)}) collective-permute-start(bf16[2,384,768]{2,1,0:T(8,128)(2,1)} %bitcast.5), channel_id=1, source_target_pairs={{0,2},{1,5},{2,0},{3,7},{4,6},{5,1},{6,4},{7,3},{8,10},{9,13},{10,... | collective-permute-start | bytes 3538952 | tf_op jit(solution)/shard_map/ppermute | solution.py:994
  61.3 9.2 %collective-permute-start.11 = (bf16[512,768]{1,0:T(8,128)(2,1)}, bf16[512,768]{1,0:T(8,128)(2,1)}, u32[]{:S(2)}, u32[]{:S(2)}) collective-permute-start(bf16[512,768]{1,0:T(8,128)(2,1)} %get-tuple-element.151.hidden.mixed), channel_id=1, source_target_pairs={{0,1},{1,0},{2,3},{3,2},{4,5},{5,4},{6,7},{7,6},{8,9},{9,8},{10,11... | collective-permute-start | bytes 2359304 | tf_op jit(solution)/shard_map/ppermute | solution.py:1013
  69.9 8.2 %copy-start.3 = (bf16[768,768]{1,0:T(8,128)(2,1)S(1)}, bf16[768,768]{1,0:T(8,128)(2,1)}, u32[]{:S(2)}) copy-start(bf16[768,768]{1,0:T(8,128)(2,1)} %copy-done.2) | copy-start | bytes 3538948
  69.9 19.7 %collective-permute-start.15 = (bf16[512,768]{1,0:T(8,128)(2,1)S(1)}, bf16[512,768]{1,0:T(8,128)(2,1)S(1)}, u32[]{:S(2)}, u32[]{:S(2)}) collective-permute-start(bf16[512,768]{1,0:T(8,128)(2,1)S(1)} %get-tuple-element.185.grad_attn.grad), channel_id=1, source_target_pairs={{0,1},{1,0},{2,3},{3,2},{4,5},{5,4},{6,7},{7,6},{8,9},{9,8},{10,11... | collective-permute-start | bytes 2359304 | tf_op jit(solution)/shard_map/ppermute | solution.py:1013
  77.0 3.5 %copy-start = (bf16[384,1536]{1,0:T(8,128)(2,1)}, bf16[384,1536]{1,0:T(8,128)(2,1)S(1)}, u32[]{:S(2)}) copy-start(bf16[384,1536]{1,0:T(8,128)(2,1)S(1)} %get-tuple-element.194) | copy-start | bytes 3538948
  77.0 4.4 %copy-start.11 = (bf16[512,384]{1,0:T(8,128)(2,1)S(1)}, bf16[512,384]{1,0:T(8,128)(2,1)}, u32[]{:S(2)}) copy-start(bf16[512,384]{1,0:T(8,128)(2,1)} %get-tuple-element.189) | copy-start | bytes 1179652
  77.0 32.4 %collective-permute-start.17 = (bf16[384,1536]{1,0:T(8,128)(2,1)}, bf16[384,1536]{1,0:T(8,128)(2,1)}, u32[]{:S(2)}, u32[]{:S(2)}) collective-permute-start(bf16[384,1536]{1,0:T(8,128)(2,1)} %get-tuple-element.195), channel_id=1, source_target_pairs={{0,2},{1,5},{2,0},{3,7},{4,6},{5,1},{6,4},{7,3},{8,10},{9,13},{10,... | collective-permute-start | bytes 3538952 | tf_op jit(solution)/shard_map/ppermute | solution.py:994
  80.4 16.4 %collective-permute-start.16 = (bf16[384,768]{1,0:T(8,128)(2,1)S(1)}, bf16[384,768]{1,0:T(8,128)(2,1)}, u32[]{:S(2)}, u32[]{:S(2)}) collective-permute-start(bf16[384,768]{1,0:T(8,128)(2,1)S(1)} %get-tuple-element.260), channel_id=1, source_target_pairs={{0,4},{1,3},{2,6},{3,1},{4,0},{5,7},{6,2},{7,5},{8,12},{9,11},{10,... | collective-permute-start | bytes 1769480 | tf_op jit(solution)/shard_map/ppermute | solution.py:994
  81.4 8.2 %collective-permute-start.14 = (bf16[512,384]{1,0:T(8,128)(2,1)S(1)}, bf16[512,384]{1,0:T(8,128)(2,1)S(1)}, u32[]{:S(2)}, u32[]{:S(2)}) collective-permute-start(bf16[512,384]{1,0:T(8,128)(2,1)S(1)} %copy-done.11), channel_id=1, source_target_pairs={{0,1},{1,0},{2,3},{3,2},{4,5},{5,4},{6,7},{7,6},{8,9},{9,8},{10,11... | collective-permute-start | bytes 1179656 | tf_op jit(solution)/shard_map/ppermute | solution.py:1013
  81.4 72.1 %collective-permute-start.29 = (bf16[512,384]{1,0:T(8,128)(2,1)}, bf16[512,384]{1,0:T(8,128)(2,1)S(1)}, u32[]{:S(2)}, u32[]{:S(2)}) collective-permute-start(bf16[512,384]{1,0:T(8,128)(2,1)} %get-tuple-element.215), channel_id=1, source_target_pairs={{0,1},{1,0},{2,3},{3,2},{4,5},{5,4},{6,7},{7,6},{8,9},{9,8},{10,11... | collective-permute-start | bytes 1179656 | tf_op jit(solution)/shard_map/ppermute | solution.py:1013
  82.0 7.6 %copy-start.4 = (bf16[512,384]{1,0:T(8,128)(2,1)S(1)}, bf16[512,384]{1,0:T(8,128)(2,1)}, u32[]{:S(2)}) copy-start(bf16[512,384]{1,0:T(8,128)(2,1)} %get-tuple-element.188.gated) | copy-start | bytes 1179652
  89.5 7.3 %copy-start.5 = (bf16[384,768]{1,0:T(8,128)(2,1)S(1)}, bf16[384,768]{1,0:T(8,128)(2,1)}, u32[]{:S(2)}) copy-start(bf16[384,768]{1,0:T(8,128)(2,1)} %get-tuple-element.191) | copy-start | bytes 1769476
  91.1 19.9 %collective-permute-start.18 = (bf16[96,1536]{1,0:T(8,128)(2,1)S(1)}, bf16[96,1536]{1,0:T(8,128)(2,1)S(1)}, u32[]{:S(2)}, u32[]{:S(2)}) collective-permute-start(bf16[96,1536]{1,0:T(8,128)(2,1)S(1)} %get-tuple-element.197), channel_id=1, source_target_pairs={{0,2},{1,5},{2,0},{3,7},{4,6},{5,1},{6,4},{7,3},{8,10},{9,13},{10,... | collective-permute-start | bytes 884744 | tf_op jit(solution)/shard_map/ppermute | solution.py:994
  92.7 19.9 %collective-permute-start.19 = (bf16[512,1152]{1,0:T(8,128)(2,1)S(1)}, bf16[512,1152]{1,0:T(8,128)(2,1)S(1)}, u32[]{:S(2)}, u32[]{:S(2)}) collective-permute-start(bf16[512,1152]{1,0:T(8,128)(2,1)S(1)} %get-tuple-element.200.grad_peer), channel_id=1, source_target_pairs={{0,1},{1,0},{2,3},{3,2},{4,5},{5,4},{6,7},{7,6},{8,9},{9,8},{10,11... | collective-permute-start | bytes 3538952 | tf_op jit(solution)/shard_map/ppermute | solution.py:1013
  98.0 11.4 %copy-start.1 = (bf16[384,1536]{1,0:T(8,128)(2,1)S(1)}, bf16[384,1536]{1,0:T(8,128)(2,1)}, u32[]{:S(2)}) copy-start(bf16[384,1536]{1,0:T(8,128)(2,1)} %copy-done) | copy-start | bytes 3538948
  105.7 15.6 %collective-permute-start.20 = (bf16[384,768]{1,0:T(8,128)(2,1)S(1)}, bf16[384,768]{1,0:T(8,128)(2,1)S(1)}, u32[]{:S(2)}, u32[]{:S(2)}) collective-permute-start(bf16[384,768]{1,0:T(8,128)(2,1)S(1)} %add_convert_fusion.6), channel_id=1, source_target_pairs={{0,8},{1,9},{2,10},{3,11},{4,12},{5,13},{6,14},{7,15},{24,16},{25,... | collective-permute-start | bytes 1769480 | tf_op jit(solution)/shard_map/ppermute | solution.py:1005
  111.4 16.3 %collective-permute-start.21 = (bf16[240,1536]{1,0:T(8,128)(2,1)S(1)}, bf16[240,1536]{1,0:T(8,128)(2,1)S(1)}, u32[]{:S(2)}, u32[]{:S(2)}) collective-permute-start(bf16[240,1536]{1,0:T(8,128)(2,1)S(1)} %get-tuple-element.262), channel_id=1, source_target_pairs={{0,4},{1,3},{2,6},{3,1},{4,0},{5,7},{6,2},{7,5},{8,12},{9,11},{10,... | collective-permute-start | bytes 2211848 | tf_op jit(solution)/shard_map/ppermute | solution.py:994
  112.4 22.1 %collective-permute-start.24 = (f32[19,768]{1,0:T(8,128)S(1)}, f32[19,768]{1,0:T(8,128)S(1)}, u32[]{:S(2)}, u32[]{:S(2)}) collective-permute-start(f32[19,768]{1,0:T(8,128)S(1)} %pad_maximum_fusion.1), channel_id=1, source_target_pairs={{0,1},{1,0},{2,3},{3,2},{4,5},{5,4},{6,7},{7,6},{8,9},{9,8},{10,11... | collective-permute-start | bytes 175112 | tf_op jit(solution)/shard_map/ppermute | solution.py:1013
  114.9 17.0 %collective-permute-start.22 = (bf16[2,192,1152]{2,1,0:T(8,128)(2,1)S(1)}, bf16[2,192,1152]{2,1,0:T(8,128)(2,1)S(1)}, u32[]{:S(2)}, u32[]{:S(2)}) collective-permute-start(bf16[2,192,1152]{2,1,0:T(8,128)(2,1)S(1)} %bitcast.34), channel_id=1, source_target_pairs={{0,2},{1,5},{2,0},{3,7},{4,6},{5,1},{6,4},{7,3},{8,10},{9,13},{10,... | collective-permute-start | bytes 2654216 | tf_op jit(solution)/shard_map/ppermute | solution.py:994
  121.4 11.7 %collective-permute-start.23 = (bf16[384,768]{1,0:T(8,128)(2,1)S(1)}, bf16[384,768]{1,0:T(8,128)(2,1)S(1)}, u32[]{:S(2)}, u32[]{:S(2)}) collective-permute-start(bf16[384,768]{1,0:T(8,128)(2,1)S(1)} %add_convert_fusion.5), channel_id=1, source_target_pairs={{8,16},{9,17},{10,18},{11,19},{12,20},{13,21},{14,22},{15,23},{16,... | collective-permute-start | bytes 1769480 | tf_op jit(solution)/shard_map/ppermute | solution.py:1005
  127.8 15.7 %collective-permute-start.25 = (bf16[240,1536]{1,0:T(8,128)(2,1)S(1)}, bf16[240,1536]{1,0:T(8,128)(2,1)S(1)}, u32[]{:S(2)}, u32[]{:S(2)}) collective-permute-start(bf16[240,1536]{1,0:T(8,128)(2,1)S(1)} %add_convert_fusion.3), channel_id=1, source_target_pairs={{0,8},{1,9},{2,10},{3,11},{4,12},{5,13},{6,14},{7,15},{24,16},{25,... | collective-permute-start | bytes 2211848 | tf_op jit(solution)/shard_map/ppermute | solution.py:1005
  132.2 11.6 %collective-permute-start.26 = (bf16[192,1152]{1,0:T(8,128)(2,1)S(1)}, bf16[192,1152]{1,0:T(8,128)(2,1)S(1)}, u32[]{:S(2)}, u32[]{:S(2)}) collective-permute-start(bf16[192,1152]{1,0:T(8,128)(2,1)S(1)} %get-tuple-element.264), channel_id=1, source_target_pairs={{0,4},{1,3},{2,6},{3,1},{4,0},{5,7},{6,2},{7,5},{8,12},{9,11},{10,... | collective-permute-start | bytes 1327112 | tf_op jit(solution)/shard_map/ppermute | solution.py:994
  133.2 18.7 %collective-permute-start.27 = (bf16[384,768]{1,0:T(8,128)(2,1)S(1)}, bf16[384,768]{1,0:T(8,128)(2,1)S(1)}, u32[]{:S(2)}, u32[]{:S(2)}) collective-permute-start(bf16[384,768]{1,0:T(8,128)(2,1)S(1)} %add_convert_fusion.4), channel_id=1, source_target_pairs={{8,0},{9,1},{10,2},{11,3},{12,4},{13,5},{14,6},{15,7},{16,24},{17,... | collective-permute-start | bytes 1769480 | tf_op jit(solution)/shard_map/ppermute | solution.py:1005
  134.6 19.0 %collective-permute-start.28 = (f32[19,768]{1,0:T(8,128)S(1)}, f32[19,768]{1,0:T(8,128)S(1)}, u32[]{:S(2)}, u32[]{:S(2)}) collective-permute-start(f32[19,768]{1,0:T(8,128)S(1)} %add.92), channel_id=1, source_target_pairs={{0,2},{1,5},{2,0},{3,7},{4,6},{5,1},{6,4},{7,3},{8,10},{9,13},{10,... | collective-permute-start | bytes 175112 | tf_op jit(solution)/shard_map/ppermute | solution.py:994
  143.6 11.2 %collective-permute-start.30 = (f32[512,384]{1,0:T(8,128)S(1)}, f32[512,384]{1,0:T(8,128)S(1)}, u32[]{:S(2)}, u32[]{:S(2)}) collective-permute-start(f32[512,384]{1,0:T(8,128)S(1)} %get-tuple-element.209), channel_id=1, source_target_pairs={{0,1},{1,0},{2,3},{3,2},{4,5},{5,4},{6,7},{7,6},{8,9},{9,8},{10,11... | collective-permute-start | bytes 2359304 | tf_op jit(solution)/shard_map/ppermute | solution.py:1013
  143.8 9.8 %copy-start.10 = (bf16[512,384]{1,0:T(8,128)(2,1)S(1)}, bf16[512,384]{1,0:T(8,128)(2,1)}, u32[]{:S(2)}) copy-start(bf16[512,384]{1,0:T(8,128)(2,1)} %get-tuple-element.214) | copy-start | bytes 1179652
  143.8 12.2 %collective-permute-start.31 = (bf16[240,1536]{1,0:T(8,128)(2,1)S(1)}, bf16[240,1536]{1,0:T(8,128)(2,1)S(1)}, u32[]{:S(2)}, u32[]{:S(2)}) collective-permute-start(bf16[240,1536]{1,0:T(8,128)(2,1)S(1)} %add_convert_fusion.2), channel_id=1, source_target_pairs={{8,16},{9,17},{10,18},{11,19},{12,20},{13,21},{14,22},{15,23},{16,... | collective-permute-start | bytes 2211848 | tf_op jit(solution)/shard_map/ppermute | solution.py:1005
  152.0 10.5 %collective-permute-start.32 = (bf16[192,1152]{1,0:T(8,128)(2,1)S(1)}, bf16[192,1152]{1,0:T(8,128)(2,1)S(1)}, u32[]{:S(2)}, u32[]{:S(2)}) collective-permute-start(bf16[192,1152]{1,0:T(8,128)(2,1)S(1)} %add_convert_fusion.11), channel_id=1, source_target_pairs={{0,8},{1,9},{2,10},{3,11},{4,12},{5,13},{6,14},{7,15},{24,16},{25,... | collective-permute-start | bytes 1327112 | tf_op jit(solution)/shard_map/ppermute | solution.py:1005
  156.2 29.5 %collective-permute-start.35 = (bf16[240,1536]{1,0:T(8,128)(2,1)S(1)}, bf16[240,1536]{1,0:T(8,128)(2,1)S(1)}, u32[]{:S(2)}, u32[]{:S(2)}) collective-permute-start(bf16[240,1536]{1,0:T(8,128)(2,1)S(1)} %add_convert_fusion.1), channel_id=1, source_target_pairs={{8,0},{9,1},{10,2},{11,3},{12,4},{13,5},{14,6},{15,7},{16,24},{17,... | collective-permute-start | bytes 2211848 | tf_op jit(solution)/shard_map/ppermute | solution.py:1005
  157.5 9.9 %collective-permute-start.33 = (bf16[384,768]{1,0:T(8,128)(2,1)S(1)}, bf16[384,768]{1,0:T(8,128)(2,1)S(1)}, u32[]{:S(2)}, u32[]{:S(2)}) collective-permute-start(bf16[384,768]{1,0:T(8,128)(2,1)S(1)} %broadcast_select_fusion.3), channel_id=1, source_target_pairs={{0,4},{1,3},{2,6},{3,1},{4,0},{5,7},{6,2},{7,5},{8,12},{9,11},{10,... | collective-permute-start | bytes 1769480 | tf_op jit(solution)/shard_map/ppermute | solution.py:994
  158.0 10.5 %collective-permute-start.34 = (f32[19,768]{1,0:T(8,128)S(1)}, f32[19,768]{1,0:T(8,128)S(1)}, u32[]{:S(2)}, u32[]{:S(2)}) collective-permute-start(f32[19,768]{1,0:T(8,128)S(1)} %add.95), channel_id=1, source_target_pairs={{0,4},{1,3},{2,6},{3,1},{4,0},{5,7},{6,2},{7,5},{8,12},{9,11},{10,... | collective-permute-start | bytes 175112 | tf_op jit(solution)/shard_map/ppermute | solution.py:994
  162.5 23.3 %collective-permute-start.36 = (bf16[192,1152]{1,0:T(8,128)(2,1)S(1)}, bf16[192,1152]{1,0:T(8,128)(2,1)S(1)}, u32[]{:S(2)}, u32[]{:S(2)}) collective-permute-start(bf16[192,1152]{1,0:T(8,128)(2,1)S(1)} %add_convert_fusion.10), channel_id=1, source_target_pairs={{8,16},{9,17},{10,18},{11,19},{12,20},{13,21},{14,22},{15,23},{16,... | collective-permute-start | bytes 1327112 | tf_op jit(solution)/shard_map/ppermute | solution.py:1005
  167.6 33.3 %collective-permute-start.38 = (bf16[2,384,768]{2,1,0:T(8,128)(2,1)S(1)}, bf16[2,384,768]{2,1,0:T(8,128)(2,1)S(1)}, u32[]{:S(2)}, u32[]{:S(2)}) collective-permute-start(bf16[2,384,768]{2,1,0:T(8,128)(2,1)S(1)} %maximum_select_fusion.2.half), channel_id=1, source_target_pairs={{0,2},{1,5},{2,0},{3,7},{4,6},{5,1},{6,4},{7,3},{8,10},{9,13},{10,... | collective-permute-start | bytes 3538952 | tf_op jit(solution)/shard_map/ppermute | solution.py:994
  186.0 13.9 %collective-permute-start.37 = (bf16[192,1152]{1,0:T(8,128)(2,1)S(1)}, bf16[192,1152]{1,0:T(8,128)(2,1)S(1)}, u32[]{:S(2)}, u32[]{:S(2)}) collective-permute-start(bf16[192,1152]{1,0:T(8,128)(2,1)S(1)} %add_convert_fusion.9), channel_id=1, source_target_pairs={{8,0},{9,1},{10,2},{11,3},{12,4},{13,5},{14,6},{15,7},{16,24},{17,... | collective-permute-start | bytes 1327112 | tf_op jit(solution)/shard_map/ppermute | solution.py:1005
  187.3 16.2 %collective-permute-start.40 = (bf16[240,1536]{1,0:T(8,128)(2,1)S(1)}, bf16[240,1536]{1,0:T(8,128)(2,1)S(1)}, u32[]{:S(2)}, u32[]{:S(2)}) collective-permute-start(bf16[240,1536]{1,0:T(8,128)(2,1)S(1)} %broadcast_select_fusion), channel_id=1, source_target_pairs={{0,4},{1,3},{2,6},{3,1},{4,0},{5,7},{6,2},{7,5},{8,12},{9,11},{10,... | collective-permute-start | bytes 2211848 | tf_op jit(solution)/shard_map/ppermute | solution.py:994
  188.2 15.3 %collective-permute-start.39 = (f32[19,768]{1,0:T(8,128)S(1)}, f32[19,768]{1,0:T(8,128)S(1)}, u32[]{:S(2)}, u32[]{:S(2)}) collective-permute-start(f32[19,768]{1,0:T(8,128)S(1)} %add.98), channel_id=1, source_target_pairs={{0,8},{1,25},{2,10},{3,27},{4,12},{5,29},{6,14},{7,31},{8,0},{9,17... | collective-permute-start | bytes 175112 | tf_op jit(solution)/shard_map/ppermute | solution.py:994
  199.9 11.3 %collective-permute-start.41 = (bf16[192,1152]{1,0:T(8,128)(2,1)S(1)}, bf16[192,1152]{1,0:T(8,128)(2,1)S(1)}, u32[]{:S(2)}, u32[]{:S(2)}) collective-permute-start(bf16[192,1152]{1,0:T(8,128)(2,1)S(1)} %broadcast_select_fusion.4), channel_id=1, source_target_pairs={{0,4},{1,3},{2,6},{3,1},{4,0},{5,7},{6,2},{7,5},{8,12},{9,11},{10,... | collective-permute-start | bytes 1327112 | tf_op jit(solution)/shard_map/ppermute | solution.py:994
  203.8 19.4 %collective-permute-start.43 = (bf16[2,240,1536]{2,1,0:T(8,128)(2,1)S(1)}, bf16[2,240,1536]{2,1,0:T(8,128)(2,1)S(1)}, u32[]{:S(2)}, u32[]{:S(2)}) collective-permute-start(bf16[2,240,1536]{2,1,0:T(8,128)(2,1)S(1)} %maximum_select_fusion.1), channel_id=1, source_target_pairs={{0,2},{1,5},{2,0},{3,7},{4,6},{5,1},{6,4},{7,3},{8,10},{9,13},{10,... | collective-permute-start | bytes 4423688 | tf_op jit(solution)/shard_map/ppermute | solution.py:994
  211.3 21.3 %collective-permute-start.44 = (bf16[2,192,1152]{2,1,0:T(8,128)(2,1)S(1)}, bf16[2,192,1152]{2,1,0:T(8,128)(2,1)S(1)}, u32[]{:S(2)}, u32[]{:S(2)}) collective-permute-start(bf16[2,192,1152]{2,1,0:T(8,128)(2,1)S(1)} %maximum_select_fusion.3), channel_id=1, source_target_pairs={{0,2},{1,5},{2,0},{3,7},{4,6},{5,1},{6,4},{7,3},{8,10},{9,13},{10,... | collective-permute-start | bytes 2654216 | tf_op jit(solution)/shard_map/ppermute | solution.py:994
  214.3 6.2 %collective-permute-start.42 = (f32[19,768]{1,0:T(8,128)S(1)}, f32[19,768]{1,0:T(8,128)S(1)}, u32[]{:S(2)}, u32[]{:S(2)}) collective-permute-start(f32[19,768]{1,0:T(8,128)S(1)} %add.100), channel_id=1, source_target_pairs={{0,24},{1,9},{2,26},{3,11},{4,28},{5,13},{6,30},{7,15},{8,16},{9,1... | collective-permute-start | bytes 175112 | tf_op jit(solution)/shard_map/ppermute | solution.py:994
